TPU v7x, 32 devices: a whole 2x2x4 slice. The times are simulated.
32 devices in a mesh: batch: 4 (over z), mp: 8 (over y, x, core).
Axes of the slice: x: 2, y: 2, z: 4, core: 2. Of those that a mesh axis runs over, the one named last changes fastest.
Arguments:
- tokens: bfloat16 [8192, 2048], P(('batch', 'mp')), may hold values from -6 to 6
- out_grad: bfloat16 [8192, 2048], P(('batch', 'mp')), may hold values from -6 to 6
- seq_lengths: int32 [8], replicated, may hold values from 1 to 2048, as said below
- seq_scripts: int32 [8], replicated, may hold values from 0 to 2
- seq_place: int32 [8], replicated, may hold values from 0 to 3, as said below
- norm1_gain: float32 [2048], replicated, may hold values from 0.25 to 1.75
- norm1_shift: float32 [2048], replicated, may hold values from -3 to 3
- w_qkv: bfloat16 [3, 2048, 2048], P(None, None, 'mp'), may hold values from -0.1875 to 0.1875
- qv_bias: float32 [2, 2048], P(None, 'mp'), may hold values from -3 to 3
- w_out: bfloat16 [2048, 2048], P('mp'), may hold values from -0.375 to 0.375
- out_bias: float32 [2048], replicated, may hold values from -3 to 3
- norm2_gain: float32 [2048], replicated, may hold values from 0.25 to 1.75
- norm2_shift: float32 [2048], replicated, may hold values from -3 to 3
- w_in: bfloat16 [2048, 8192], P(None, 'mp'), may hold values from -0.125 to 0.125
- in_bias: float32 [8192], P('mp'), may hold values from -3 to 3
- w_down: bfloat16 [8192, 2048], P('mp'), may hold values from -0.0625 to 0.0625
- down_bias: float32 [2048], replicated, may hold values from -3 to 3
Outputs:
- block_out: bfloat16 [8192, 2048], P(('batch', 'mp'))
- input_grad: bfloat16 [8192, 2048], P(('batch', 'mp'))
- norm1_gain_grad: float32 [2048], replicated
- norm1_shift_grad: float32 [2048], replicated
- qkv_weight_grad: float32 [3, 2048, 2048], P(None, 'batch', 'mp')
- qv_bias_grad: float32 [2, 2048], replicated
- out_weight_grad: float32 [2048, 2048], P('mp', 'batch')
- out_bias_grad: float32 [2048], replicated
- norm2_gain_grad: float32 [2048], replicated
- norm2_shift_grad: float32 [2048], replicated
- in_weight_grad: float32 [2048, 8192], P('batch', 'mp')
- in_bias_grad: float32 [8192], replicated
- down_weight_grad: float32 [8192, 2048], P('mp', 'batch')
- down_bias_grad: float32 [2048], replicated
Inputs may be any that keep to these rules, and one draw needn't show every extreme that they name: `seq_lengths`: the sequences with one value of seq_place hold 2048 tokens or fewer together; one sequence has exactly 2048 tokens and is the only one of its batch group. `seq_place`: every batch group holds at least one sequence.
All inputs are finite; a program needn't handle non-finite values.
Results may differ from a plain program's by a relative error of at most 0.018.
The roundings to bfloat16 on the way count: a program that leaves them out, or rounds other values in their place, can miss the bound.
Values may be sent and summed in bfloat16 or wider, within the bound.
A program may use at most 256 MiB of HBM per device.

v0:
```python
import jax
import jax.numpy as jnp
from jax import lax
from jax.sharding import PartitionSpec as P

HEAD_DIM = 128


EPS = 1e-05
MASKED = -1000000000.0


def segments_of(group, seq_lengths, seq_scripts, seq_place, rows):
    count = seq_lengths.shape[0]
    numbers = jnp.arange(count, dtype=jnp.int32)
    order_key = seq_scripts * count + numbers
    same = seq_place[:, None] == seq_place[None, :]
    before = order_key[None, :] < order_key[:, None]
    offsets = jnp.sum(jnp.where(same & before, seq_lengths[None, :], 0), axis=1)
    position = jnp.arange(rows, dtype=jnp.int32)[:, None]
    member = (
        (seq_place[None, :] == group)
        & (position >= offsets[None, :])
        & (position < (offsets + seq_lengths)[None, :])
    )
    labels = jnp.sum(jnp.where(member, numbers[None, :], 0), axis=1)
    return labels + jnp.where(jnp.any(member, axis=1), 0, count)


def visible(segment, first, block):
    rows = segment.shape[0]
    query_rows = first + jnp.arange(block, dtype=jnp.int32)
    query_labels = lax.dynamic_slice_in_dim(segment, first, block, 0)
    key_rows = jnp.arange(rows, dtype=jnp.int32)
    return (query_labels[:, None] == segment[None, :]) & (key_rows[None, :] <= query_rows[:, None])


def norm_forward(rows, gain, shift):
    mean = jnp.mean(rows, axis=-1, keepdims=True)
    centred = rows - mean
    inverse = lax.rsqrt(jnp.mean(centred * centred, axis=-1, keepdims=True) + EPS)
    unit = centred * inverse
    return (unit * gain + shift, unit, inverse)


def norm_backward(grad, unit, inverse, gain):
    scaled = grad * gain
    centred = (
        scaled
        - jnp.mean(scaled, axis=-1, keepdims=True)
        - unit * jnp.mean(scaled * unit, axis=-1, keepdims=True)
    )
    return (inverse * centred, jnp.sum(grad * unit, axis=0), jnp.sum(grad, axis=0))


def attend_forward(queries, keys, values, segment, block, scale):
    local_heads, rows, size = keys.shape

    def one_block(index):
        first = index * block
        query_block = lax.dynamic_slice_in_dim(queries, first, block, 1)
        scores = (
            jnp.einsum("hqd,hkd->hqk", query_block, keys, preferred_element_type=jnp.float32)
            * scale
        )
        scores = jnp.where(visible(segment, first, block)[None], scores, MASKED)
        top = jnp.max(scores, axis=-1, keepdims=True)
        exps = jnp.exp(scores - top)
        total = jnp.sum(exps, axis=-1, keepdims=True)
        weights = (exps / total).astype(jnp.bfloat16)
        mixed = jnp.einsum("hqk,hkd->hqd", weights, values, preferred_element_type=jnp.float32)
        return (mixed, (top + jnp.log(total))[..., 0])

    mixed, logsum = lax.map(one_block, jnp.arange(rows // block, dtype=jnp.int32))
    mixed = jnp.transpose(mixed, (1, 0, 2, 3)).reshape(local_heads, rows, size)
    logsum = jnp.transpose(logsum, (1, 0, 2)).reshape(local_heads, rows)
    return (mixed, logsum)


def attend_backward(queries, keys, values, grad_out, logsum, segment, block, scale):
    local_heads, rows, size = keys.shape

    def one_block(carry, index):
        key_grad, value_grad = carry
        first = index * block
        query_block = lax.dynamic_slice_in_dim(queries, first, block, 1)
        grad_block = lax.dynamic_slice_in_dim(grad_out, first, block, 1)
        logsum_block = lax.dynamic_slice_in_dim(logsum, first, block, 1)
        scores = (
            jnp.einsum("hqd,hkd->hqk", query_block, keys, preferred_element_type=jnp.float32)
            * scale
        )
        allowed = visible(segment, first, block)[None]
        probs = jnp.where(allowed, jnp.exp(scores - logsum_block[..., None]), 0.0)
        value_grad = value_grad + jnp.einsum(
            "hqk,hqd->hkd",
            probs.astype(jnp.bfloat16),
            grad_block,
            preferred_element_type=jnp.float32,
        )
        prob_grad = jnp.einsum(
            "hqd,hkd->hqk", grad_block, values, preferred_element_type=jnp.float32
        )
        inner = jnp.sum(probs * prob_grad, axis=-1, keepdims=True)
        score_grad = (probs * (prob_grad - inner)).astype(jnp.bfloat16)
        query_grad = (
            jnp.einsum("hqk,hkd->hqd", score_grad, keys, preferred_element_type=jnp.float32) * scale
        )
        key_grad = (
            key_grad
            + jnp.einsum(
                "hqk,hqd->hkd", score_grad, query_block, preferred_element_type=jnp.float32
            )
            * scale
        )
        return ((key_grad, value_grad), query_grad)

    zeros = jnp.zeros((local_heads, rows, size), jnp.float32)
    (key_grad, value_grad), query_grad = lax.scan(
        one_block, (zeros, zeros), jnp.arange(rows // block, dtype=jnp.int32)
    )
    query_grad = jnp.transpose(query_grad, (1, 0, 2, 3)).reshape(local_heads, rows, size)
    return (query_grad, key_grad, value_grad)


def body(
    tokens,
    out_grad,
    seq_lengths,
    seq_scripts,
    seq_place,
    norm1_gain,
    norm1_shift,
    w_qkv,
    qv_bias,
    w_out,
    out_bias,
    norm2_gain,
    norm2_shift,
    w_in,
    in_bias,
    w_down,
    down_bias,
):
    own_rows = tokens.shape[0]
    model_devices = lax.axis_size("mp")
    group_rows = own_rows * model_devices
    width = tokens.shape[1]
    local_width = w_qkv.shape[2]
    local_hidden = w_in.shape[1]
    local_heads = local_width // HEAD_DIM
    block = min(512, group_rows)
    scale = HEAD_DIM ** (-0.5)
    column = lax.axis_index("mp")
    segment = segments_of(lax.axis_index("batch"), seq_lengths, seq_scripts, seq_place, group_rows)

    def split_heads(matrix):
        return jnp.transpose(matrix.reshape(group_rows, local_heads, HEAD_DIM), (1, 0, 2))

    def join_heads(tensor):
        return jnp.transpose(tensor, (1, 0, 2)).reshape(group_rows, local_width)

    inputs = tokens.astype(jnp.float32)
    normed1, unit1, inverse1 = norm_forward(inputs, norm1_gain, norm1_shift)
    first_rows = normed1.astype(jnp.bfloat16)
    first_all = lax.all_gather(first_rows, "mp", axis=0, tiled=True)
    projected = jnp.einsum("td,cde->cte", first_all, w_qkv, preferred_element_type=jnp.float32)
    queries = split_heads((projected[0] + qv_bias[0]).astype(jnp.bfloat16))
    keys = split_heads(projected[1].astype(jnp.bfloat16))
    values = split_heads((projected[2] + qv_bias[1]).astype(jnp.bfloat16))
    mixed, logsum = attend_forward(queries, keys, values, segment, block, scale)
    attended = join_heads(mixed).astype(jnp.bfloat16)
    branch = lax.psum_scatter(
        jnp.dot(attended, w_out, preferred_element_type=jnp.float32),
        "mp",
        scatter_dimension=0,
        tiled=True,
    )
    middle = inputs + branch + out_bias
    normed2, unit2, inverse2 = norm_forward(middle, norm2_gain, norm2_shift)
    second_rows = normed2.astype(jnp.bfloat16)
    second_all = lax.all_gather(second_rows, "mp", axis=0, tiled=True)
    hidden = jnp.dot(second_all, w_in, preferred_element_type=jnp.float32) + in_bias
    activated = jax.nn.gelu(hidden, approximate=True).astype(jnp.bfloat16)
    feed = lax.psum_scatter(
        jnp.dot(activated, w_down, preferred_element_type=jnp.float32).astype(jnp.bfloat16),
        "mp",
        scatter_dimension=0,
        tiled=True,
    ).astype(jnp.float32)
    block_out = (middle + feed + down_bias).astype(jnp.bfloat16)
    upstream = out_grad.astype(jnp.float32)
    grad_all = lax.all_gather(out_grad, "mp", axis=0, tiled=True)
    act_grad = jnp.dot(grad_all, w_down.T, preferred_element_type=jnp.float32)
    down_weight_part = jnp.dot(activated.T, grad_all, preferred_element_type=jnp.float32)
    down_bias_part = jnp.sum(upstream, axis=0)
    unused_value, gelu_pull = jax.vjp(lambda pre: jax.nn.gelu(pre, approximate=True), hidden)
    hidden_grad = gelu_pull(act_grad)[0].astype(jnp.bfloat16)
    in_weight_part = jnp.dot(second_all.T, hidden_grad, preferred_element_type=jnp.float32)
    in_bias_part = jnp.sum(hidden_grad.astype(jnp.float32), axis=0)
    second_grad = lax.psum_scatter(
        jnp.dot(hidden_grad, w_in.T, preferred_element_type=jnp.float32),
        "mp",
        scatter_dimension=0,
        tiled=True,
    )
    middle_part, gain2_part, shift2_part = norm_backward(second_grad, unit2, inverse2, norm2_gain)
    middle_grad = upstream + middle_part
    out_bias_part = jnp.sum(middle_grad, axis=0)
    branch_grad = middle_grad.astype(jnp.bfloat16)
    branch_all = lax.all_gather(branch_grad, "mp", axis=0, tiled=True)
    attended_grad = jnp.dot(branch_all, w_out.T, preferred_element_type=jnp.float32).astype(
        jnp.bfloat16
    )
    out_weight_part = jnp.dot(attended.T, branch_all, preferred_element_type=jnp.float32)
    query_grad, key_grad, value_grad = attend_backward(
        queries, keys, values, split_heads(attended_grad), logsum, segment, block, scale
    )
    projected_grad = jnp.stack(
        [join_heads(query_grad), join_heads(key_grad), join_heads(value_grad)]
    ).astype(jnp.bfloat16)
    qkv_weight_part = jnp.einsum(
        "td,cte->cde", first_all, projected_grad, preferred_element_type=jnp.float32
    )
    qv_bias_part = jnp.stack(
        [
            jnp.sum(projected_grad[0].astype(jnp.float32), axis=0),
            jnp.sum(projected_grad[2].astype(jnp.float32), axis=0),
        ]
    )
    first_grad = lax.psum_scatter(
        jnp.einsum("cte,cde->td", projected_grad, w_qkv, preferred_element_type=jnp.float32).astype(
            jnp.bfloat16
        ),
        "mp",
        scatter_dimension=0,
        tiled=True,
    ).astype(jnp.float32)
    input_part, gain1_part, shift1_part = norm_backward(first_grad, unit1, inverse1, norm1_gain)
    input_grad = (middle_grad + input_part).astype(jnp.bfloat16)
    qkv_weight_grad, out_weight_grad, in_weight_grad, down_weight_grad = (
        lax.psum_scatter(
            qkv_weight_part.astype(jnp.bfloat16), "batch", scatter_dimension=1, tiled=True
        ).astype(jnp.float32),
        lax.psum_scatter(
            out_weight_part.astype(jnp.bfloat16), "batch", scatter_dimension=1, tiled=True
        ).astype(jnp.float32),
        lax.psum_scatter(
            in_weight_part.astype(jnp.bfloat16), "batch", scatter_dimension=0, tiled=True
        ).astype(jnp.float32),
        lax.psum_scatter(
            down_weight_part.astype(jnp.bfloat16), "batch", scatter_dimension=1, tiled=True
        ).astype(jnp.float32),
    )
    qv_full = lax.dynamic_update_slice(
        jnp.zeros((2, width), jnp.float32), qv_bias_part, (jnp.int32(0), column * local_width)
    )
    in_full = lax.dynamic_update_slice(
        jnp.zeros((local_hidden * model_devices,), jnp.float32),
        in_bias_part,
        (column * local_hidden,),
    )
    (
        gain1_grad,
        shift1_grad,
        qv_bias_grad,
        out_bias_grad,
        gain2_grad,
        shift2_grad,
        in_bias_grad,
        down_bias_grad,
    ) = lax.psum(
        (
            gain1_part,
            shift1_part,
            qv_full,
            out_bias_part,
            gain2_part,
            shift2_part,
            in_full,
            down_bias_part,
        ),
        ("batch", "mp"),
    )
    return (
        block_out,
        input_grad,
        gain1_grad,
        shift1_grad,
        qkv_weight_grad,
        qv_bias_grad,
        out_weight_grad,
        out_bias_grad,
        gain2_grad,
        shift2_grad,
        in_weight_grad,
        in_bias_grad,
        down_weight_grad,
        down_bias_grad,
    )


def solution(mesh):
    return jax.shard_map(
        body,
        mesh=mesh,
        in_specs=(
            P(("batch", "mp"), None),
            P(("batch", "mp"), None),
            P(),
            P(),
            P(),
            P(),
            P(),
            P(None, None, "mp"),
            P(None, "mp"),
            P("mp", None),
            P(),
            P(),
            P(),
            P(None, "mp"),
            P("mp"),
            P("mp", None),
            P(),
        ),
        out_specs=(
            P(("batch", "mp"), None),
            P(("batch", "mp"), None),
            P(),
            P(),
            P(None, "batch", "mp"),
            P(),
            P("mp", "batch"),
            P(),
            P(),
            P(),
            P("batch", "mp"),
            P(),
            P("mp", "batch"),
            P(),
        ),
        check_vma=False,
    )
```

profile of v0, /device:TPU:8, one launch (start us, length us, event | category | flops | bytes accessed | tf_op | source)
XLA Modules:
  0.0 1154.0 jit_solution(5623939413086637745)
XLA Ops:
  14.4 55.1 %all-gather.5.cloned.1.call-done = bf16[2048,2048]{1,0:T(8,128)(2,1)} async-done(((bf16[256,2048]{1,0:T(8,128)(2,1)}), bf16[2048,2048]{1,0:T(8,128)(2,1)}) %all-gather.5.cloned.1.call-update) | async-done | bytes 8388624 | tf_op jit(solution)/shard_map/all_gather | solution.py:166
  69.5 9.4 fusion.45
  90.7 3.9 fusion.71
  95.6 49.4 %while.27 = (s32[]{:T(128)}, bf16[4,2,512,128]{3,2,0,1:T(8,128)(2,1)}, f32[4,2,512]{2,1,0:T(2,128)}, s32[4]{0:T(128)S(1)}, s32[2048]{0:T(1024)S(1)}, /*index=5*/...) while((s32[]{:T(128)}, ...), condition=%wide.region_8.9_spmd, body=%wide.region_5.8_spmd.sunk | while | flops 1102052864 | bytes 44878112 | solution.py:74
  98.2 3.3 fusion.135
  147.5 9.6 fusion.82
  157.2 116.0 %reduce-scatter.9.cloned.1.call-done = f32[256,2048]{1,0:T(8,128)} async-done(((f32[2048,2048]{1,0:T(8,128)}), f32[256,2048]{1,0:T(8,128)}) %reduce-scatter.9.cloned.1.call-update) | async-done | bytes 2097168 | tf_op jit(solution)/shard_map/reduce_scatter | solution.py:173
  278.9 53.9 %all-gather.7.cloned.1.call-done = bf16[2048,2048]{1,0:T(8,128)(2,1)} async-done(((bf16[256,2048]{1,0:T(8,128)(2,1)}), bf16[2048,2048]{1,0:T(8,128)(2,1)}) %all-gather.7.cloned.1.call-update) | async-done | bytes 8388624 | tf_op jit(solution)/shard_map/all_gather | solution.py:182
  332.8 14.4 %fusion.83 = f32[2048,1024]{1,0:T(8,128)} fusion(bf16[2048,2048]{1,0:T(8,128)(2,1)} %all-gather.7.cloned.1.call-done, bf16[2048,1024]{1,0:T(8,128)(2,1)} %param.34), kind=kOutput, calls=%fused_computation.137 | convolution fusion | flops 8589934592 | bytes 20971520 | tf_op jit(solution)/shard_map/dot_general | solution.py:183
  347.2 41.8 %all-gather.9.cloned.1.call-done = bf16[2048,2048]{1,0:T(8,128)(2,1)} async-done(((bf16[256,2048]{1,0:T(8,128)(2,1)}), bf16[2048,2048]{1,0:T(8,128)(2,1)}) %all-gather.9.cloned.1.call-update) | async-done | bytes 8388624 | tf_op jit(solution)/shard_map/all_gather | solution.py:193
  389.0 20.8 %convert_reduce_fusion = (f32[1024]{0:T(1024)}, bf16[2048,1024]{1,0:T(8,128)(2,1)S(1)}) fusion(f32[2048,1024]{1,0:T(8,128)} %fusion.83, f32[1024]{0:T(1024)S(1)} %copy-done.34, bf16[2048,2048]{1,0:T(8,128)(2,1)} %all-gather.9.cloned.1.call-done, bf16[1024,2048]{1,0:T(8,128)(2,1)} %param.36), kind=kOutput, calls=%fused_computation.59 | convolution fusion | flops 8638168064 | bytes 25174016 | tf_op jit(solution)/shard_map/dot_general | solution.py:194
  411.7 12.1 %fusion.84 = f32[2048,2048]{1,0:T(8,128)} fusion(bf16[2048,1024]{1,0:T(8,128)(2,1)S(1)} %get-tuple-element.254, bf16[2048,1024]{1,0:T(8,128)(2,1)S(1)} %copy-done.33), kind=kOutput, calls=%fused_computation.138 | convolution fusion | flops 8589934592 | bytes 25165824 | tf_op jit(solution)/shard_map/dot_general | solution.py:202
  423.9 15.8 %convolution_convert_fusion = bf16[2048,2048]{1,0:T(8,128)(2,1)} fusion(bf16[1024,2048]{1,0:T(8,128)(2,1)} %param.36, f32[2048,1024]{1,0:T(8,128)} %fusion.83, f32[1024]{0:T(1024)S(1)} %copy-done.34), kind=kOutput, calls=%fused_computation.61 | convolution fusion | flops 8615100416 | bytes 20975616 | tf_op jit(solution)/shard_map/dot_general | solution.py:186
  439.8 100.2 %reduce-scatter.13.cloned.1.call-done = f32[256,2048]{1,0:T(8,128)} async-done(((f32[2048,2048]{1,0:T(8,128)}), f32[256,2048]{1,0:T(8,128)}) %reduce-scatter.13.cloned.1.call-update) | async-done | bytes 2097168 | tf_op jit(solution)/shard_map/reduce_scatter | solution.py:201
  540.0 3.7 multiply_reduce_fusion.1
  543.7 70.9 %reduce-scatter.11.cloned.1.call-done = bf16[256,2048]{1,0:T(8,128)(2,1)} async-done(((bf16[2048,2048]{1,0:T(8,128)(2,1)}), bf16[256,2048]{1,0:T(8,128)(2,1)}) %reduce-scatter.11.cloned.1.call-update) | async-done | bytes 1048592 | tf_op jit(solution)/shard_map/reduce_scatter | solution.py:185
  614.6 5.8 fusion.77
  622.9 16.7 %convolution_convert_fusion.1 = bf16[1024,2048]{1,0:T(8,128)(2,1)} fusion(bf16[2048,2048]{1,0:T(8,128)(2,1)} %all-gather.9.cloned.1.call-done, f32[2048,1024]{1,0:T(8,128)} %fusion.83, f32[1024]{0:T(1024)S(1)} %copy-done.34), kind=kOutput, calls=%fused_computation.63 | convolution fusion | flops 8613003264 | bytes 20975616 | tf_op jit(solution)/shard_map/dot_general | solution.py:195
  639.7 14.0 %convolution_convert_fusion.2 = bf16[2048,1024]{1,0:T(8,128)(2,1)} fusion(bf16[2048,2048]{1,0:T(8,128)(2,1)} %all-gather.7.cloned.1.call-done, bf16[2048,1024]{1,0:T(8,128)(2,1)} %copy-done.36), kind=kOutput, calls=%fused_computation.64 | convolution fusion | flops 8592031744 | bytes 16777216 | tf_op jit(solution)/shard_map/dot_general | solution.py:199
  653.8 23.5 %all-gather.11.cloned.1.call-done = bf16[2048,2048]{1,0:T(8,128)(2,1)} async-done(((bf16[256,2048]{1,0:T(8,128)(2,1)}), bf16[2048,2048]{1,0:T(8,128)(2,1)}) %all-gather.11.cloned.1.call-update) | async-done | bytes 8388624 | tf_op jit(solution)/shard_map/all_gather | solution.py:211
  677.3 6.9 convolution_convert_fusion.4
  687.7 107.3 %while.28 = (s32[]{:T(128)}, f32[2,2048,128]{2,1,0:T(8,128)}, f32[2,2048,128]{2,1,0:T(8,128)}, bf16[4,2,512,128]{3,2,0,1:T(8,128)(2,1)}, s32[4]{0:T(128)S(1)}, /...) while((s32[]{:T(128)}, f32[2,2048,128]{2,1,0:T(8,128)}, ...), condition=%wide.region_18.19_spmd.clone, body=%wide.region_16.18_spmd.clone.sunk | while | flops 2721709568 | bytes 134789648 | solution.py:119
  693.9 3.8 fusion.150
  697.7 5.3 multiply_reduce_fusion.6
  703.0 4.9 multiply_convert_fusion.5
  709.6 3.6 fusion.149
  720.5 3.8 fusion.150
  724.3 5.3 multiply_reduce_fusion.6
  729.7 5.0 multiply_convert_fusion.5
  736.3 3.6 fusion.149
  747.3 3.8 fusion.150
  751.1 5.3 multiply_reduce_fusion.6
  756.4 4.9 multiply_convert_fusion.5
  762.9 3.6 fusion.149
  773.9 3.8 fusion.150
  777.7 5.3 multiply_reduce_fusion.6
  783.0 4.9 multiply_convert_fusion.5
  789.6 3.6 fusion.149
  795.0 3.6 copy.67
  802.8 9.5 copy.68
  816.5 9.5 copy.69
  830.9 7.0 convolution_convert_fusion.3
  842.6 12.2 %fusion.51 = bf16[3,2048,256]{1,2,0:T(8,128)(2,1)} fusion(bf16[3,2048,256]{2,1,0:T(8,128)(2,1)} %constant_dynamic-update-slice_fusion, bf16[2048,2048]{1,0:T(8,128)(2,1)} %all-gather.5.cloned.1.call-done), kind=kOutput, calls=%fused_computation.72 | convolution fusion | flops 6444023808 | bytes 14680064 | tf_op jit(solution)/shard_map/td,cte->cde/dot_general | solution.py:222
  855.0 10.9 bitcast_convert_fusion
  876.2 51.2 %reduce-scatter.17.cloned.1.call-done = bf16[3,512,256]{1,2,0:T(8,128)(2,1)} async-done(((bf16[3,2048,256]{1,2,0:T(8,128)(2,1)}), bf16[3,512,256]{1,2,0:T(8,128)(2,1)}) %reduce-scatter.17.cloned.1.call-update) | async-done | bytes 786448 | tf_op jit(solution)/shard_map/reduce_scatter | solution.py:242
  930.0 72.6 %reduce-scatter.15.cloned.1.call-done = bf16[256,2048]{1,0:T(8,128)(2,1)} async-done(((bf16[2048,2048]{1,0:T(8,128)(2,1)}), bf16[256,2048]{1,0:T(8,128)(2,1)}) %reduce-scatter.15.cloned.1.call-update) | async-done | bytes 1048592 | tf_op jit(solution)/shard_map/reduce_scatter | solution.py:231
  1005.8 4.0 fusion.66
  1009.8 127.0 %all-reduce.3.cloned.1.call-done = (f32[2048]{0:T(1024)}, f32[2048]{0:T(1024)}, f32[2,2048]{1,0:T(2,128)}, f32[2048]{0:T(1024)}, f32[2048]{0:T(1024)}, /*index=5*/f32[2048]{0:T(1024)}, f32[8192]{0:T(1024)}, f32[2048]{0:T(1024)}) async-done(((f32[2048]{0:T(1024)}, f32[2048]{0:T(1024)}, f32[2,2048]{1,0:T(2,128)}, f32[2048]{0:T(1024)}, f32[2048]{0:T(1024)}, /*index=5*/f32[2048]{0:T(1024)}, f32[8192]{0:T(1024)}, ...) | async-done | bytes 98320 | tf_op jit(solution)/shard_map/psum | solution.py:272
  (298 shorter events, 156.5 us)
Async XLA Ops:
  7.2 62.3 %copy-start = (bf16[3,2048,256]{2,1,0:T(8,128)(2,1)S(1)}, bf16[3,2048,256]{2,1,0:T(8,128)(2,1)}, u32[]{:S(2)}) copy-start(bf16[3,2048,256]{2,1,0:T(8,128)(2,1)} %param.28) | copy-start | bytes 9437188
  7.2 6.7 copy-start.35
  7.2 6.7 copy-start.30
  7.2 6.7 copy-start.32
  7.2 7.1 copy-start.31
  7.2 62.3 %all-gather.5.cloned.1.call-start = ((), (), s32[]{:S(2)}) async-start(), calls=%async_computation.8 | async-start | bytes 9437184 | tf_op jit(solution)/shard_map/all_gather | solution.py:166
  13.8 259.5 %reduce-scatter.9.cloned.1.call-start = ((), (), s32[]{:S(2)}) async-start(), calls=%async_computation.9 | async-start | bytes 18874368 | tf_op jit(solution)/shard_map/reduce_scatter | solution.py:173
  145.0 12.1 %copy-start.16 = (s32[2048]{0:T(1024)}, s32[2048]{0:T(1024)S(1)}, u32[]{:S(2)}) copy-start(s32[2048]{0:T(1024)S(1)} %get-tuple-element.546) | copy-start | bytes 24580
  157.1 116.1 %copy-start.26 = (f32[2048]{0:T(1024)S(1)}, f32[2048]{0:T(1024)}, u32[]{:S(2)}) copy-start(f32[2048]{0:T(1024)} %param.31) | copy-start | bytes 24580
  157.2 119.7 %copy-start.20 = (f32[2048]{0:T(1024)S(1)}, f32[2048]{0:T(1024)}, u32[]{:S(2)}) copy-start(f32[2048]{0:T(1024)} %param.32) | copy-start | bytes 24580
  157.2 119.7 %copy-start.27 = (f32[2048]{0:T(1024)S(1)}, f32[2048]{0:T(1024)}, u32[]{:S(2)}) copy-start(f32[2048]{0:T(1024)} %param.33) | copy-start | bytes 24580
  157.2 175.6 %all-gather.7.cloned.1.call-start = ((), (), s32[]{:S(2)}) async-start(), calls=%async_computation.10 | async-start | bytes 9437184 | tf_op jit(solution)/shard_map/all_gather | solution.py:182
  278.3 110.7 %all-gather.9.cloned.1.call-start = ((), (), s32[]{:S(2)}) async-start(), calls=%async_computation.12 | async-start | bytes 9437184 | tf_op jit(solution)/shard_map/all_gather | solution.py:193
  278.9 110.1 %copy-start.34 = (f32[1024]{0:T(1024)S(1)}, f32[1024]{0:T(1024)}, u32[]{:S(2)}) copy-start(f32[1024]{0:T(1024)} %param.35) | copy-start | bytes 12292
  278.9 261.1 %reduce-scatter.13.cloned.1.call-start = ((), (), s32[]{:S(2)}) async-start(), calls=%async_computation.13 | async-start | bytes 18874368 | tf_op jit(solution)/shard_map/reduce_scatter | solution.py:201
  389.0 22.7 %copy-start.33 = (bf16[2048,1024]{1,0:T(8,128)(2,1)S(1)}, bf16[2048,1024]{1,0:T(8,128)(2,1)}, u32[]{:S(2)}) copy-start(bf16[2048,1024]{1,0:T(8,128)(2,1)} %param.34) | copy-start | bytes 12582916
  423.9 190.7 %reduce-scatter.11.cloned.1.call-start = ((), (), s32[]{:S(2)}) async-start(), calls=%async_computation.11 | async-start | bytes 9437184 | tf_op jit(solution)/shard_map/reduce_scatter | solution.py:185
  439.7 174.9 %copy-start.28 = (f32[2048]{0:T(1024)S(1)}, f32[2048]{0:T(1024)}, u32[]{:S(2)}) copy-start(f32[2048]{0:T(1024)} %param.37) | copy-start | bytes 24580
  439.7 237.6 %all-gather.11.cloned.1.call-start = ((), (), s32[]{:S(2)}) async-start(), calls=%async_computation.14 | async-start | bytes 9437184 | tf_op jit(solution)/shard_map/all_gather | solution.py:211
  622.8 243.9 %reduce-scatter.23.cloned.1.call-start = ((), (), s32[]{:S(2)}) async-start(), calls=%async_computation.19 | async-start | bytes 5242880 | tf_op jit(solution)/shard_map/reduce_scatter | solution.py:251
  639.6 230.0 %reduce-scatter.21.cloned.1.call-start = ((), (), s32[]{:S(2)}) async-start(), calls=%async_computation.18 | async-start | bytes 5242880 | tf_op jit(solution)/shard_map/reduce_scatter | solution.py:248
  653.7 33.9 %copy-start.17 = (s32[2048]{0:T(1024)S(1)}, s32[2048]{0:T(1024)}, u32[]{:S(2)}) copy-start(s32[2048]{0:T(1024)} %copy-done.16) | copy-start | bytes 24580
  653.8 220.6 %reduce-scatter.19.cloned.1.call-start = ((), (), s32[]{:S(2)}) async-start(), calls=%async_computation.17 | async-start | bytes 1310720 | tf_op jit(solution)/shard_map/reduce_scatter | solution.py:245
  693.9 3.8 copy-start.6
  697.7 5.4 copy-start.15
  703.0 4.9 copy-start.1
  703.0 4.9 copy-start.10
  720.5 3.8 copy-start.6
  724.3 5.3 copy-start.15
  729.7 5.0 copy-start.1
  729.7 5.0 copy-start.10
  747.3 3.8 copy-start.6
  751.1 5.3 copy-start.15
  756.4 4.9 copy-start.1
  756.4 4.9 copy-start.10
  773.9 3.8 copy-start.6
  777.7 5.3 copy-start.15
  783.0 5.0 copy-start.1
  783.0 5.0 copy-start.10
  838.0 89.4 %reduce-scatter.17.cloned.1.call-start = ((), (), s32[]{:S(2)}) async-start(), calls=%async_computation.16 | async-start | bytes 3932160 | tf_op jit(solution)/shard_map/reduce_scatter | solution.py:242
  854.9 147.7 %reduce-scatter.15.cloned.1.call-start = ((), (), s32[]{:S(2)}) async-start(), calls=%async_computation.15 | async-start | bytes 9437184 | tf_op jit(solution)/shard_map/reduce_scatter | solution.py:231
  865.9 270.9 %all-reduce.3.cloned.1.call-start = ((), (), s32[]{:S(2)}) async-start(), calls=%async_computation.20 | async-start | bytes 196608 | tf_op jit(solution)/shard_map/psum | solution.py:272
  866.7 7.6 copy-start.18
  869.6 133.0 %copy-start.19 = (f32[2048]{0:T(1024)S(1)}, f32[2048]{0:T(1024)}, u32[]{:S(2)}) copy-start(f32[2048]{0:T(1024)} %param.26) | copy-start | bytes 24580
  869.6 133.0 %copy-start.23 = (f32[256]{0:T(256)S(1)}, f32[256]{0:T(256)}, u32[]{:S(2)}) copy-start(f32[256]{0:T(256)} %copy-done.22) | copy-start | bytes 3076
  869.6 133.0 %copy-start.25 = (f32[256]{0:T(256)S(1)}, f32[256]{0:T(256)}, u32[]{:S(2)}) copy-start(f32[256]{0:T(256)} %copy-done.24) | copy-start | bytes 3076
  869.6 4.4 copy-start.8
  874.4 131.4 %copy-start.21 = (f32[2,2048]{1,0:T(2,128)}, f32[2,2048]{1,0:T(2,128)S(1)}, u32[]{:S(2)}) copy-start(f32[2,2048]{1,0:T(2,128)S(1)} %maximum_dynamic-update-slice_fusion) | copy-start | bytes 49156
  (38 other events, 79.7 us)
Sparse Core Ops, SparseCore 0:
  13.9 55.5 all-gather.4
  157.3 115.9 reduce-scatter.8
  278.4 54.3 all-gather.6
  334.6 54.3 all-gather.8
  424.0 115.9 reduce-scatter.12
  543.3 71.2 reduce-scatter.10
  622.9 54.3 all-gather.10
  679.7 76.7 reduce-scatter.22
  758.8 77.2 reduce-scatter.20
  839.0 25.5 reduce-scatter.18
  866.9 60.4 reduce-scatter.16
  930.7 71.8 reduce-scatter.14
  1011.3 125.4 all-reduce.2
where the time goes:
time: 1170 us; the launch traced here: 1150 us
  waiting for transfers between devices  713 us (61%)
  matrix products  242 us (21%)
  local copies, waits for them, and re-layouts  90.1 us (8%)
  other arithmetic  86.7 us (7%)
  between operations  14.5 us (1%)
    psum x1, waiting for transfers between devices, body(): lax.psum((gain1_part, shift1_part, qv_full, out_bias_part, gain2_part, sh...  127 us
    reduce_scatter x1, waiting for transfers between devices, body(): lax.psum_scatter(jnp.dot(attended, w_out, preferred_element_type=jnp.floa...  116 us
    reduce_scatter x1, waiting for transfers between devices, body(): lax.psum_scatter(jnp.dot(hidden_grad, w_in.T, preferred_element_type=jnp....  100 us
    reduce_scatter x1, waiting for transfers between devices, body(): lax.psum_scatter(jnp.einsum('cte,cde->td', projected_grad, w_qkv, preferr...  72.6 us
    reduce_scatter x1, waiting for transfers between devices, body(): lax.psum_scatter(jnp.dot(activated, w_down, preferred_element_type=jnp.fl...  70.9 us
    all_gather x1, waiting for transfers between devices, body(): first_all = lax.all_gather(first_rows, 'mp', axis=0, tiled=True)  55.1 us
    all_gather x1, waiting for transfers between devices, body(): second_all = lax.all_gather(second_rows, 'mp', axis=0, tiled=True)  53.9 us
    reduce_scatter x1, waiting for transfers between devices, body(): lax.psum_scatter(qkv_weight_part.astype(jnp.bfloat16), 'batch', scatter_d...  51.2 us
  transfers between devices with their start and end apart: 13, of which 10 were waited for; matrix products, arithmetic and copies ran while one was open for 22% of the time, Pallas kernels for 0%

commit v1 on v0

v1 whole, which is shorter than its diff:
```python
import functools

import jax
import jax.numpy as jnp
from jax import lax
from jax.experimental import pallas as pl
from jax.experimental.pallas import tpu as pltpu
from jax.sharding import PartitionSpec as P

HEAD_DIM = 128
EPS = 1e-05
NEGATIVE = -1e30
LOG2E = 1.4426950408889634
f32 = jnp.float32
bf16 = jnp.bfloat16
MESH = pl.DeviceIdType.MESH
ANY = pl.BlockSpec(memory_space=pl.ANY)
VMEM = pl.BlockSpec(memory_space=pltpu.VMEM)
SMEM = pl.BlockSpec(memory_space=pltpu.SMEM)


def dot(left, right, contract_left, contract_right):
    return lax.dot_general(
        left,
        right,
        (((contract_left,), (contract_right,)), ((), ())),
        preferred_element_type=f32,
    )


def flip(index, mask):
    bit = 1
    while bit <= mask:
        if mask & bit:
            index = index + bit * (1 - 2 * lax.rem(lax.div(index, bit), 2))
        bit *= 2
    return index


def loop(count, step, body):
    def one(index, carry):
        body(pl.multiple_of(index * step, step))
        return carry

    lax.fori_loop(0, count // step, one, 0)


class Plan:
    def __init__(self, devices):
        bits = []
        bit = 2
        while bit < devices:
            bits.append(bit)
            bit *= 2
        self.devices = devices
        self.bits = bits
        self.orders = [tuple(bits)] + ([tuple(reversed(bits))] if len(bits) > 1 else [])
        self.parts = len(self.orders)
        self.offsets = list(range(0, devices, 2))
        self.keys = [(part, offset) for part in range(self.parts) for offset in self.offsets if offset]
        self.keys.sort(key=lambda key: (bin(key[1]).count("1"), self.last(*key)))
        self.shares = [(part, offset) for offset in self.offsets for part in range(self.parts)]

    def last(self, part, offset):
        steps = [step for step, bit in enumerate(self.orders[part]) if bit & offset]
        return max(steps) if steps else -1

    def bit(self, part, offset):
        return self.orders[part][self.last(part, offset)]

    def later(self, part, offset):
        order = self.orders[part]
        return [offset | order[step] for step in range(self.last(part, offset) + 1, len(order))]


class Place:
    def __init__(self, plan):
        self.plan = plan
        self.batch = lax.axis_index("batch")
        self.me = lax.axis_index("mp")

    def at(self, mask):
        return (self.batch, flip(self.me, mask))

    def barrier(self):
        semaphore = pltpu.get_barrier_semaphore()
        masks = [1] + self.plan.bits
        for mask in masks:
            pl.semaphore_signal(semaphore, inc=1, device_id=self.at(mask), device_id_type=MESH)
        pl.semaphore_wait(semaphore, len(masks))


class Gather:
    def __init__(self, place, buf, own, rows, sems):
        self.place, self.plan, self.buf, self.own, self.rows = place, place.plan, buf, own, rows
        self.link_send, self.link_recv, self.core_send, self.core_recv = sems
        self.part_rows = rows // self.plan.parts

    def span(self, mask, part):
        block = flip(self.place.me, mask)
        start = block * self.rows + part * self.part_rows
        return self.buf.at[pl.ds(pl.multiple_of(start, self.part_rows), self.part_rows), :]

    def source(self, offset, part):
        if offset == 0 and self.own is not None:
            return self.own.at[pl.ds(part * self.part_rows, self.part_rows), :]
        return self.span(offset, part)

    def link(self, key):
        part, offset = key
        bit = self.plan.bit(part, offset)
        index = self.plan.keys.index(key)
        return pltpu.make_async_remote_copy(
            src_ref=self.source(offset ^ bit, part),
            dst_ref=self.span(offset ^ bit, part),
            send_sem=self.link_send.at[index],
            recv_sem=self.link_recv.at[index],
            device_id=self.place.at(bit),
            device_id_type=MESH,
        )

    def core(self, key):
        part, offset = key
        index = self.plan.shares.index(key)
        return pltpu.make_async_remote_copy(
            src_ref=self.source(offset, part),
            dst_ref=self.span(offset, part),
            send_sem=self.core_send.at[index],
            recv_sem=self.core_recv.at[index],
            device_id=self.place.at(1),
            device_id_type=MESH,
        )

    def landed(self, ref, semaphore):
        pltpu.make_async_remote_copy(
            src_ref=ref,
            dst_ref=ref,
            send_sem=semaphore,
            recv_sem=semaphore,
            device_id=self.place.at(1),
            device_id_type=MESH,
        ).wait_recv()

    def start(self):
        for part in range(self.plan.parts):
            self.core((part, 0)).start()
        for key in self.plan.keys:
            if bin(key[1]).count("1") == 1:
                self.link(key).start()

    def arrive(self, key):
        part, offset = key
        self.landed(self.span(offset, part), self.link_recv.at[self.plan.keys.index(key)])
        for target in self.plan.later(part, offset):
            self.link((part, target)).start()
        self.core(key).start()

    def share(self, offset):
        for part in range(self.plan.parts):
            index = self.plan.shares.index((part, offset))
            self.landed(self.span(offset | 1, part), self.core_recv.at[index])

    def steps(self):
        singles = [offset for offset in self.plan.offsets if bin(offset).count("1") == 1]
        rest = [offset for offset in self.plan.offsets if bin(offset).count("1") > 1]
        rest.sort(key=lambda offset: bin(offset).count("1"))
        groups = [[key for key in self.plan.keys if key[1] in singles]]
        groups += [[key for key in self.plan.keys if key[1] == offset] for offset in rest]
        return groups, [singles] + [[offset] for offset in rest]

    def finish(self):
        for key in self.plan.keys:
            self.link(key).wait_send()
        for key in self.plan.shares:
            self.core(key).wait_send()

    @staticmethod
    def semaphores(plan):
        return [pltpu.SemaphoreType.DMA((len(plan.keys),))] * 2 + [
            pltpu.SemaphoreType.DMA((len(plan.shares),))
        ] * 2


class Scatter:
    def __init__(self, place, rows, width, core_out, core_in, kept, link_out, link_in, sems):
        self.place, self.plan, self.rows, self.width = place, place.plan, rows, width
        self.core_out, self.core_in, self.kept = core_out, core_in, kept
        self.link_out, self.link_in = link_out, link_in
        self.link_send, self.link_recv, self.core_send, self.core_recv = sems
        self.part_rows = rows // self.plan.parts
        self.step = min(32, self.part_rows)
        self.order = sorted(self.plan.offsets, key=lambda offset: -bin(offset).count("1"))

    def core(self, offset):
        index = offset // 2
        return pltpu.make_async_remote_copy(
            src_ref=self.core_out.at[index],
            dst_ref=self.core_in.at[index],
            send_sem=self.core_send.at[index],
            recv_sem=self.core_recv.at[index],
            device_id=self.place.at(1),
            device_id_type=MESH,
        )

    def link(self, key):
        index = self.plan.keys.index(key)
        return pltpu.make_async_remote_copy(
            src_ref=self.link_out.at[index],
            dst_ref=self.link_in.at[index],
            send_sem=self.link_send.at[index],
            recv_sem=self.link_recv.at[index],
            device_id=self.place.at(self.plan.bit(*key)),
            device_id_type=MESH,
        )

    def total(self, offset, part, start, arrived):
        rows = pl.ds(pl.multiple_of(part * self.part_rows + start, self.step), self.step)
        value = self.kept[offset // 2, rows, :].astype(f32) + self.core_in[offset // 2, rows, :].astype(f32)
        for key in arrived:
            value += self.link_in[self.plan.keys.index(key), pl.ds(start, self.step), :].astype(f32)
        return value

    def pass_on(self, part, offset):
        arrived = [(part, target) for target in self.plan.later(part, offset)]
        for key in arrived:
            self.link(key).wait_recv()
        index = self.plan.keys.index((part, offset))

        def add(start):
            self.link_out[index, pl.ds(start, self.step), :] = self.total(
                offset, part, start, arrived
            ).astype(bf16)

        loop(self.part_rows, self.step, add)
        self.link((part, offset)).start()

    def begin(self, partial):
        for offset in self.order:
            index = offset // 2
            partial(flip(self.place.me, offset | 1), self.core_out.at[index])
            self.core(offset).start()
            partial(flip(self.place.me, offset), self.kept.at[index])
            self.core(offset).wait_recv()
            for part in range(self.plan.parts):
                if offset and not self.plan.later(part, offset):
                    self.pass_on(part, offset)

    def middle(self):
        for offset in self.order:
            for part in range(self.plan.parts):
                if offset and self.plan.later(part, offset):
                    self.pass_on(part, offset)

    def end(self, use):
        for part in range(self.plan.parts):
            arrived = [(part, target) for target in self.plan.later(part, 0)]
            for key in arrived:
                self.link(key).wait_recv()

            def piece(start):
                row = pl.multiple_of(part * self.part_rows + start, self.step)
                use(row, self.step, self.total(0, part, start, arrived))

            loop(self.part_rows, self.step, piece)

    def finish(self):
        for key in self.plan.keys:
            self.link(key).wait_send()
        for offset in self.plan.offsets:
            self.core(offset).wait_send()

    @staticmethod
    def scratch(plan, rows, width, kept):
        chips, keys = len(plan.offsets), len(plan.keys)
        return [
            pltpu.VMEM((chips, rows, width), bf16),
            pltpu.VMEM((chips, rows, width), bf16),
            pltpu.VMEM((chips, rows, width), kept),
            pltpu.VMEM((keys, rows // plan.parts, width), bf16),
            pltpu.VMEM((keys, rows // plan.parts, width), bf16),
            pltpu.SemaphoreType.DMA((keys,)),
            pltpu.SemaphoreType.DMA((keys,)),
            pltpu.SemaphoreType.DMA((chips,)),
            pltpu.SemaphoreType.DMA((chips,)),
        ]


class Moves:
    def __init__(self, sems):
        self.sems, self.count = sems, 0

    def start(self, source, target):
        copy = pltpu.make_async_copy(source, target, self.sems.at[self.count])
        self.count += 1
        copy.start()
        return copy


def norm_rows(rows):
    mean = jnp.mean(rows, axis=-1, keepdims=True)
    centred = rows - mean
    inverse = lax.rsqrt(jnp.mean(centred * centred, axis=-1, keepdims=True) + EPS)
    return centred * inverse, inverse


def norm_back(grad, unit, inverse, gain):
    scaled = grad * gain
    return inverse * (
        scaled
        - jnp.mean(scaled, axis=-1, keepdims=True)
        - unit * jnp.mean(scaled * unit, axis=-1, keepdims=True)
    )


def segment_starts(bounds, rows):
    position = lax.broadcasted_iota(jnp.int32, (1, rows), 1)
    first = jnp.zeros((1, rows), jnp.int32)
    for index in range(bounds.shape[0]):
        first = jnp.maximum(first, jnp.where(position >= bounds[index], bounds[index], 0))
    return first


def head_columns(part, head, width):
    return pl.ds(part * width + head * HEAD_DIM, HEAD_DIM)


def first_kernel(
    plan, block, tok, gain, shift, w_qkv, qv_bias, bounds, out_grad, first_out, qkv_out, att_out,
    sum_out, grad_out, buf, weights, qkv, starts, sums, attended, local, *sems,
):
    place = Place(plan)
    own, depth = tok.shape
    rows = buf.shape[0]
    width = w_qkv.shape[2]
    moves = Moves(local)
    loads = [
        moves.start(w_qkv.at[part], weights.at[:, pl.ds(part * width, width)]) for part in range(3)
    ]
    place.barrier()
    step = min(32, own)
    mine = pl.multiple_of(place.me * own, own)

    def normalise(start):
        unit, _ = norm_rows(tok[pl.ds(start, step), :].astype(f32))
        buf[pl.ds(pl.multiple_of(mine + start, step), step), :] = (unit * gain[...] + shift[...]).astype(bf16)

    loop(own, step, normalise)
    gather = Gather(place, buf, None, own, sems[:4])
    gather.start()
    stores = [moves.start(out_grad, grad_out.at[pl.ds(mine, own), :])]
    starts[...] = segment_starts(bounds, rows)
    for copy in loads:
        copy.wait()

    def project(offset):
        chip = lax.div(flip(place.me, offset), 2)
        span = pl.ds(pl.multiple_of(chip * 2 * own, 2 * own), 2 * own)
        stores.append(moves.start(buf.at[span, :], first_out.at[span, :]))
        qkv[span, :] = (dot(buf[span, :], weights[...], 1, 0) + qv_bias[...]).astype(bf16)

    gather.share(0)
    project(0)
    arrivals, chips = gather.steps()
    for keys, offsets in zip(arrivals, chips):
        for key in keys:
            gather.arrive(key)
        for offset in offsets:
            gather.share(offset)
            project(offset)
    gather.finish()
    gather = Gather(place, grad_out, out_grad, own, sems[4:])
    gather.start()
    stores.append(moves.start(qkv, qkv_out))

    scale = HEAD_DIM ** (-0.5) * LOG2E
    heads = width // HEAD_DIM
    row_in = lax.broadcasted_iota(jnp.int32, (block, block), 0)
    col_in = lax.broadcasted_iota(jnp.int32, (block, block), 1)
    key_in = lax.broadcasted_iota(jnp.int32, (block, 1), 0)

    def attend(index):
        span = pl.ds(index * block, block)
        first = starts[:, span]
        queries = [qkv[span, head_columns(0, head, width)] for head in range(heads)]

        def against(key_block, carry, diagonal):
            key_span = pl.ds(pl.multiple_of(key_block * block, block), block)
            allowed = key_in + key_block * block >= first
            if diagonal:
                allowed = allowed & (row_in <= col_in)
            result = []
            for head in range(heads):
                top, total, mixed = carry[head]
                keys = qkv[key_span, head_columns(1, head, width)]
                values = qkv[key_span, head_columns(2, head, width)]
                scores = jnp.where(allowed, dot(keys, queries[head], 1, 1) * scale, NEGATIVE)
                new_top = jnp.maximum(top, jnp.max(scores, axis=0, keepdims=True))
                exps = jnp.exp2(scores - new_top)
                fade = jnp.exp2(top - new_top)
                total = total * fade + jnp.sum(exps, axis=0, keepdims=True)
                mixed = mixed * fade + dot(values, exps.astype(bf16), 0, 0)
                result.append((new_top, total, mixed))
            return tuple(result)

        carry = tuple(
            (
                jnp.full((1, block), NEGATIVE, f32),
                jnp.zeros((1, block), f32),
                jnp.zeros((HEAD_DIM, block), f32),
            )
            for head in range(heads)
        )
        if index:
            carry = lax.fori_loop(0, index, lambda key_block, c: against(key_block, c, False), carry)
        carry = against(index, carry, True)
        for head in range(heads):
            top, total, mixed = carry[head]
            attended[span, pl.ds(head * HEAD_DIM, HEAD_DIM)] = (mixed * (1.0 / total)).T.astype(bf16)
            sums[pl.ds(head, 1), span] = top + jnp.log2(total)

    blocks = rows // block
    groups = list(zip(arrivals, chips))
    taken = 0
    for index in range(blocks):
        attend(index)
        if index >= blocks - 2 and taken < len(groups):
            for key in groups[taken][0]:
                gather.arrive(key)
            taken += 1
    stores.append(moves.start(attended, att_out))
    stores.append(moves.start(sums, sum_out))
    while taken < len(groups):
        for key in groups[taken][0]:
            gather.arrive(key)
        taken += 1
    for offset in plan.offsets:
        gather.share(offset)
    gather.finish()
    for copy in stores:
        copy.wait()


def params(number):
    return pltpu.CompilerParams(
        collective_id=number, has_side_effects=True, vmem_limit_bytes=62 * 2**20
    )


def run_first(plan, block, tok, gain, shift, w_qkv, qv_bias, bounds, out_grad):
    own, depth = tok.shape
    rows = own * plan.devices
    width = w_qkv.shape[2]
    heads = width // HEAD_DIM
    return pl.pallas_call(
        functools.partial(first_kernel, plan, block),
        out_shape=(
            jax.ShapeDtypeStruct((rows, depth), bf16),
            jax.ShapeDtypeStruct((rows, 3 * width), bf16),
            jax.ShapeDtypeStruct((rows, width), bf16),
            jax.ShapeDtypeStruct((8, rows), f32),
            jax.ShapeDtypeStruct((rows, depth), bf16),
        ),
        in_specs=[VMEM, VMEM, VMEM, ANY, VMEM, SMEM, ANY],
        out_specs=(ANY,) * 5,
        scratch_shapes=[
            pltpu.VMEM((rows, depth), bf16),
            pltpu.VMEM((depth, 3 * width), bf16),
            pltpu.VMEM((rows, 3 * width), bf16),
            pltpu.VMEM((1, rows), jnp.int32),
            pltpu.VMEM((8, rows), f32),
            pltpu.VMEM((rows, width), bf16),
            pltpu.SemaphoreType.DMA((16,)),
        ]
        + Gather.semaphores(plan) * 2,
        compiler_params=params(0),
        name="first",
    )(tok, gain, shift, w_qkv, qv_bias, bounds, out_grad)


def feed_kernel(
    plan, tok, att, w_out, out_bias, gain, shift, w_in, in_bias, w_down, grad_all,
    second_out, act_out, hidden_out, middle_out, bias_out,
    att_in, w_o, w_i, w_d, grad_in, buf, act, back, middle, local, *rest,
):
    scatter_refs, gather_sems = rest[:9], rest[9:]
    place = Place(plan)
    own, depth = tok.shape
    rows = buf.shape[0]
    hidden_width = w_in.shape[1]
    chip_rows = 2 * own
    moves = Moves(local)
    load_att = moves.start(att, att_in)
    load_out = moves.start(w_out, w_o)
    load_in = moves.start(w_in, w_i)
    load_down = moves.start(w_down, w_d)
    place.barrier()
    scatter = Scatter(place, own, depth, *scatter_refs[:5], scatter_refs[5:])
    load_att.wait()
    load_out.wait()
    tile = min(1024, depth)

    def partial(owner, target):
        lines = att_in[pl.ds(pl.multiple_of(owner * own, own), own), :]

        def columns(start):
            target[:, pl.ds(start, tile)] = dot(lines, w_o[:, pl.ds(start, tile)], 1, 0).astype(target.dtype)

        loop(depth, tile, columns)

    scatter.begin(partial)
    scatter.middle()
    mine = pl.multiple_of(place.me * own, own)

    def close(start, count, value):
        span = pl.ds(start, count)
        total = tok[span, :].astype(f32) + value + out_bias[...]
        middle[span, :] = total
        unit, _ = norm_rows(total)
        buf[pl.ds(pl.multiple_of(mine + start, count), count), :] = (unit * gain[...] + shift[...]).astype(bf16)

    scatter.end(close)
    gather = Gather(place, buf, None, own, gather_sems)
    gather.start()
    scatter.finish()
    stores = [moves.start(middle, middle_out)]
    load_in.wait()
    load_down.wait()
    bias_out[...] = jnp.zeros_like(bias_out)
    part_cols = min(512, hidden_width)

    def chip_span(offset):
        chip = lax.div(flip(place.me, offset), 2)
        return pl.ds(pl.multiple_of(chip * chip_rows, chip_rows), chip_rows)

    order = []

    def prefetch(offset):
        slot = len(order) % 2
        order.append(moves.start(grad_all.at[chip_span(offset), :], grad_in.at[slot]))

    def expand(offset, slot):
        span = chip_span(offset)
        stores.append(moves.start(buf.at[span, :], second_out.at[span, :]))
        order[slot].wait()

        def columns(start):
            cols = pl.ds(start, part_cols)
            pre = dot(buf[span, :], w_i[:, cols], 1, 0) + in_bias[:, cols]
            up = dot(grad_in[slot % 2], w_d[cols, :], 1, 1)
            root = 0.7978845608028654
            square = pre * pre
            inner = jnp.tanh(root * (pre + 0.044715 * (square * pre)))
            half = 0.5 * (1.0 + inner)
            slope = half + 0.5 * pre * (1.0 - inner * inner) * (root * (1.0 + 3 * 0.044715 * square))
            act[span, cols] = (pre * half).astype(bf16)
            down = (up * slope).astype(bf16)
            back[span, cols] = down
            bias_out[:, cols] += jnp.sum(down.astype(f32), axis=0, keepdims=True)

        loop(hidden_width, part_cols, columns)
        stores.append(moves.start(act.at[span, :], act_out.at[span, :]))
        stores.append(moves.start(back.at[span, :], hidden_out.at[span, :]))

    arrivals, chips = gather.steps()
    sequence = [0] + [offset for offsets in chips for offset in offsets]
    prefetch(sequence[0])
    prefetch(sequence[1])
    gather.share(0)
    expand(0, 0)
    number = 1
    for keys, offsets in zip(arrivals, chips):
        for key in keys:
            gather.arrive(key)
        for offset in offsets:
            if number + 1 < len(sequence):
                prefetch(sequence[number + 1])
            gather.share(offset)
            expand(offset, number)
            number += 1
    gather.finish()
    for copy in stores:
        copy.wait()


def run_feed(plan, tok, att, w_out, out_bias, gain, shift, w_in, in_bias, w_down, grad_all):
    own, depth = tok.shape
    rows = own * plan.devices
    width = att.shape[1]
    hidden = w_in.shape[1]
    return pl.pallas_call(
        functools.partial(feed_kernel, plan),
        out_shape=(
            jax.ShapeDtypeStruct((rows, depth), bf16),
            jax.ShapeDtypeStruct((rows, hidden), bf16),
            jax.ShapeDtypeStruct((rows, hidden), bf16),
            jax.ShapeDtypeStruct((own, depth), f32),
            jax.ShapeDtypeStruct((1, hidden), f32),
        ),
        in_specs=[VMEM, ANY, ANY, VMEM, VMEM, VMEM, ANY, VMEM, ANY, ANY],
        out_specs=(ANY, ANY, ANY, ANY, VMEM),
        scratch_shapes=[
            pltpu.VMEM((rows, width), bf16),
            pltpu.VMEM((width, depth), bf16),
            pltpu.VMEM((depth, hidden), bf16),
            pltpu.VMEM((hidden, depth), bf16),
            pltpu.VMEM((2, 2 * own, depth), bf16),
            pltpu.VMEM((rows, depth), bf16),
            pltpu.VMEM((rows, hidden), bf16),
            pltpu.VMEM((rows, hidden), bf16),
            pltpu.VMEM((own, depth), f32),
            pltpu.SemaphoreType.DMA((48,)),
        ]
        + Scatter.scratch(plan, own, depth, bf16)
        + Gather.semaphores(plan),
        compiler_params=params(1),
        name="feed",
    )(tok, att, w_out, out_bias, gain, shift, w_in, in_bias, w_down, grad_all)


def middle_kernel(
    plan, hidden_grad, w_in, middle, out_grad, gain, w_out,
    middle_grad_out, branch_out, att_grad_out, sums_out,
    h_in, w_i, w_o, buf, middle_grad, att_grad, local, *rest,
):
    scatter_refs, gather_sems = rest[:9], rest[9:]
    place = Place(plan)
    own, depth = middle.shape
    chip_rows = 2 * own
    moves = Moves(local)
    loads = [moves.start(hidden_grad, h_in), moves.start(w_in, w_i)]
    load_out = moves.start(w_out, w_o)
    place.barrier()
    scatter = Scatter(place, own, depth, *scatter_refs[:5], scatter_refs[5:])
    for copy in loads:
        copy.wait()
    tile = min(1024, depth)

    def partial(owner, target):
        lines = h_in[pl.ds(pl.multiple_of(owner * own, own), own), :]

        def columns(start):
            target[:, pl.ds(start, tile)] = dot(lines, w_i[pl.ds(start, tile), :], 1, 1).astype(target.dtype)

        loop(depth, tile, columns)

    scatter.begin(partial)
    scatter.middle()
    mine = pl.multiple_of(place.me * own, own)
    sums_out[...] = jnp.zeros_like(sums_out)

    def close(start, count, value):
        span = pl.ds(start, count)
        unit, inverse = norm_rows(middle[span, :])
        total = out_grad[span, :].astype(f32) + norm_back(value, unit, inverse, gain[...])
        middle_grad[span, :] = total
        buf[pl.ds(pl.multiple_of(mine + start, count), count), :] = total.astype(bf16)
        sums_out[0:1, :] += jnp.sum(value * unit, axis=0, keepdims=True)
        sums_out[1:2, :] += jnp.sum(value, axis=0, keepdims=True)
        sums_out[2:3, :] += jnp.sum(total, axis=0, keepdims=True)
        sums_out[3:4, :] += jnp.sum(out_grad[span, :].astype(f32), axis=0, keepdims=True)

    scatter.end(close)
    gather = Gather(place, buf, None, own, gather_sems)
    gather.start()
    scatter.finish()
    stores = [moves.start(middle_grad, middle_grad_out)]
    load_out.wait()

    def project(offset):
        chip = lax.div(flip(place.me, offset), 2)
        span = pl.ds(pl.multiple_of(chip * chip_rows, chip_rows), chip_rows)
        stores.append(moves.start(buf.at[span, :], branch_out.at[span, :]))
        att_grad[span, :] = dot(buf[span, :], w_o[...], 1, 1).astype(bf16)

    gather.share(0)
    project(0)
    arrivals, chips = gather.steps()
    for keys, offsets in zip(arrivals, chips):
        for key in keys:
            gather.arrive(key)
        for offset in offsets:
            gather.share(offset)
            project(offset)
    stores.append(moves.start(att_grad, att_grad_out))
    gather.finish()
    for copy in stores:
        copy.wait()


def run_middle(plan, hidden_grad, w_in, middle, out_grad, gain, w_out):
    own, depth = middle.shape
    rows = own * plan.devices
    width = w_out.shape[0]
    hidden = w_in.shape[1]
    return pl.pallas_call(
        functools.partial(middle_kernel, plan),
        out_shape=(
            jax.ShapeDtypeStruct((own, depth), f32),
            jax.ShapeDtypeStruct((rows, depth), bf16),
            jax.ShapeDtypeStruct((rows, width), bf16),
            jax.ShapeDtypeStruct((8, depth), f32),
        ),
        in_specs=[ANY, ANY, VMEM, VMEM, VMEM, ANY],
        out_specs=(ANY, ANY, ANY, VMEM),
        scratch_shapes=[
            pltpu.VMEM((rows, hidden), bf16),
            pltpu.VMEM((depth, hidden), bf16),
            pltpu.VMEM((width, depth), bf16),
            pltpu.VMEM((rows, depth), bf16),
            pltpu.VMEM((own, depth), f32),
            pltpu.VMEM((rows, width), bf16),
            pltpu.SemaphoreType.DMA((16,)),
        ]
        + Scatter.scratch(plan, own, depth, f32)
        + Gather.semaphores(plan),
        compiler_params=params(2),
        name="middle",
    )(hidden_grad, w_in, middle, out_grad, gain, w_out)


def back_kernel(
    plan, block, bounds, qkv, att, att_grad, sums, activated, w_down, middle, down_bias,
    qkv_grad_out, block_out, bias_out,
    qkv_in, att_in, grad_in, act_in, w_d, starts, key_grad, value_grad, result, local, *rest,
):
    place = Place(plan)
    own, depth = middle.shape
    rows = qkv_in.shape[0]
    width = att_in.shape[1]
    heads = width // HEAD_DIM
    moves = Moves(local)
    feeds = [moves.start(activated, act_in), moves.start(w_down, w_d)]
    loads = [moves.start(qkv, qkv_in), moves.start(att, att_in), moves.start(att_grad, grad_in)]
    place.barrier()
    scatter = Scatter(place, own, depth, *rest[:5], rest[5:])
    for copy in feeds:
        copy.wait()
    tile = min(1024, depth)

    def partial(owner, target):
        lines = act_in[pl.ds(pl.multiple_of(owner * own, own), own), :]

        def columns(start):
            target[:, pl.ds(start, tile)] = dot(lines, w_d[:, pl.ds(start, tile)], 1, 0).astype(target.dtype)

        loop(depth, tile, columns)

    scatter.begin(partial)
    starts[...] = segment_starts(bounds, rows)
    bias_out[...] = jnp.zeros_like(bias_out)
    key_grad[...] = jnp.zeros_like(key_grad)
    value_grad[...] = jnp.zeros_like(value_grad)
    for copy in loads:
        copy.wait()
    scale = HEAD_DIM ** (-0.5)
    row_in = lax.broadcasted_iota(jnp.int32, (block, block), 0)
    col_in = lax.broadcasted_iota(jnp.int32, (block, block), 1)
    key_in = lax.broadcasted_iota(jnp.int32, (block, 1), 0)

    def attend(index):
        span = pl.ds(index * block, block)
        first = starts[:, span]
        queries, outer, inner, logs = [], [], [], []
        for head in range(heads):
            columns = pl.ds(head * HEAD_DIM, HEAD_DIM)
            queries.append(qkv_in[span, head_columns(0, head, width)])
            outer.append(grad_in[span, columns])
            product = grad_in[span, columns].astype(f32) * att_in[span, columns].astype(f32)
            inner.append(jnp.sum(product.T, axis=0, keepdims=True))
            logs.append(sums[pl.ds(head, 1), span])

        def against(key_block, carry, diagonal):
            key_span = pl.ds(pl.multiple_of(key_block * block, block), block)
            allowed = key_in + key_block * block >= first
            if diagonal:
                allowed = allowed & (row_in <= col_in)
            result = []
            for head in range(heads):
                columns = pl.ds(head * HEAD_DIM, HEAD_DIM)
                keys = qkv_in[key_span, head_columns(1, head, width)]
                values = qkv_in[key_span, head_columns(2, head, width)]
                scores = dot(keys, queries[head], 1, 1) * (scale * LOG2E)
                probs = jnp.exp2(jnp.where(allowed, scores - logs[head], NEGATIVE))
                value_grad[key_span, columns] += dot(probs.astype(bf16), outer[head], 1, 0)
                prob_grad = dot(values, outer[head], 1, 1)
                score_grad = (probs * (prob_grad - inner[head])).astype(bf16)
                key_grad[key_span, columns] += dot(score_grad, queries[head], 1, 0)
                result.append(carry[head] + dot(score_grad, keys, 0, 0))
            return tuple(result)

        carry = tuple(jnp.zeros((block, HEAD_DIM), f32) for head in range(heads))
        if index:
            carry = lax.fori_loop(0, index, lambda key_block, c: against(key_block, c, False), carry)
        carry = against(index, carry, True)
        for head in range(heads):
            query_grad = (carry[head] * scale).astype(bf16)
            qkv_in[span, head_columns(0, head, width)] = query_grad
            columns = pl.ds(head * HEAD_DIM, HEAD_DIM)
            bias_out[0:1, columns] += jnp.sum(query_grad.astype(f32), axis=0, keepdims=True)

    blocks = rows // block
    for index in range(blocks):
        attend(index)
        if index == blocks // 2:
            scatter.middle()
    kept = min(256, rows)

    def write(start):
        span = pl.ds(start, kept)
        qkv_in[span, pl.ds(width, width)] = (key_grad[span, :] * scale).astype(bf16)
        rounded = value_grad[span, :].astype(bf16)
        qkv_in[span, pl.ds(2 * width, width)] = rounded
        bias_out[1:2, :] += jnp.sum(rounded.astype(f32), axis=0, keepdims=True)

    loop(rows, kept, write)
    stores = [moves.start(qkv_in, qkv_grad_out)]

    def close(start, count, value):
        span = pl.ds(start, count)
        result[span, :] = (middle[span, :] + value + down_bias[...]).astype(bf16)

    scatter.end(close)
    stores.append(moves.start(result, block_out))
    scatter.finish()
    for copy in stores:
        copy.wait()


def run_back(plan, block, bounds, qkv, att, att_grad, sums, activated, w_down, middle, down_bias):
    own, depth = middle.shape
    rows, width = att.shape
    hidden = w_down.shape[0]
    return pl.pallas_call(
        functools.partial(back_kernel, plan, block),
        out_shape=(
            jax.ShapeDtypeStruct((rows, 3 * width), bf16),
            jax.ShapeDtypeStruct((own, depth), bf16),
            jax.ShapeDtypeStruct((8, width), f32),
        ),
        in_specs=[SMEM, ANY, ANY, ANY, VMEM, ANY, ANY, VMEM, VMEM],
        out_specs=(ANY, ANY, VMEM),
        scratch_shapes=[
            pltpu.VMEM((rows, 3 * width), bf16),
            pltpu.VMEM((rows, width), bf16),
            pltpu.VMEM((rows, width), bf16),
            pltpu.VMEM((rows, hidden), bf16),
            pltpu.VMEM((hidden, depth), bf16),
            pltpu.VMEM((1, rows), jnp.int32),
            pltpu.VMEM((rows, width), f32),
            pltpu.VMEM((rows, width), f32),
            pltpu.VMEM((own, depth), bf16),
            pltpu.SemaphoreType.DMA((16,)),
        ]
        + Scatter.scratch(plan, own, depth, f32),
        compiler_params=params(3),
        name="back",
    )(bounds, qkv, att, att_grad, sums, activated, w_down, middle, down_bias)


def last_kernel(
    plan, qkv_grad, w_qkv, tok, middle_grad, gain, input_out, sums_out, g_in, weights, result, local, *rest
):
    place = Place(plan)
    own, depth = tok.shape
    width = w_qkv.shape[2]
    moves = Moves(local)
    loads = [
        moves.start(w_qkv.at[part], weights.at[:, pl.ds(part * width, width)]) for part in range(3)
    ]
    loads.append(moves.start(qkv_grad, g_in))
    place.barrier()
    scatter = Scatter(place, own, depth, *rest[:5], rest[5:])
    for copy in loads:
        copy.wait()
    tile = min(1024, depth)

    def partial(owner, target):
        lines = g_in[pl.ds(pl.multiple_of(owner * own, own), own), :]

        def columns(start):
            target[:, pl.ds(start, tile)] = dot(lines, weights[pl.ds(start, tile), :], 1, 1).astype(target.dtype)

        loop(depth, tile, columns)

    scatter.begin(partial)
    scatter.middle()
    sums_out[...] = jnp.zeros_like(sums_out)

    def close(start, count, value):
        span = pl.ds(start, count)
        unit, inverse = norm_rows(tok[span, :].astype(f32))
        total = middle_grad[span, :] + norm_back(value, unit, inverse, gain[...])
        result[span, :] = total.astype(bf16)
        sums_out[0:1, :] += jnp.sum(value * unit, axis=0, keepdims=True)
        sums_out[1:2, :] += jnp.sum(value, axis=0, keepdims=True)

    scatter.end(close)
    store = moves.start(result, input_out)
    scatter.finish()
    store.wait()


def run_last(plan, qkv_grad, w_qkv, tok, middle_grad, gain):
    own, depth = tok.shape
    rows = qkv_grad.shape[0]
    width = w_qkv.shape[2]
    return pl.pallas_call(
        functools.partial(last_kernel, plan),
        out_shape=(
            jax.ShapeDtypeStruct((own, depth), bf16),
            jax.ShapeDtypeStruct((8, depth), f32),
        ),
        in_specs=[ANY, ANY, VMEM, VMEM, VMEM],
        out_specs=(ANY, VMEM),
        scratch_shapes=[
            pltpu.VMEM((rows, 3 * width), bf16),
            pltpu.VMEM((depth, 3 * width), bf16),
            pltpu.VMEM((own, depth), bf16),
            pltpu.SemaphoreType.DMA((8,)),
        ]
        + Scatter.scratch(plan, own, depth, f32),
        compiler_params=params(4),
        name="last",
    )(qkv_grad, w_qkv, tok, middle_grad, gain)


def segment_bounds(group, seq_lengths, seq_scripts, seq_place):
    count = seq_lengths.shape[0]
    numbers = jnp.arange(count, dtype=jnp.int32)
    order_key = seq_scripts * count + numbers
    same = seq_place[:, None] == seq_place[None, :]
    before = order_key[None, :] < order_key[:, None]
    offsets = jnp.sum(jnp.where(same & before, seq_lengths[None, :], 0), axis=1)
    mine = seq_place == group
    firsts = jnp.where(mine, offsets, 0)
    total = jnp.sum(jnp.where(mine, seq_lengths, 0))
    return jnp.concatenate([firsts, total[None]]).astype(jnp.int32)


def body(
    tokens,
    out_grad,
    seq_lengths,
    seq_scripts,
    seq_place,
    norm1_gain,
    norm1_shift,
    w_qkv,
    qv_bias,
    w_out,
    out_bias,
    norm2_gain,
    norm2_shift,
    w_in,
    in_bias,
    w_down,
    down_bias,
):
    own, depth = tokens.shape
    devices = lax.axis_size("mp")
    plan = Plan(devices)
    rows = own * devices
    width = w_qkv.shape[2]
    hidden = w_in.shape[1]
    block = min(512, rows)
    column = lax.axis_index("mp")
    bounds = segment_bounds(lax.axis_index("batch"), seq_lengths, seq_scripts, seq_place)

    def line(vector):
        return vector.reshape(1, -1)

    bias3 = jnp.concatenate([qv_bias[0], jnp.zeros_like(qv_bias[0]), qv_bias[1]])
    first_all, qkv, att, sums, grad_all = run_first(
        plan, block, tokens, line(norm1_gain), line(norm1_shift), w_qkv, line(bias3), bounds, out_grad
    )
    second_all, activated, hidden_grad, middle, in_part = run_feed(
        plan, tokens, att, w_out, line(out_bias), line(norm2_gain), line(norm2_shift), w_in, line(in_bias),
        w_down, grad_all,
    )

    def over_batch(partial, dimension):
        return lax.psum_scatter(partial, "batch", scatter_dimension=dimension, tiled=True).astype(f32)

    def weight_part(left, right):
        return dot(left, right, 0, 0).astype(bf16)

    down_weight_grad = over_batch(weight_part(activated, grad_all), 1)
    middle_grad, branch_all, att_grad, sums2 = run_middle(
        plan, hidden_grad, w_in, middle, out_grad, line(norm2_gain), w_out
    )
    in_weight_grad = over_batch(weight_part(second_all, hidden_grad), 0)
    qkv_grad, block_out, qv_part = run_back(
        plan, block, bounds, qkv, att, att_grad, sums, activated, w_down, middle, line(down_bias)
    )
    out_weight_grad = over_batch(weight_part(att, branch_all), 1)
    qkv_part = jnp.stack(
        [weight_part(first_all, qkv_grad[:, part * width : (part + 1) * width]) for part in range(3)]
    )
    qkv_weight_grad = over_batch(qkv_part, 1)
    input_grad, sums1 = run_last(plan, qkv_grad, w_qkv, tokens, middle_grad, line(norm1_gain))

    local = jnp.concatenate([qv_part[0], qv_part[1], in_part[0]])
    spread = lax.dynamic_update_slice(
        jnp.zeros((devices, local.shape[0]), f32), local[None], (column, jnp.int32(0))
    )
    packed = jnp.concatenate([sums1[:2].reshape(-1), sums2[:4].reshape(-1), spread.reshape(-1)])
    packed = lax.psum(packed, ("batch", "mp"))
    vectors = packed[: 6 * depth].reshape(6, depth)
    spread = packed[6 * depth :].reshape(devices, -1)
    qv_bias_grad = jnp.stack([spread[:, :width].reshape(-1), spread[:, width : 2 * width].reshape(-1)])
    return (
        block_out,
        input_grad,
        vectors[0],
        vectors[1],
        qkv_weight_grad,
        qv_bias_grad,
        out_weight_grad,
        vectors[4],
        vectors[2],
        vectors[3],
        in_weight_grad,
        spread[:, 2 * width :].reshape(-1),
        down_weight_grad,
        vectors[5],
    )


def solution(mesh):
    return jax.shard_map(
        body,
        mesh=mesh,
        in_specs=(
            P(("batch", "mp"), None),
            P(("batch", "mp"), None),
            P(),
            P(),
            P(),
            P(),
            P(),
            P(None, None, "mp"),
            P(None, "mp"),
            P("mp", None),
            P(),
            P(),
            P(),
            P(None, "mp"),
            P("mp"),
            P("mp", None),
            P(),
        ),
        out_specs=(
            P(("batch", "mp"), None),
            P(("batch", "mp"), None),
            P(),
            P(),
            P(None, "batch", "mp"),
            P(),
            P("mp", "batch"),
            P(),
            P(),
            P(),
            P("batch", "mp"),
            P(),
            P("mp", "batch"),
            P(),
        ),
        check_vma=False,
    )
```

time: 1170 us -> 688 us (0.59)
  waiting for transfers between devices: 713 us -> 226 us
  Pallas kernels: 0 us -> 361 us
  matrix products: 242 us -> 50.2 us
  local copies, waits for them, and re-layouts: 90.1 us -> 8 us
  other arithmetic: 86.7 us -> 17.4 us
    reduce_scatter x8 -> x4, waiting for transfers between devices: 411 us -> 0.02 us  [over_batch(): lax.psum_scatter(partial, 'batch', scatter_dimension=dimension, tiled=True)]
    pallas_call x0 -> x5, Pallas kernels: none -> 361 us  [the longest x1 91.3 us: run_feed(): pl.pallas_call(functools.partial(feed_kernel, plan), out_shape=(jax.Shape...]
    dot_general x40 -> x6, matrix products: 242 us -> 50.2 us  [dot(): lax.dot_general(left, right, (((contract_left,), (contract_right,)), ((),...]
    all_gather x4 -> x0, waiting for transfers between devices: 174 us -> none  [the longest x1 55.1 us: body(): first_all = lax.all_gather(first_rows, 'mp', axis=0, tiled=True)]
    psum x1, waiting for transfers between devices: 127 us -> 226 us  [body(): packed = lax.psum(packed, ('batch', 'mp'))]
    reduce_sum x15 -> x1, other arithmetic: 30.5 us -> 0.91 us  [segment_bounds(): offsets = jnp.sum(jnp.where(same & before, seq_lengths[None, :], 0), axis=1)]
    convert_element_type x11 -> x4, other arithmetic: 36.5 us -> 10 us  [over_batch(): lax.psum_scatter(partial, 'batch', scatter_dimension=dimension, tiled=True)]
    transpose x3 -> x0, local copies, waits for them, and re-layouts: 22.5 us -> none  [join_heads(): return jnp.transpose(tensor, (1, 0, 2)).reshape(group_rows, local_width)]
  transfers between devices with their start and end apart: 13 -> 5, of which waited for: 10 -> 1; matrix products, arithmetic and copies ran while one was open for 22% -> 9% of each run, Pallas kernels for 0% -> 0%
where the time goes in v1:
time: 688 us; the launch traced here: 679 us
  Pallas kernels  361 us (52%)
  waiting for transfers between devices  226 us (33%)
  matrix products  50.2 us (7%)
  other arithmetic  17.4 us (3%)
  between operations  16.1 us (2%)
  local copies, waits for them, and re-layouts  8 us (1%)
    psum x1, waiting for transfers between devices, body(): packed = lax.psum(packed, ('batch', 'mp'))  226 us
    pallas_call x1, Pallas kernels, run_feed(): pl.pallas_call(functools.partial(feed_kernel, plan), out_shape=(jax.Shape...  91.3 us
    pallas_call x1, Pallas kernels, run_middle(): pl.pallas_call(functools.partial(middle_kernel, plan), out_shape=(jax.Sha...  89 us
    pallas_call x1, Pallas kernels, run_first(): pl.pallas_call(functools.partial(first_kernel, plan, block), out_shape=(j...  83.3 us
    dot_general x6, matrix products, dot(): lax.dot_general(left, right, (((contract_left,), (contract_right,)), ((),...  50.2 us
    pallas_call x1, Pallas kernels, run_last(): pl.pallas_call(functools.partial(last_kernel, plan), out_shape=(jax.Shape...  49.8 us
    pallas_call x1, Pallas kernels, run_back(): pl.pallas_call(functools.partial(back_kernel, plan, block), out_shape=(ja...  47.2 us
  transfers between devices with their start and end apart: 5, of which 1 were waited for; matrix products, arithmetic and copies ran while one was open for 9% of the time, Pallas kernels for 0%

profile of v1, /device:TPU:8, one launch (start us, length us, event | category | flops | bytes accessed | tf_op | source)
XLA Modules:
  0.0 678.9 jit_solution(10756821766396390287)
XLA Ops:
  8.0 0.0 all-reduce.2.cloned.1.call-start
  8.1 0.7 iota_add_fusion
  8.7 0.8 fusion.9
  9.5 0.6 reshape.95.qv_bias
  10.1 0.9 select_reduce_fusion
  11.0 1.3 compare_select_fusion.1
  12.3 1.2 pad_add_fusion.bounds
  13.5 83.3 %first.1 = (bf16[2048,2048]{1,0:T(8,128)(2,1)}, bf16[2048,768]{1,0:T(8,128)(2,1)}, bf16[2048,256]{1,0:T(8,128)(2,1)}, f32[8,2048]{1,0:T(8,128)}, bf16[2048,2048]{1,0:T(8,128)(2,1)}) custom-call(bf16[256,2048]{1,0:T(8,128)(2,1)} %tok.5, f32[1,2048]{1,0:T(1,128)} %bitcast.54, f32[1,2048]{1,0:T(1,128)} %bitcast.56, bf16[3,2048,256]{2,1,0:T(8,128)(2,1)} %w_qkv.3, ...), custom_call_target="tpu_custom_call" | custom-call | tf_op jit(solution)/shard_map/first/pallas_call | solution.py:454
  96.8 91.3 %feed.1 = (bf16[2048,2048]{1,0:T(8,128)(2,1)}, bf16[2048,1024]{1,0:T(8,128)(2,1)}, bf16[2048,1024]{1,0:T(8,128)(2,1)}, f32[256,2048]{1,0:T(8,128)}, f32[1,1024]{1,0:T(1,128)}) custom-call(bf16[256,2048]{1,0:T(8,128)(2,1)} %tok.5, bf16[2048,256]{1,0:T(8,128)(2,1)} %get-tuple-element.34.att, bf16[256,2048]{1,0:T(8,128)(2,1)} %w_out.3, f32[1,2048]{1,0:T(1,128)} %bitcast.57, ...), custom_call_target="tpu_custom_call" | custom-call | tf_op jit(solution)/shard_map/feed/pallas_call | solution.py:590
  188.1 89.0 %middle.1 = (f32[256,2048]{1,0:T(8,128)}, bf16[2048,2048]{1,0:T(8,128)(2,1)}, bf16[2048,256]{1,0:T(8,128)(2,1)}, f32[8,2048]{1,0:T(8,128)}) custom-call(bf16[2048,1024]{1,0:T(8,128)(2,1)} %get-tuple-element.36.hidden_grad, bf16[2048,1024]{1,0:T(8,128)(2,1)} %w_in.3, f32[256,2048]{1,0:T(8,128)} %get-tuple-element.37.middle, bf16[256,2048]{1,0:T(8,128)(2,1)} %out_grad.3, ...), custom_call_target="tpu_custom_call" | custom-call | tf_op jit(solution)/shard_map/middle/pallas_call | solution.py:695
  277.2 47.2 %back.1 = (bf16[2048,768]{1,0:T(8,128)(2,1)}, bf16[256,2048]{1,0:T(8,128)(2,1)}, f32[8,256]{1,0:T(8,128)}) custom-call(s32[9]{0:T(128)} %pad_add_fusion.bounds, bf16[2048,768]{1,0:T(8,128)(2,1)} %get-tuple-element.33.qkv, bf16[2048,256]{1,0:T(8,128)(2,1)} %get-tuple-element.34.att, bf16[2048,256]{1,0:T(8,128)(2,1)} %get-tuple-element.38.att_grad, ...), custom_call_target="tpu_custom_call" | custom-call | tf_op jit(solution)/shard_map/back/pallas_call | solution.py:833
  324.4 0.8 fusion.8
  325.2 0.2 dynamic_update_slice.3
  325.4 49.8 %last.1 = (bf16[256,2048]{1,0:T(8,128)(2,1)}, f32[8,2048]{1,0:T(8,128)}) custom-call(bf16[2048,768]{1,0:T(8,128)(2,1)} %get-tuple-element.42.qkv_grad, bf16[3,2048,256]{2,1,0:T(8,128)(2,1)} %w_qkv.3, bf16[256,2048]{1,0:T(8,128)(2,1)} %tok.5, f32[256,2048]{1,0:T(8,128)} %get-tuple-element.43.middle_grad, f32[1,2048]{1,0:T(1,128)} %bitcast.55), custom_call_target="tpu_custom_call" | custom-call | tf_op jit(solution)/shard_map/last/pallas_call | solution.py:907
  375.2 0.8 slice_bitcast_fusion.2
  376.0 0.0 copy-done.4
  376.1 0.6 pad_maximum_fusion.1
  376.7 0.0 all-reduce.2.cloned.1.call-update
  376.8 0.0 reduce-scatter.7.cloned.1.call-start
  376.8 6.7 convolution_convert_fusion.2
  383.5 0.0 reduce-scatter.7.cloned.1.call-update
  383.5 0.3 reduce-scatter.5.cloned.1.call-start
  383.9 0.0 slice-start
  383.9 6.3 fusion.2
  390.2 0.0 slice-start.1
  390.2 6.1 fusion.1
  396.3 2.5 fusion
  398.8 2.0 pad_maximum_fusion
  400.8 0.0 reduce-scatter.5.cloned.1.call-update
  400.9 0.5 reduce-scatter.11.cloned.1.call-start
  401.4 14.1 %convolution_convert_fusion = bf16[1024,2048]{1,0:T(8,128)(2,1)} fusion(bf16[2048,1024]{1,0:T(8,128)(2,1)} %get-tuple-element.40.activated, bf16[2048,2048]{1,0:T(8,128)(2,1)} %get-tuple-element.35.grad_all), kind=kOutput, calls=%fused_computation | convolution fusion | flops 8592031744 | bytes 16777216 | tf_op jit(solution)/shard_map/dot_general | solution.py:23
  415.4 0.0 reduce-scatter.11.cloned.1.call-update
  415.5 0.0 reduce-scatter.9.cloned.1.call-start
  415.5 14.5 %convolution_convert_fusion.1 = bf16[2048,1024]{1,0:T(8,128)(2,1)} fusion(bf16[2048,2048]{1,0:T(8,128)(2,1)} %get-tuple-element.51, bf16[2048,1024]{1,0:T(8,128)(2,1)} %get-tuple-element.36.hidden_grad), kind=kOutput, calls=%fused_computation.1 | convolution fusion | flops 8592031744 | bytes 16777216 | tf_op jit(solution)/shard_map/dot_general | solution.py:23
  430.0 0.0 reduce-scatter.9.cloned.1.call-update
  430.1 225.6 %all-reduce.2.cloned.1.call-done = f32[24576]{0:T(1024)} async-done(((f32[24576]{0:T(1024)}), f32[24576]{0:T(1024)}) %all-reduce.2.cloned.1.call-update) | async-done | bytes 98320 | tf_op jit(solution)/shard_map/psum | solution.py:1007
  655.6 0.8 slice.102
  656.5 0.6 copy.37
  657.1 0.6 pad_maximum_fusion.2
  657.7 1.4 fusion.7
  659.1 0.0 reduce-scatter.7.cloned.1.call-done
  659.2 1.8 convert_element_type.35
  661.0 2.5 convert_element_type.33
  663.5 2.9 convert_element_type.39
  666.4 2.8 convert_element_type.37
  669.2 0.0 copy-done.2
  669.2 1.0 copy.42
  670.2 1.0 copy.43
  (30 shorter events, 0.1 us)
Async XLA Ops:
  8.0 647.6 %all-reduce.2.cloned.1.call-start = ((), (), s32[]{:S(2)}) async-start(), calls=%async_computation.4 | async-start | bytes 196608 | tf_op jit(solution)/shard_map/psum | solution.py:1007
  277.1 48.0 %copy-start.5 = (f32[1,1024]{1,0:T(1,128)S(1)}, f32[1,1024]{1,0:T(1,128)}, u32[]{:S(2)}) copy-start(f32[1,1024]{1,0:T(1,128)} %get-tuple-element.48) | copy-start | bytes 12292
  325.4 50.7 %copy-start.4 = (f32[8,2048]{1,0:T(8,128)S(1)}, f32[8,2048]{1,0:T(8,128)}, u32[]{:S(2)}) copy-start(f32[8,2048]{1,0:T(8,128)} %get-tuple-element.46) | copy-start | bytes 196612
  325.4 51.4 %copy-start = (bf16[2048,256]{1,0:T(8,128)(2,1)S(1)}, bf16[2048,256]{1,0:T(8,128)(2,1)}, u32[]{:S(2)}) copy-start(bf16[2048,256]{1,0:T(8,128)(2,1)} %get-tuple-element.34.att) | copy-start | bytes 3145732
  376.8 282.4 %reduce-scatter.7.cloned.1.call-start = ((), (), s32[]{:S(2)}) async-start(), calls=%async_computation.6 | async-start | bytes 1310720 | tf_op jit(solution)/shard_map/reduce_scatter | solution.py:982
  383.5 277.4 %reduce-scatter.5.cloned.1.call-start = ((), (), s32[]{:S(2)}) async-start(), calls=%async_computation.5 | async-start | bytes 3932160 | tf_op jit(solution)/shard_map/reduce_scatter | solution.py:982
  383.8 6.3 copy-start.1
  383.9 12.4 %slice-start = ((s8[8388608]{0:T(1024)(128)(4,1)}), s8[4194304]{0:T(1024)(128)(4,1)S(1)}, s32[]{:S(2)}) async-start(s8[8388608]{0:T(1024)(128)(4,1)} %bitcast.66), calls=%async_computation.9 | async-start | bytes 8388608
  390.2 6.1 slice-start.1
  400.9 262.6 %reduce-scatter.11.cloned.1.call-start = ((), (), s32[]{:S(2)}) async-start(), calls=%async_computation.8 | async-start | bytes 5242880 | tf_op jit(solution)/shard_map/reduce_scatter | solution.py:982
  415.5 250.9 %reduce-scatter.9.cloned.1.call-start = ((), (), s32[]{:S(2)}) async-start(), calls=%async_computation.7 | async-start | bytes 5242880 | tf_op jit(solution)/shard_map/reduce_scatter | solution.py:982
  661.0 8.2 %copy-start.2 = (bf16[256,2048]{1,0:T(8,128)(2,1)S(1)}, bf16[256,2048]{1,0:T(8,128)(2,1)}, u32[]{:S(2)}) copy-start(bf16[256,2048]{1,0:T(8,128)(2,1)} %get-tuple-element.80) | copy-start | bytes 3145732
  663.5 6.7 copy-start.3
Sparse Core Ops, SparseCore 0:
  376.9 278.7 all-reduce.1
Sparse Core Ops, SparseCore 1:
  383.6 25.3 reduce-scatter.6
  411.3 60.7 reduce-scatter.4
  474.3 77.4 reduce-scatter.10
  554.1 77.5 reduce-scatter.8

commit v2 on v1

--- a/solution.py
+++ b/solution.py
@@ -77,17 +77,45 @@
     def __init__(self, plan):
         self.plan = plan
         self.batch = lax.axis_index("batch")
+        self.groups = lax.axis_size("batch")
         self.me = lax.axis_index("mp")
 
     def at(self, mask):
         return (self.batch, flip(self.me, mask))
 
-    def barrier(self):
+    def beside(self, step):
+        return (self.batch + step, self.me)
+
+    def barrier(self, line=False, halves=False):
         semaphore = pltpu.get_barrier_semaphore()
         masks = [1] + self.plan.bits
         for mask in masks:
             pl.semaphore_signal(semaphore, inc=1, device_id=self.at(mask), device_id_type=MESH)
-        pl.semaphore_wait(semaphore, len(masks))
+        count = len(masks)
+        if line:
+            for step, there in ((-1, self.batch > 0), (1, self.batch < self.groups - 1)):
+
+                @pl.when(there)
+                def greet():
+                    pl.semaphore_signal(semaphore, inc=1, device_id=self.beside(step), device_id_type=MESH)
+
+                count = count + there.astype(jnp.int32)
+        if halves:
+            for bit in self.group_bits():
+                pl.semaphore_signal(semaphore, inc=1, device_id=self.across(bit), device_id_type=MESH)
+                count = count + 1
+        pl.semaphore_wait(semaphore, count)
+
+    def group_bits(self):
+        bits = []
+        bit = 1
+        while bit < self.groups:
+            bits.append(bit)
+            bit *= 2
+        return bits
+
+    def across(self, bit):
+        return (flip(self.batch, bit), self.me)
 
 
 class Gather:
@@ -234,8 +262,8 @@
         loop(self.part_rows, self.step, add)
         self.link((part, offset)).start()
 
-    def begin(self, partial):
-        for offset in self.order:
+    def begin(self, partial, between=None):
+        for number, offset in enumerate(self.order):
             index = offset // 2
             partial(flip(self.place.me, offset | 1), self.core_out.at[index])
             self.core(offset).start()
@@ -244,6 +272,8 @@
             for part in range(self.plan.parts):
                 if offset and not self.plan.later(part, offset):
                     self.pass_on(part, offset)
+            if between is not None:
+                between(number)
 
     def middle(self):
         for offset in self.order:
@@ -283,6 +313,141 @@
             pltpu.SemaphoreType.DMA((chips,)),
             pltpu.SemaphoreType.DMA((chips,)),
         ]
+
+
+class Line:
+    def __init__(self, place, own, up, down, pieces, sems):
+        self.place, self.own, self.up, self.down, self.pieces = place, own, up, down, pieces
+        self.groups, self.batch = place.groups, place.batch
+        self.rows = own.shape[1] // pieces
+        self.step = min(32, self.rows)
+        self.sems = sems
+
+    def span(self, piece):
+        start = piece * self.rows
+        return pl.ds(start if isinstance(start, int) else pl.multiple_of(start, self.rows), self.rows)
+
+    def slot(self, upward, target):
+        return self.up.at[target - 1] if upward else self.down.at[target]
+
+    def copy(self, upward, target, piece, source):
+        send, recv = self.sems[:2] if upward else self.sems[2:]
+        index = target * self.pieces + piece
+        return pltpu.make_async_remote_copy(
+            src_ref=source.at[self.span(piece), :],
+            dst_ref=self.slot(upward, target).at[self.span(piece), :],
+            send_sem=send.at[index],
+            recv_sem=recv.at[index],
+            device_id=self.place.beside(1 if upward else -1),
+            device_id_type=MESH,
+        )
+
+    def start(self, target):
+        if target > 0:
+
+            @pl.when(self.batch == 0)
+            def first():
+                for piece in range(self.pieces):
+                    self.copy(True, target, piece, self.own.at[target]).start()
+
+        if target < self.groups - 1:
+
+            @pl.when(self.batch == self.groups - 1)
+            def last():
+                for piece in range(self.pieces):
+                    self.copy(False, target, piece, self.own.at[target]).start()
+
+    def order(self):
+        count = self.groups
+        result = []
+        for index in range((count + 1) // 2):
+            for target in (count - 1 - index, index):
+                if target not in result:
+                    result.append(target)
+        return result
+
+    def ticks(self):
+        return range(1, (self.groups - 1) * self.pieces + self.groups)
+
+    def tick(self, number):
+        for upward in (True, False):
+            place = self.batch if upward else self.groups - 1 - self.batch
+            for distance in range(2, self.groups):
+                target = distance if upward else self.groups - 1 - distance
+                piece = number - (self.groups - 1 - distance) * self.pieces - place
+                due = (place > 0) & (place < distance) & (piece >= 0) & (piece < self.pieces)
+
+                @pl.when(due)
+                def forward():
+                    slot = self.slot(upward, target)
+                    copy = self.copy(upward, target, piece, slot)
+                    copy.wait_recv()
+
+                    def add(start):
+                        rows = pl.ds(pl.multiple_of(piece * self.rows + start, self.step), self.step)
+                        total = slot[rows, :].astype(f32) + self.own[target, rows, :].astype(f32)
+                        slot[rows, :] = total.astype(bf16)
+
+                    loop(self.rows, self.step, add)
+                    copy.start()
+
+    def end(self, target_ref):
+        below, above = self.batch > 0, self.batch < self.groups - 1
+        total = self.own.shape[1]
+
+        @pl.when(below)
+        def up():
+            slot = self.slot(True, self.batch)
+            for piece in range(self.pieces):
+                self.copy(True, self.batch, piece, slot).wait_recv()
+
+        @pl.when(above)
+        def down():
+            slot = self.slot(False, self.batch)
+            for piece in range(self.pieces):
+                self.copy(False, self.batch, piece, slot).wait_recv()
+
+        def add(sides):
+            def rows_of(start):
+                rows = pl.ds(start, self.step)
+                value = self.own[self.batch, rows, :].astype(f32)
+                for upward in sides:
+                    value += self.slot(upward, self.batch)[rows, :].astype(f32)
+                target_ref[rows, :] = value
+
+            loop(total, self.step, rows_of)
+
+        @pl.when(jnp.logical_not(above))
+        def at_top():
+            add([True])
+
+        @pl.when(jnp.logical_not(below))
+        def at_bottom():
+            add([False])
+
+        @pl.when(below & above)
+        def between():
+            add([True, False])
+
+    def finish(self):
+        for target in range(self.groups):
+            for upward in (True, False):
+                if target == (0 if upward else self.groups - 1):
+                    continue
+
+                @pl.when(self.batch < target if upward else self.batch > target)
+                def sent():
+                    slot = self.slot(upward, target)
+                    for piece in range(self.pieces):
+                        self.copy(upward, target, piece, slot).wait_send()
+
+    @staticmethod
+    def scratch(groups, rows, columns, pieces):
+        return [
+            pltpu.VMEM((groups, rows, columns), bf16),
+            pltpu.VMEM((groups - 1, rows, columns), bf16),
+            pltpu.VMEM((groups - 1, rows, columns), bf16),
+        ] + [pltpu.SemaphoreType.DMA((groups * pieces,))] * 4
 
 
 class Moves:
@@ -444,6 +609,10 @@
     return pltpu.CompilerParams(
         collective_id=number, has_side_effects=True, vmem_limit_bytes=62 * 2**20
     )
+
+
+def cost(micros):
+    return pl.CostEstimate(flops=micros * 10**9, bytes_accessed=10**7, transcendentals=0)
 
 
 def run_first(plan, block, tok, gain, shift, w_qkv, qv_bias, bounds, out_grad):
@@ -474,6 +643,7 @@
         + Gather.semaphores(plan) * 2,
         compiler_params=params(0),
         name="first",
+        cost_estimate=cost(80),
     )(tok, gain, shift, w_qkv, qv_bias, bounds, out_grad)
 
 
@@ -614,23 +784,34 @@
         + Gather.semaphores(plan),
         compiler_params=params(1),
         name="feed",
+        cost_estimate=cost(90),
     )(tok, att, w_out, out_bias, gain, shift, w_in, in_bias, w_down, grad_all)
 
 
+PIECES = 2
+
+
 def middle_kernel(
-    plan, hidden_grad, w_in, middle, out_grad, gain, w_out,
-    middle_grad_out, branch_out, att_grad_out, sums_out,
-    h_in, w_i, w_o, buf, middle_grad, att_grad, local, *rest,
+    plan, hidden_grad, w_in, middle, out_grad, gain, w_out, activated, grad_all, second_all,
+    middle_grad_out, branch_out, att_grad_out, sums_out, down_out, in_part_out,
+    h_in, w_i, w_o, buf, middle_grad, att_grad, act, staged, total, local, *rest,
 ):
-    scatter_refs, gather_sems = rest[:9], rest[9:]
+    scatter_refs, gather_sems, line_refs = rest[:9], rest[9:13], rest[13:]
     place = Place(plan)
     own, depth = middle.shape
+    rows = buf.shape[0]
     chip_rows = 2 * own
+    hidden = w_in.shape[1]
+    groups = place.groups
+    cut = depth // groups
     moves = Moves(local)
     loads = [moves.start(hidden_grad, h_in), moves.start(w_in, w_i)]
+    load_act = moves.start(activated, act)
+    load_grad = moves.start(grad_all, buf)
     load_out = moves.start(w_out, w_o)
-    place.barrier()
+    place.barrier(line=True)
     scatter = Scatter(place, own, depth, *scatter_refs[:5], scatter_refs[5:])
+    line = Line(place, *line_refs[:3], PIECES, line_refs[3:])
     for copy in loads:
         copy.wait()
     tile = min(1024, depth)
@@ -643,20 +824,75 @@
 
         loop(depth, tile, columns)
 
-    scatter.begin(partial)
+    order = line.order()
+    part = min(512, hidden)
+
+    def down_slice(target):
+        def piece(start):
+            line.own[target, pl.ds(start, part), :] = dot(
+                act[:, pl.ds(start, part)], buf[:, pl.ds(target * cut, cut)], 0, 0
+            ).astype(bf16)
+
+        loop(hidden, part, piece)
+        line.start(target)
+
+    def between(number):
+        if number == 0:
+            load_act.wait()
+            load_grad.wait()
+            for target in order[:2]:
+                down_slice(target)
+        if number == 1:
+            for target in order[2:]:
+                down_slice(target)
+
+    scatter.begin(partial, between)
+
+    in_stores = []
+    in_loads = {}
+
+    def load_slice(number):
+        columns = pl.ds(number * cut, cut)
+        in_loads[number] = moves.start(second_all.at[:, columns], act.at[:, pl.ds((number % 2) * cut, cut)])
+
+    def in_slice(number):
+        in_loads[number].wait()
+        if number >= 2:
+            in_stores[number - 2].wait()
+        slot = number % 2
+
+        def piece(start):
+            columns = pl.ds(start, part)
+            staged[slot, :, columns] = dot(
+                act[:, pl.ds(slot * cut, cut)], h_in[:, columns], 0, 0
+            ).astype(bf16)
+
+        loop(hidden, part, piece)
+        in_stores.append(moves.start(staged.at[slot], in_part_out.at[number]))
+        if number + 2 < groups:
+            load_slice(number + 2)
+
+    ticks = list(line.ticks())
+    for number in range(min(2, groups)):
+        load_slice(number)
+    line.tick(ticks.pop(0))
     scatter.middle()
+    half = groups // 2
+    for number in range(half):
+        in_slice(number)
+    line.tick(ticks.pop(0))
     mine = pl.multiple_of(place.me * own, own)
     sums_out[...] = jnp.zeros_like(sums_out)
 
     def close(start, count, value):
         span = pl.ds(start, count)
         unit, inverse = norm_rows(middle[span, :])
-        total = out_grad[span, :].astype(f32) + norm_back(value, unit, inverse, gain[...])
-        middle_grad[span, :] = total
-        buf[pl.ds(pl.multiple_of(mine + start, count), count), :] = total.astype(bf16)
+        sum_rows = out_grad[span, :].astype(f32) + norm_back(value, unit, inverse, gain[...])
+        middle_grad[span, :] = sum_rows
+        buf[pl.ds(pl.multiple_of(mine + start, count), count), :] = sum_rows.astype(bf16)
         sums_out[0:1, :] += jnp.sum(value * unit, axis=0, keepdims=True)
         sums_out[1:2, :] += jnp.sum(value, axis=0, keepdims=True)
-        sums_out[2:3, :] += jnp.sum(total, axis=0, keepdims=True)
+        sums_out[2:3, :] += jnp.sum(sum_rows, axis=0, keepdims=True)
         sums_out[3:4, :] += jnp.sum(out_grad[span, :].astype(f32), axis=0, keepdims=True)
 
     scatter.end(close)
@@ -674,6 +910,9 @@
 
     gather.share(0)
     project(0)
+    for number in range(half, groups):
+        in_slice(number)
+    line.tick(ticks.pop(0))
     arrivals, chips = gather.steps()
     for keys, offsets in zip(arrivals, chips):
         for key in keys:
@@ -681,17 +920,24 @@
         for offset in offsets:
             gather.share(offset)
             project(offset)
+        line.tick(ticks.pop(0))
     stores.append(moves.start(att_grad, att_grad_out))
+    for number in ticks:
+        line.tick(number)
+    line.end(total)
+    stores.append(moves.start(total, down_out))
     gather.finish()
-    for copy in stores:
+    line.finish()
+    for copy in stores + in_stores[-2:]:
         copy.wait()
 
 
-def run_middle(plan, hidden_grad, w_in, middle, out_grad, gain, w_out):
+def run_middle(plan, groups, hidden_grad, w_in, middle, out_grad, gain, w_out, activated, grad_all, second_all):
     own, depth = middle.shape
     rows = own * plan.devices
     width = w_out.shape[0]
     hidden = w_in.shape[1]
+    cut = depth // groups
     return pl.pallas_call(
         functools.partial(middle_kernel, plan),
         out_shape=(
@@ -699,9 +945,11 @@
             jax.ShapeDtypeStruct((rows, depth), bf16),
             jax.ShapeDtypeStruct((rows, width), bf16),
             jax.ShapeDtypeStruct((8, depth), f32),
+            jax.ShapeDtypeStruct((hidden, cut), f32),
+            jax.ShapeDtypeStruct((groups, cut, hidden), bf16),
         ),
-        in_specs=[ANY, ANY, VMEM, VMEM, VMEM, ANY],
-        out_specs=(ANY, ANY, ANY, VMEM),
+        in_specs=[ANY, ANY, VMEM, VMEM, VMEM, ANY, ANY, ANY, ANY],
+        out_specs=(ANY, ANY, ANY, VMEM, ANY, ANY),
         scratch_shapes=[
             pltpu.VMEM((rows, hidden), bf16),
             pltpu.VMEM((depth, hidden), bf16),
@@ -709,30 +957,52 @@
             pltpu.VMEM((rows, depth), bf16),
             pltpu.VMEM((own, depth), f32),
             pltpu.VMEM((rows, width), bf16),
-            pltpu.SemaphoreType.DMA((16,)),
+            pltpu.VMEM((rows, max(hidden, 2 * cut)), bf16),
+            pltpu.VMEM((2, cut, hidden), bf16),
+            pltpu.VMEM((hidden, cut), f32),
+            pltpu.SemaphoreType.DMA((40,)),
         ]
-        + Scatter.scratch(plan, own, depth, f32)
-        + Gather.semaphores(plan),
+        + Scatter.scratch(plan, own, depth, bf16)
+        + Gather.semaphores(plan)
+        + Line.scratch(groups, hidden, cut, PIECES),
         compiler_params=params(2),
         name="middle",
-    )(hidden_grad, w_in, middle, out_grad, gain, w_out)
+        cost_estimate=cost(80),
+    )(hidden_grad, w_in, middle, out_grad, gain, w_out, activated, grad_all, second_all)
 
 
 def back_kernel(
-    plan, block, bounds, qkv, att, att_grad, sums, activated, w_down, middle, down_bias,
-    qkv_grad_out, block_out, bias_out,
-    qkv_in, att_in, grad_in, act_in, w_d, starts, key_grad, value_grad, result, local, *rest,
+    plan, block, bounds, qkv, att, att_grad, sums, activated, w_down, middle, down_bias, in_part, branch_all,
+    qkv_grad_out, block_out, bias_out, in_out, out_part_out,
+    qkv_in, att_in, grad_in, act_in, w_d, starts, key_grad, value_grad, result, branch, staged, total, local,
+    *rest,
 ):
+    scatter_refs, line_refs = rest[:9], rest[9:]
     place = Place(plan)
     own, depth = middle.shape
     rows = qkv_in.shape[0]
     width = att_in.shape[1]
     heads = width // HEAD_DIM
+    groups = place.groups
+    cut = depth // groups
     moves = Moves(local)
+    line = Line(place, *line_refs[:3], PIECES, line_refs[3:])
+    order = line.order()
+    parts = [moves.start(in_part.at[target], line.own.at[target]) for target in order]
     feeds = [moves.start(activated, act_in), moves.start(w_down, w_d)]
     loads = [moves.start(qkv, qkv_in), moves.start(att, att_in), moves.start(att_grad, grad_in)]
-    place.barrier()
-    scatter = Scatter(place, own, depth, *rest[:5], rest[5:])
+    branch_loads = {}
+
+    def load_slice(number):
+        branch_loads[number] = moves.start(branch_all.at[:, pl.ds(number * cut, cut)], branch.at[number % 2])
+
+    for number in range(min(2, groups)):
+        load_slice(number)
+    place.barrier(line=True)
+    scatter = Scatter(place, own, depth, *scatter_refs[:5], scatter_refs[5:])
+    for target, copy in zip(order, parts):
+        copy.wait()
+        line.start(target)
     for copy in feeds:
         copy.wait()
     tile = min(1024, depth)
@@ -746,12 +1016,20 @@
         loop(depth, tile, columns)
 
     scatter.begin(partial)
+    ticks = list(line.ticks())
+    line.tick(ticks.pop(0))
     starts[...] = segment_starts(bounds, rows)
     bias_out[...] = jnp.zeros_like(bias_out)
     key_grad[...] = jnp.zeros_like(key_grad)
     value_grad[...] = jnp.zeros_like(value_grad)
     for copy in loads:
         copy.wait()
+    for number in range(groups):
+        branch_loads[number].wait()
+        staged[number, :, :] = dot(att_in[...], branch[number % 2], 0, 0).astype(bf16)
+        if number + 2 < groups:
+            load_slice(number + 2)
+    stores = [moves.start(staged, out_part_out)]
     scale = HEAD_DIM ** (-0.5)
     row_in = lax.broadcasted_iota(jnp.int32, (block, block), 0)
     col_in = lax.broadcasted_iota(jnp.int32, (block, block), 1)
@@ -774,7 +1052,7 @@
             allowed = key_in + key_block * block >= first
             if diagonal:
                 allowed = allowed & (row_in <= col_in)
-            result = []
+            out = []
             for head in range(heads):
                 columns = pl.ds(head * HEAD_DIM, HEAD_DIM)
                 keys = qkv_in[key_span, head_columns(1, head, width)]
@@ -785,8 +1063,8 @@
                 prob_grad = dot(values, outer[head], 1, 1)
                 score_grad = (probs * (prob_grad - inner[head])).astype(bf16)
                 key_grad[key_span, columns] += dot(score_grad, queries[head], 1, 0)
-                result.append(carry[head] + dot(score_grad, keys, 0, 0))
-            return tuple(result)
+                out.append(carry[head] + dot(score_grad, keys, 0, 0))
+            return tuple(out)
 
         carry = tuple(jnp.zeros((block, HEAD_DIM), f32) for head in range(heads))
         if index:
@@ -803,6 +1081,8 @@
         attend(index)
         if index == blocks // 2:
             scatter.middle()
+        if index:
+            line.tick(ticks.pop(0))
     kept = min(256, rows)
 
     def write(start):
@@ -813,7 +1093,7 @@
         bias_out[1:2, :] += jnp.sum(rounded.astype(f32), axis=0, keepdims=True)
 
     loop(rows, kept, write)
-    stores = [moves.start(qkv_in, qkv_grad_out)]
+    stores.append(moves.start(qkv_in, qkv_grad_out))
 
     def close(start, count, value):
         span = pl.ds(start, count)
@@ -821,24 +1101,34 @@
 
     scatter.end(close)
     stores.append(moves.start(result, block_out))
+    for number in ticks:
+        line.tick(number)
+    line.end(total)
+    stores.append(moves.start(total, in_out))
     scatter.finish()
+    line.finish()
     for copy in stores:
         copy.wait()
 
 
-def run_back(plan, block, bounds, qkv, att, att_grad, sums, activated, w_down, middle, down_bias):
+def run_back(
+    plan, groups, block, bounds, qkv, att, att_grad, sums, activated, w_down, middle, down_bias, in_part, branch_all
+):
     own, depth = middle.shape
     rows, width = att.shape
     hidden = w_down.shape[0]
+    cut = depth // groups
     return pl.pallas_call(
         functools.partial(back_kernel, plan, block),
         out_shape=(
             jax.ShapeDtypeStruct((rows, 3 * width), bf16),
             jax.ShapeDtypeStruct((own, depth), bf16),
             jax.ShapeDtypeStruct((8, width), f32),
+            jax.ShapeDtypeStruct((cut, hidden), f32),
+            jax.ShapeDtypeStruct((groups, width, cut), bf16),
         ),
-        in_specs=[SMEM, ANY, ANY, ANY, VMEM, ANY, ANY, VMEM, VMEM],
-        out_specs=(ANY, ANY, VMEM),
+        in_specs=[SMEM, ANY, ANY, ANY, VMEM, ANY, ANY, VMEM, VMEM, ANY, ANY],
+        out_specs=(ANY, ANY, VMEM, ANY, ANY),
         scratch_shapes=[
             pltpu.VMEM((rows, 3 * width), bf16),
             pltpu.VMEM((rows, width), bf16),
@@ -849,27 +1139,54 @@
             pltpu.VMEM((rows, width), f32),
             pltpu.VMEM((rows, width), f32),
             pltpu.VMEM((own, depth), bf16),
-            pltpu.SemaphoreType.DMA((16,)),
+            pltpu.VMEM((2, rows, cut), bf16),
+            pltpu.VMEM((groups, width, cut), bf16),
+            pltpu.VMEM((cut, hidden), f32),
+            pltpu.SemaphoreType.DMA((40,)),
         ]
-        + Scatter.scratch(plan, own, depth, f32),
+        + Scatter.scratch(plan, own, depth, bf16)
+        + Line.scratch(groups, cut, hidden, PIECES),
         compiler_params=params(3),
         name="back",
-    )(bounds, qkv, att, att_grad, sums, activated, w_down, middle, down_bias)
+        cost_estimate=cost(75),
+    )(bounds, qkv, att, att_grad, sums, activated, w_down, middle, down_bias, in_part, branch_all)
 
 
 def last_kernel(
-    plan, qkv_grad, w_qkv, tok, middle_grad, gain, input_out, sums_out, g_in, weights, result, local, *rest
+    plan, qkv_grad, w_qkv, tok, middle_grad, gain, out_part, first_all, sums2, in_sums, qv_sums,
+    input_out, out_out, qkv_out, vectors_out, spread_out,
+    g_in, weights, result, first, out_total, qkv_total, wide, many, wide_in, many_in, local, *rest,
 ):
+    scatter_refs, rest = rest[:9], rest[9:]
+    out_refs, rest = rest[:7], rest[7:]
+    qkv_refs, (wide_send, wide_recv, many_send, many_recv) = rest[:7], rest[7:]
     place = Place(plan)
     own, depth = tok.shape
     width = w_qkv.shape[2]
+    groups = place.groups
+    cut = depth // groups
     moves = Moves(local)
+    out_line = Line(place, *out_refs[:3], 1, out_refs[3:])
+    qkv_line = Line(place, *qkv_refs[:3], PIECES, qkv_refs[3:])
+    order = qkv_line.order()
+    parts = [moves.start(out_part.at[target], out_line.own.at[target]) for target in order]
     loads = [
         moves.start(w_qkv.at[part], weights.at[:, pl.ds(part * width, width)]) for part in range(3)
     ]
     loads.append(moves.start(qkv_grad, g_in))
-    place.barrier()
-    scatter = Scatter(place, own, depth, *rest[:5], rest[5:])
+    first_loads = {}
+
+    def load_slice(number):
+        columns = pl.ds(order[number] * cut, cut)
+        first_loads[number] = moves.start(first_all.at[:, columns], first.at[number % 2])
+
+    for number in range(min(2, groups)):
+        load_slice(number)
+    place.barrier(line=True, halves=True)
+    scatter = Scatter(place, own, depth, *scatter_refs[:5], scatter_refs[5:])
+    for target, copy in zip(order, parts):
+        copy.wait()
+        out_line.start(target)
     for copy in loads:
         copy.wait()
     tile = min(1024, depth)
@@ -882,46 +1199,135 @@
 
         loop(depth, tile, columns)
 
-    scatter.begin(partial)
+    def qkv_slice(number):
+        first_loads[number].wait()
+        qkv_line.own[order[number]] = dot(first[number % 2], g_in[...], 0, 0).astype(bf16)
+        qkv_line.start(order[number])
+        if number + 2 < groups:
+            load_slice(number + 2)
+
+    def between(number):
+        if number == 0:
+            for index in range(groups // 2):
+                qkv_slice(index)
+        if number == 1:
+            for index in range(groups // 2, groups):
+                qkv_slice(index)
+
+    scatter.begin(partial, between)
+    for number in out_line.ticks():
+        out_line.tick(number)
+    ticks = list(qkv_line.ticks())
     scatter.middle()
-    sums_out[...] = jnp.zeros_like(sums_out)
+    qkv_line.tick(ticks.pop(0))
+    out_line.end(out_total)
+    stores = [moves.start(out_total, out_out)]
+    wide[...] = jnp.zeros_like(wide)
+    wide[2:6, :] = sums2[0:4, :]
+    mine = lax.broadcasted_iota(jnp.int32, (many.shape[0], 1), 0) == place.me
+    many[:, pl.ds(0, width)] = jnp.where(mine, qv_sums[0:1, :], 0.0)
+    many[:, pl.ds(width, width)] = jnp.where(mine, qv_sums[1:2, :], 0.0)
+    many[:, pl.ds(2 * width, in_sums.shape[1])] = jnp.where(mine, in_sums[...], 0.0)
+    qkv_line.tick(ticks.pop(0))
 
     def close(start, count, value):
         span = pl.ds(start, count)
         unit, inverse = norm_rows(tok[span, :].astype(f32))
-        total = middle_grad[span, :] + norm_back(value, unit, inverse, gain[...])
-        result[span, :] = total.astype(bf16)
-        sums_out[0:1, :] += jnp.sum(value * unit, axis=0, keepdims=True)
-        sums_out[1:2, :] += jnp.sum(value, axis=0, keepdims=True)
+        sum_rows = middle_grad[span, :] + norm_back(value, unit, inverse, gain[...])
+        result[span, :] = sum_rows.astype(bf16)
+        wide[0:1, :] += jnp.sum(value * unit, axis=0, keepdims=True)
+        wide[1:2, :] += jnp.sum(value, axis=0, keepdims=True)
 
     scatter.end(close)
-    store = moves.start(result, input_out)
+    stores.append(moves.start(result, input_out))
+    qkv_line.tick(ticks.pop(0))
+    partners = [place.at(mask) for mask in [1] + plan.bits]
+    partners += [place.across(bit) for bit in place.group_bits()]
+    for index, partner in enumerate(partners):
+        copies = [
+            pltpu.make_async_remote_copy(
+                src_ref=source.at[index],
+                dst_ref=target.at[index],
+                send_sem=send.at[index],
+                recv_sem=recv.at[index],
+                device_id=partner,
+                device_id_type=MESH,
+            )
+            for source, target, send, recv in (
+                (wide_in[0], wide_in[1], wide_send, wide_recv),
+                (many_in[0], many_in[1], many_send, many_recv),
+            )
+        ]
+        wide_in[0][index] = wide[...]
+        many_in[0][index] = many[...]
+        for copy in copies:
+            copy.start()
+        for copy in copies:
+            copy.wait_recv()
+        wide[...] = wide_in[0][index] + wide_in[1][index]
+        many[...] = many_in[0][index] + many_in[1][index]
+        for copy in copies:
+            copy.wait_send()
+    vectors_out[...] = wide[...]
+    spread_out[...] = many[...]
+    for number in ticks:
+        qkv_line.tick(number)
+    qkv_line.end(qkv_total)
+    for part in range(3):
+        stores.append(moves.start(qkv_total.at[:, pl.ds(part * width, width)], qkv_out.at[part]))
     scatter.finish()
-    store.wait()
-
-
-def run_last(plan, qkv_grad, w_qkv, tok, middle_grad, gain):
+    out_line.finish()
+    qkv_line.finish()
+    for copy in stores:
+        copy.wait()
+
+
+def run_last(plan, groups, qkv_grad, w_qkv, tok, middle_grad, gain, out_part, first_all, sums2, in_sums, qv_sums):
     own, depth = tok.shape
     rows = qkv_grad.shape[0]
     width = w_qkv.shape[2]
+    cut = depth // groups
+    many = (plan.devices, 2 * width + in_sums.shape[1])
+    rounds = (plan.devices.bit_length() - 1) + (groups.bit_length() - 1)
+
+    def kernel(*refs):
+        head, tail = refs[: 10 + 5 + 8], refs[10 + 5 + 8 :]
+        last_kernel(plan, *head, (tail[0], tail[1]), (tail[2], tail[3]), *tail[4:])
+
     return pl.pallas_call(
-        functools.partial(last_kernel, plan),
+        kernel,
         out_shape=(
             jax.ShapeDtypeStruct((own, depth), bf16),
+            jax.ShapeDtypeStruct((width, cut), f32),
+            jax.ShapeDtypeStruct((3, cut, width), f32),
             jax.ShapeDtypeStruct((8, depth), f32),
+            jax.ShapeDtypeStruct(many, f32),
         ),
-        in_specs=[ANY, ANY, VMEM, VMEM, VMEM],
-        out_specs=(ANY, VMEM),
+        in_specs=[ANY, ANY, VMEM, VMEM, VMEM, ANY, ANY, VMEM, VMEM, VMEM],
+        out_specs=(ANY, ANY, ANY, VMEM, VMEM),
         scratch_shapes=[
             pltpu.VMEM((rows, 3 * width), bf16),
             pltpu.VMEM((depth, 3 * width), bf16),
             pltpu.VMEM((own, depth), bf16),
-            pltpu.SemaphoreType.DMA((8,)),
+            pltpu.VMEM((2, rows, cut), bf16),
+            pltpu.VMEM((width, cut), f32),
+            pltpu.VMEM((cut, 3 * width), f32),
+            pltpu.VMEM((8, depth), f32),
+            pltpu.VMEM(many, f32),
+            pltpu.VMEM((rounds, 8, depth), f32),
+            pltpu.VMEM((rounds, 8, depth), f32),
+            pltpu.VMEM((rounds,) + many, f32),
+            pltpu.VMEM((rounds,) + many, f32),
+            pltpu.SemaphoreType.DMA((40,)),
         ]
-        + Scatter.scratch(plan, own, depth, f32),
+        + Scatter.scratch(plan, own, depth, bf16)
+        + Line.scratch(groups, width, cut, 1)
+        + Line.scratch(groups, cut, 3 * width, PIECES)
+        + [pltpu.SemaphoreType.DMA((rounds,))] * 4,
         compiler_params=params(4),
         name="last",
-    )(qkv_grad, w_qkv, tok, middle_grad, gain)
+        cost_estimate=cost(75),
+    )(qkv_grad, w_qkv, tok, middle_grad, gain, out_part, first_all, sums2, in_sums, qv_sums)
 
 
 def segment_bounds(group, seq_lengths, seq_scripts, seq_place):
@@ -961,9 +1367,7 @@
     plan = Plan(devices)
     rows = own * devices
     width = w_qkv.shape[2]
-    hidden = w_in.shape[1]
     block = min(512, rows)
-    column = lax.axis_index("mp")
     bounds = segment_bounds(lax.axis_index("batch"), seq_lengths, seq_scripts, seq_place)
 
     def line(vector):
@@ -978,35 +1382,18 @@
         w_down, grad_all,
     )
 
-    def over_batch(partial, dimension):
-        return lax.psum_scatter(partial, "batch", scatter_dimension=dimension, tiled=True).astype(f32)
-
-    def weight_part(left, right):
-        return dot(left, right, 0, 0).astype(bf16)
-
-    down_weight_grad = over_batch(weight_part(activated, grad_all), 1)
-    middle_grad, branch_all, att_grad, sums2 = run_middle(
-        plan, hidden_grad, w_in, middle, out_grad, line(norm2_gain), w_out
+    groups = lax.axis_size("batch")
+    middle_grad, branch_all, att_grad, sums2, down_weight_grad, in_part2 = run_middle(
+        plan, groups, hidden_grad, w_in, middle, out_grad, line(norm2_gain), w_out, activated, grad_all, second_all
     )
-    in_weight_grad = over_batch(weight_part(second_all, hidden_grad), 0)
-    qkv_grad, block_out, qv_part = run_back(
-        plan, block, bounds, qkv, att, att_grad, sums, activated, w_down, middle, line(down_bias)
+    qkv_grad, block_out, qv_part, in_weight_grad, out_part = run_back(
+        plan, groups, block, bounds, qkv, att, att_grad, sums, activated, w_down, middle, line(down_bias),
+        in_part2, branch_all,
     )
-    out_weight_grad = over_batch(weight_part(att, branch_all), 1)
-    qkv_part = jnp.stack(
-        [weight_part(first_all, qkv_grad[:, part * width : (part + 1) * width]) for part in range(3)]
+    input_grad, out_weight_grad, qkv_weight_grad, vectors, spread = run_last(
+        plan, groups, qkv_grad, w_qkv, tokens, middle_grad, line(norm1_gain), out_part, first_all, sums2, in_part,
+        qv_part,
     )
-    qkv_weight_grad = over_batch(qkv_part, 1)
-    input_grad, sums1 = run_last(plan, qkv_grad, w_qkv, tokens, middle_grad, line(norm1_gain))
-
-    local = jnp.concatenate([qv_part[0], qv_part[1], in_part[0]])
-    spread = lax.dynamic_update_slice(
-        jnp.zeros((devices, local.shape[0]), f32), local[None], (column, jnp.int32(0))
-    )
-    packed = jnp.concatenate([sums1[:2].reshape(-1), sums2[:4].reshape(-1), spread.reshape(-1)])
-    packed = lax.psum(packed, ("batch", "mp"))
-    vectors = packed[: 6 * depth].reshape(6, depth)
-    spread = packed[6 * depth :].reshape(devices, -1)
     qv_bias_grad = jnp.stack([spread[:, :width].reshape(-1), spread[:, width : 2 * width].reshape(-1)])
     return (
         block_out,

time: 688 us -> 485 us (0.70)
  waiting for transfers between devices: 226 us -> 0 us
  Pallas kernels: 361 us -> 457 us
  matrix products: 50.2 us -> 0 us
  between operations: 16.1 us -> 0.92 us
  other arithmetic: 17.4 us -> 4.75 us
    psum x1 -> x0, waiting for transfers between devices: 226 us -> none  [body(): packed = lax.psum(packed, ('batch', 'mp'))]
    dot_general x6 -> x0, matrix products: 50.2 us -> none  [dot(): lax.dot_general(left, right, (((contract_left,), (contract_right,)), ((),...]
    pallas_call x1, Pallas kernels: 49.8 us -> 95 us  [run_last(): pl.pallas_call(kernel, out_shape=(jax.ShapeDtypeStruct((own, depth), bf16...]
    pallas_call x1, Pallas kernels: 47.2 us -> 85 us  [run_back(): pl.pallas_call(functools.partial(back_kernel, plan, block), out_shape=(ja...]
    pallas_call x1, Pallas kernels: 89 us -> 102 us  [run_middle(): pl.pallas_call(functools.partial(middle_kernel, plan), out_shape=(jax.Sha...]
    convert_element_type x4 -> x0, other arithmetic: 10 us -> none  [over_batch(): lax.psum_scatter(partial, 'batch', scatter_dimension=dimension, tiled=True)]
  transfers between devices with their start and end apart: 5 -> 0, of which waited for: 1 -> 0; matrix products, arithmetic and copies ran while one was open for 9% -> 0% of each run, Pallas kernels for 0% -> 0%
where the time goes in v2:
time: 485 us; the launch traced here: 476 us
  Pallas kernels  457 us (94%)
  local copies, waits for them, and re-layouts  13.3 us (3%)
    pallas_call x1, Pallas kernels, run_middle(): pl.pallas_call(functools.partial(middle_kernel, plan), out_shape=(jax.Sha...  102 us
    pallas_call x1, Pallas kernels, run_last(): pl.pallas_call(kernel, out_shape=(jax.ShapeDtypeStruct((own, depth), bf16...  95 us
    pallas_call x1, Pallas kernels, run_feed(): pl.pallas_call(functools.partial(feed_kernel, plan), out_shape=(jax.Shape...  91.2 us
    pallas_call x1, Pallas kernels, run_back(): pl.pallas_call(functools.partial(back_kernel, plan, block), out_shape=(ja...  85 us
    pallas_call x1, Pallas kernels, run_first(): pl.pallas_call(functools.partial(first_kernel, plan, block), out_shape=(j...  83.3 us
    unnamed x21, local copies, waits for them, and re-layouts  10.3 us

profile of v2, /device:TPU:8, one launch (start us, length us, event | category | flops | bytes accessed | tf_op | source)
XLA Modules:
  0.0 475.9 jit_solution(7944020204122791196)
XLA Ops:
  0.6 0.7 iota_add_fusion
  1.3 0.9 select_reduce_fusion
  2.2 1.3 compare_select_fusion.1
  3.5 1.2 pad_add_fusion.bounds
  4.8 0.8 fusion.2
  5.5 0.6 reshape.64.qv_bias
  6.1 83.3 %first.1 = (bf16[2048,2048]{1,0:T(8,128)(2,1)}, bf16[2048,768]{1,0:T(8,128)(2,1)}, bf16[2048,256]{1,0:T(8,128)(2,1)}, f32[8,2048]{1,0:T(8,128)}, bf16[2048,2048]{1,0:T(8,128)(2,1)}) custom-call(bf16[256,2048]{1,0:T(8,128)(2,1)} %refs_2_.1, f32[1,2048]{1,0:T(1,128)} %bitcast.46, f32[1,2048]{1,0:T(1,128)} %bitcast.40, bf16[3,2048,256]{2,1,0:T(8,128)(2,1)} %refs_1_.1, ...), custom_call_target="tpu_custom_call" | custom-call | flops 80000000000 | bytes 10000000 | tf_op jit(solution)/shard_map/first/pallas_call | solution.py:623
  89.4 91.2 %feed.1 = (bf16[2048,2048]{1,0:T(8,128)(2,1)}, bf16[2048,1024]{1,0:T(8,128)(2,1)}, bf16[2048,1024]{1,0:T(8,128)(2,1)}, f32[256,2048]{1,0:T(8,128)}, f32[1,1024]{1,0:T(1,128)}) custom-call(bf16[256,2048]{1,0:T(8,128)(2,1)} %refs_2_.1, bf16[2048,256]{1,0:T(8,128)(2,1)} %get-tuple-element.41.att, bf16[256,2048]{1,0:T(8,128)(2,1)} %w_out.3, f32[1,2048]{1,0:T(1,128)} %bitcast.41, ...), custom_call_target="tpu_custom_call" | custom-call | flops 89999998976 | bytes 10000000 | tf_op jit(solution)/shard_map/feed/pallas_call | solution.py:760
  180.6 102.5 %middle.1 = (f32[256,2048]{1,0:T(8,128)}, bf16[2048,2048]{1,0:T(8,128)(2,1)}, bf16[2048,256]{1,0:T(8,128)(2,1)}, f32[8,2048]{1,0:T(8,128)}, f32[1024,512]{1,0:T(8,128)}, /*index=5*/bf16[4,512,1024]{2,1,0:T(8,128)(2,1)}) custom-call(bf16[2048,1024]{1,0:T(8,128)(2,1)} %get-tuple-element.43.hidden_grad, bf16[2048,1024]{1,0:T(8,128)(2,1)} %w_in.3, ...), custom_call_target="tpu_custom_call" | custom-call | flops 80000000000 | bytes 10000000 | tf_op jit(solution)/shard_map/middle/pallas_call | solution.py:941
  283.1 85.0 %back.1 = (bf16[2048,768]{1,0:T(8,128)(2,1)}, bf16[256,2048]{1,0:T(8,128)(2,1)}, f32[8,256]{1,0:T(8,128)}, f32[512,1024]{1,0:T(8,128)}, bf16[4,256,512]{2,1,0:T(8,128)(2,1)}) custom-call(s32[9]{0:T(128)} %pad_add_fusion.bounds, bf16[2048,768]{1,0:T(8,128)(2,1)} %get-tuple-element.40.qkv, bf16[2048,256]{1,0:T(8,128)(2,1)} %get-tuple-element.41.att, ...), custom_call_target="tpu_custom_call" | custom-call | flops 74999996416 | bytes 10000000 | tf_op jit(solution)/shard_map/back/pallas_call | solution.py:1121
  368.0 0.0 copy-start.3
  368.0 95.0 %last.1 = (bf16[256,2048]{1,0:T(8,128)(2,1)}, f32[256,512]{1,0:T(8,128)}, f32[3,512,256]{2,1,0:T(8,128)}, f32[8,2048]{1,0:T(8,128)}, f32[8,1536]{1,0:T(8,128)}) custom-call(bf16[2048,768]{1,0:T(8,128)(2,1)} %get-tuple-element.52.refs_0_, bf16[3,2048,256]{2,1,0:T(8,128)(2,1)} %refs_1_.1, bf16[256,2048]{1,0:T(8,128)(2,1)} %refs_2_.1, ...), custom_call_target="tpu_custom_call" | custom-call | flops 74999996416 | bytes 10000000 | tf_op jit(solution)/shard_map/last/pallas_call | solution.py:1297
  463.1 0.0 copy-start.2
  463.1 0.8 slice_bitcast_fusion.2
  463.9 0.8 slice_bitcast_fusion
  464.7 0.6 copy.35
  465.3 0.6 pad_maximum_fusion
  466.0 1.7 fusion.1
  467.7 0.0 copy-done.3
  467.7 0.0 copy-start.4
  467.7 1.0 copy.42
  468.7 0.0 copy-start.1
  468.7 2.5 copy.43
  471.1 0.0 copy-done.2
  471.1 1.1 copy.44
  472.3 0.0 copy-done.4
  472.3 0.0 copy-start
  472.3 0.8 copy.45
  473.1 0.0 copy-done.1
  473.1 1.3 copy.46
  474.4 0.0 copy-done
  474.4 1.3 copy.47
  (4 shorter events, 0.0 us)
Async XLA Ops:
  368.0 99.7 %copy-start.3 = (bf16[256,2048]{1,0:T(8,128)(2,1)S(1)}, bf16[256,2048]{1,0:T(8,128)(2,1)}, u32[]{:S(2)}) copy-start(bf16[256,2048]{1,0:T(8,128)(2,1)} %get-tuple-element.92) | copy-start | bytes 3145732
  463.1 8.1 %copy-start.2 = (f32[3,512,256]{2,1,0:T(8,128)S(1)}, f32[3,512,256]{2,1,0:T(8,128)}, u32[]{:S(2)}) copy-start(f32[3,512,256]{2,1,0:T(8,128)} %get-tuple-element.96) | copy-start | bytes 4718596
  467.7 4.6 copy-start.4
  468.7 4.4 copy-start.1
  472.3 2.1 copy-start

commit v3 on v2

--- a/solution.py
+++ b/solution.py
@@ -46,7 +46,7 @@
 
 
 class Plan:
-    def __init__(self, devices):
+    def __init__(self, devices, halves=1):
         bits = []
         bit = 2
         while bit < devices:
@@ -54,12 +54,20 @@
             bit *= 2
         self.devices = devices
         self.bits = bits
-        self.orders = [tuple(bits)] + ([tuple(reversed(bits))] if len(bits) > 1 else [])
+        self.ways = [tuple(bits)] + ([tuple(reversed(bits))] if len(bits) > 1 else [])
+        self.halves = halves
+        self.orders = self.ways * halves
         self.parts = len(self.orders)
         self.offsets = list(range(0, devices, 2))
         self.keys = [(part, offset) for part in range(self.parts) for offset in self.offsets if offset]
-        self.keys.sort(key=lambda key: (bin(key[1]).count("1"), self.last(*key)))
+        self.keys.sort(key=lambda key: (self.half(key[0]), bin(key[1]).count("1"), self.last(*key)))
         self.shares = [(part, offset) for offset in self.offsets for part in range(self.parts)]
+
+    def half(self, part):
+        return part // len(self.ways)
+
+    def parts_of(self, half):
+        return range(half * len(self.ways), (half + 1) * len(self.ways))
 
     def last(self, part, offset):
         steps = [step for step, bit in enumerate(self.orders[part]) if bit & offset]
@@ -86,36 +94,83 @@
     def beside(self, step):
         return (self.batch + step, self.me)
 
-    def barrier(self, line=False, halves=False):
+    def around(self, step):
+        return (lax.rem(self.batch + step, self.groups), self.me)
+
+    def barrier(self, groups=False):
         semaphore = pltpu.get_barrier_semaphore()
-        masks = [1] + self.plan.bits
-        for mask in masks:
-            pl.semaphore_signal(semaphore, inc=1, device_id=self.at(mask), device_id_type=MESH)
-        count = len(masks)
-        if line:
-            for step, there in ((-1, self.batch > 0), (1, self.batch < self.groups - 1)):
-
-                @pl.when(there)
-                def greet():
-                    pl.semaphore_signal(semaphore, inc=1, device_id=self.beside(step), device_id_type=MESH)
-
-                count = count + there.astype(jnp.int32)
-        if halves:
-            for bit in self.group_bits():
-                pl.semaphore_signal(semaphore, inc=1, device_id=self.across(bit), device_id_type=MESH)
-                count = count + 1
-        pl.semaphore_wait(semaphore, count)
-
-    def group_bits(self):
-        bits = []
-        bit = 1
-        while bit < self.groups:
-            bits.append(bit)
-            bit *= 2
-        return bits
-
-    def across(self, bit):
-        return (flip(self.batch, bit), self.me)
+        partners = [self.at(mask) for mask in [1] + self.plan.bits]
+        if groups:
+            partners += [self.around(step) for step in range(1, self.groups)]
+        for partner in partners:
+            pl.semaphore_signal(semaphore, inc=1, device_id=partner, device_id_type=MESH)
+        pl.semaphore_wait(semaphore, len(partners))
+
+
+class Total:
+    def __init__(self, place, value, sent, came, slots, sems):
+        self.place, self.value, self.sent, self.came, self.slots = place, value, sent, came, slots
+        self.send, self.recv, self.slot_send, self.slot_recv = sems
+
+    def plane(self, others=()):
+        totals = (self,) + tuple(others)
+        for index, mask in enumerate([1] + self.place.plan.bits):
+            copies = [
+                pltpu.make_async_remote_copy(
+                    src_ref=total.sent.at[index],
+                    dst_ref=total.came.at[index],
+                    send_sem=total.send.at[index],
+                    recv_sem=total.recv.at[index],
+                    device_id=self.place.at(mask),
+                    device_id_type=MESH,
+                )
+                for total in totals
+            ]
+            for total, copy in zip(totals, copies):
+                total.sent[index] = total.value[...]
+                copy.start()
+            for total, copy in zip(totals, copies):
+                copy.wait_recv()
+                total.value[...] = total.sent[index] + total.came[index]
+                copy.wait_send()
+
+    def slot(self, step):
+        return pltpu.make_async_remote_copy(
+            src_ref=self.value,
+            dst_ref=self.slots.at[step],
+            send_sem=self.slot_send.at[step - 1],
+            recv_sem=self.slot_recv.at[step - 1],
+            device_id=self.place.around(step),
+            device_id_type=MESH,
+        )
+
+    def begin(self):
+        self.slots[0] = self.value[...]
+        for step in range(1, self.place.groups):
+            self.slot(step).start()
+
+    def end(self, result):
+        for step in range(1, self.place.groups):
+            self.slot(step).wait()
+        groups = self.place.groups
+        total = self.slots[self.place.batch]
+        for group in range(1, groups):
+            total = total + self.slots[lax.rem(self.place.batch + groups - group, groups)]
+        result[...] = total
+
+    @staticmethod
+    def scratch(plan, groups, shape):
+        rounds = len(plan.bits) + 1
+        return [
+            pltpu.VMEM(shape, f32),
+            pltpu.VMEM((rounds,) + shape, f32),
+            pltpu.VMEM((rounds,) + shape, f32),
+            pltpu.VMEM((groups,) + shape, f32),
+            pltpu.SemaphoreType.DMA((rounds,)),
+            pltpu.SemaphoreType.DMA((rounds,)),
+            pltpu.SemaphoreType.DMA((max(groups - 1, 1),)),
+            pltpu.SemaphoreType.DMA((max(groups - 1, 1),)),
+        ]
 
 
 class Gather:
@@ -169,11 +224,11 @@
             device_id_type=MESH,
         ).wait_recv()
 
-    def start(self):
-        for part in range(self.plan.parts):
+    def start(self, half=0):
+        for part in self.plan.parts_of(half):
             self.core((part, 0)).start()
         for key in self.plan.keys:
-            if bin(key[1]).count("1") == 1:
+            if bin(key[1]).count("1") == 1 and self.plan.half(key[0]) == half:
                 self.link(key).start()
 
     def arrive(self, key):
@@ -183,18 +238,30 @@
             self.link((part, target)).start()
         self.core(key).start()
 
-    def share(self, offset):
-        for part in range(self.plan.parts):
+    def share(self, offset, half=0):
+        for part in self.plan.parts_of(half):
             index = self.plan.shares.index((part, offset))
             self.landed(self.span(offset | 1, part), self.core_recv.at[index])
 
     def steps(self):
-        singles = [offset for offset in self.plan.offsets if bin(offset).count("1") == 1]
-        rest = [offset for offset in self.plan.offsets if bin(offset).count("1") > 1]
-        rest.sort(key=lambda offset: bin(offset).count("1"))
-        groups = [[key for key in self.plan.keys if key[1] in singles]]
-        groups += [[key for key in self.plan.keys if key[1] == offset] for offset in rest]
-        return groups, [singles] + [[offset] for offset in rest]
+        result = []
+        for half in range(self.plan.halves):
+            for count in range(1, len(self.plan.bits) + 1):
+                keys = [
+                    key
+                    for key in self.plan.keys
+                    if self.plan.half(key[0]) == half and bin(key[1]).count("1") == count
+                ]
+                offsets = [offset for offset in self.plan.offsets if bin(offset).count("1") == count]
+                result.append((half, keys, offsets))
+        return result
+
+    def pieces(self, offset, half):
+        count = self.rows // self.plan.halves
+        chip = lax.div(flip(self.place.me, offset), 2) * 2
+        return [
+            pl.ds(pl.multiple_of((chip + core) * self.rows + half * count, count), count) for core in range(2)
+        ]
 
     def finish(self):
         for key in self.plan.keys:
@@ -262,27 +329,37 @@
         loop(self.part_rows, self.step, add)
         self.link((part, offset)).start()
 
+    def free(self, offset, half):
+        for part in self.plan.parts_of(half):
+            if offset and not self.plan.later(part, offset):
+                self.pass_on(part, offset)
+
+    def bound(self, half):
+        for offset in self.order:
+            for part in self.plan.parts_of(half):
+                if offset and self.plan.later(part, offset):
+                    self.pass_on(part, offset)
+
     def begin(self, partial, between=None):
         for number, offset in enumerate(self.order):
             index = offset // 2
+            if offset == 0:
+                self.bound(0)
             partial(flip(self.place.me, offset | 1), self.core_out.at[index])
             self.core(offset).start()
             partial(flip(self.place.me, offset), self.kept.at[index])
             self.core(offset).wait_recv()
-            for part in range(self.plan.parts):
-                if offset and not self.plan.later(part, offset):
-                    self.pass_on(part, offset)
+            for half in range(self.plan.halves):
+                self.free(offset, half)
             if between is not None:
                 between(number)
 
     def middle(self):
-        for offset in self.order:
-            for part in range(self.plan.parts):
-                if offset and self.plan.later(part, offset):
-                    self.pass_on(part, offset)
-
-    def end(self, use):
-        for part in range(self.plan.parts):
+        for half in range(1, self.plan.halves):
+            self.bound(half)
+
+    def end(self, use, half=0):
+        for part in self.plan.parts_of(half):
             arrived = [(part, target) for target in self.plan.later(part, 0)]
             for key in arrived:
                 self.link(key).wait_recv()
@@ -342,20 +419,24 @@
             device_id_type=MESH,
         )
 
-    def start(self, target):
-        if target > 0:
+    def start(self, target, near=None, pieces=None):
+        if target > 0 and near in (None, target == 1):
 
             @pl.when(self.batch == 0)
             def first():
-                for piece in range(self.pieces):
+                for piece in range(self.pieces) if pieces is None else pieces:
                     self.copy(True, target, piece, self.own.at[target]).start()
 
-        if target < self.groups - 1:
+        if target < self.groups - 1 and near in (None, target == self.groups - 2):
 
             @pl.when(self.batch == self.groups - 1)
             def last():
-                for piece in range(self.pieces):
+                for piece in range(self.pieces) if pieces is None else pieces:
                     self.copy(False, target, piece, self.own.at[target]).start()
+
+    def start_near(self, pieces=None):
+        for target in range(self.groups):
+            self.start(target, True, pieces)
 
     def order(self):
         count = self.groups
@@ -391,43 +472,39 @@
                     loop(self.rows, self.step, add)
                     copy.start()
 
-    def end(self, target_ref):
+    def export(self, outs, moves, columns=None):
         below, above = self.batch > 0, self.batch < self.groups - 1
-        total = self.own.shape[1]
-
-        @pl.when(below)
-        def up():
-            slot = self.slot(True, self.batch)
-            for piece in range(self.pieces):
-                self.copy(True, self.batch, piece, slot).wait_recv()
-
-        @pl.when(above)
-        def down():
-            slot = self.slot(False, self.batch)
-            for piece in range(self.pieces):
-                self.copy(False, self.batch, piece, slot).wait_recv()
-
-        def add(sides):
-            def rows_of(start):
-                rows = pl.ds(start, self.step)
-                value = self.own[self.batch, rows, :].astype(f32)
-                for upward in sides:
-                    value += self.slot(upward, self.batch)[rows, :].astype(f32)
-                target_ref[rows, :] = value
-
-            loop(total, self.step, rows_of)
-
-        @pl.when(jnp.logical_not(above))
-        def at_top():
-            add([True])
-
-        @pl.when(jnp.logical_not(below))
-        def at_bottom():
-            add([False])
-
-        @pl.when(below & above)
-        def between():
-            add([True, False])
+        jobs = []
+        for out, there, upward in ((outs[0], None, None), (outs[1], below, True), (outs[2], above, False)):
+            slot = self.own.at[self.batch] if there is None else self.slot(upward, self.batch)
+            if columns is None:
+                copies = [moves.make(slot, out)]
+            else:
+                copies = [
+                    moves.make(slot.at[:, pl.ds(part * columns, columns)], out.at[part])
+                    for part in range(out.shape[0])
+                ]
+            jobs.append((there, copies))
+
+            def begin():
+                if there is not None:
+                    for piece in range(self.pieces):
+                        self.copy(upward, self.batch, piece, slot).wait_recv()
+                for copy in copies:
+                    copy.start()
+
+            begin() if there is None else pl.when(there)(begin)
+
+        def wait():
+            for there, copies in jobs:
+
+                def done():
+                    for copy in copies:
+                        copy.wait()
+
+                done() if there is None else pl.when(there)(done)
+
+        return wait
 
     def finish(self):
         for target in range(self.groups):
@@ -454,9 +531,13 @@
     def __init__(self, sems):
         self.sems, self.count = sems, 0
 
-    def start(self, source, target):
+    def make(self, source, target):
         copy = pltpu.make_async_copy(source, target, self.sems.at[self.count])
         self.count += 1
+        return copy
+
+    def start(self, source, target):
+        copy = self.make(source, target)
         copy.start()
         return copy
 
@@ -477,12 +558,27 @@
     )
 
 
-def segment_starts(bounds, rows):
+def segment_starts(group, lengths, scripts, places, rows):
     position = lax.broadcasted_iota(jnp.int32, (1, rows), 1)
     first = jnp.zeros((1, rows), jnp.int32)
-    for index in range(bounds.shape[0]):
-        first = jnp.maximum(first, jnp.where(position >= bounds[index], bounds[index], 0))
-    return first
+    count = lengths.shape[0]
+    number = [lengths[index] for index in range(count)]
+    script = [scripts[index] for index in range(count)]
+    mine = [places[index] == group for index in range(count)]
+    own = [jnp.where(mine[index], number[index], 0) for index in range(count)]
+    total = own[0]
+    for index in range(1, count):
+        total = total + own[index]
+    for index in range(count):
+        offset = jnp.int32(0)
+        for other in range(count):
+            if other < index:
+                offset = offset + jnp.where(script[other] <= script[index], own[other], 0)
+            elif other > index:
+                offset = offset + jnp.where(script[other] < script[index], own[other], 0)
+        bound = jnp.where(mine[index], offset, 0)
+        first = jnp.maximum(first, jnp.where(position >= bound, bound, 0))
+    return jnp.maximum(first, jnp.where(position >= total, total, 0))
 
 
 def head_columns(part, head, width):
@@ -490,7 +586,7 @@
 
 
 def first_kernel(
-    plan, block, tok, gain, shift, w_qkv, qv_bias, bounds, out_grad, first_out, qkv_out, att_out,
+    plan, block, tok, gain, shift, w_qkv, qv_bias, lengths, scripts, places, out_grad, first_out, qkv_out, att_out,
     sum_out, grad_out, buf, weights, qkv, starts, sums, attended, local, *sems,
 ):
     place = Place(plan)
@@ -513,7 +609,7 @@
     gather = Gather(place, buf, None, own, sems[:4])
     gather.start()
     stores = [moves.start(out_grad, grad_out.at[pl.ds(mine, own), :])]
-    starts[...] = segment_starts(bounds, rows)
+    starts[...] = segment_starts(place.batch, lengths, scripts, places, rows)
     for copy in loads:
         copy.wait()
 
@@ -521,20 +617,25 @@
         chip = lax.div(flip(place.me, offset), 2)
         span = pl.ds(pl.multiple_of(chip * 2 * own, 2 * own), 2 * own)
         stores.append(moves.start(buf.at[span, :], first_out.at[span, :]))
-        qkv[span, :] = (dot(buf[span, :], weights[...], 1, 0) + qv_bias[...]).astype(bf16)
+        product = dot(buf[span, :], weights[...], 1, 0)
+        qkv[span, 0:width] = (product[:, 0:width] + qv_bias[0:1, :]).astype(bf16)
+        qkv[span, width : 2 * width] = product[:, width : 2 * width].astype(bf16)
+        qkv[span, 2 * width : 3 * width] = (product[:, 2 * width :] + qv_bias[1:2, :]).astype(bf16)
 
     gather.share(0)
     project(0)
-    arrivals, chips = gather.steps()
-    for keys, offsets in zip(arrivals, chips):
+    steps = gather.steps()
+    grads = Gather(place, grad_out, out_grad, own, sems[4:])
+    for number, (half, keys, offsets) in enumerate(steps):
         for key in keys:
             gather.arrive(key)
+        if number == max(len(steps) - 2, 0):
+            grads.start()
         for offset in offsets:
             gather.share(offset)
             project(offset)
     gather.finish()
-    gather = Gather(place, grad_out, out_grad, own, sems[4:])
-    gather.start()
+    gather = grads
     stores.append(moves.start(qkv, qkv_out))
 
     scale = HEAD_DIM ** (-0.5) * LOG2E
@@ -584,18 +685,17 @@
             sums[pl.ds(head, 1), span] = top + jnp.log2(total)
 
     blocks = rows // block
-    groups = list(zip(arrivals, chips))
     taken = 0
     for index in range(blocks):
         attend(index)
-        if index >= blocks - 2 and taken < len(groups):
-            for key in groups[taken][0]:
+        if index >= blocks - 2 and taken < len(steps):
+            for key in steps[taken][1]:
                 gather.arrive(key)
             taken += 1
     stores.append(moves.start(attended, att_out))
     stores.append(moves.start(sums, sum_out))
-    while taken < len(groups):
-        for key in groups[taken][0]:
+    while taken < len(steps):
+        for key in steps[taken][1]:
             gather.arrive(key)
         taken += 1
     for offset in plan.offsets:
@@ -615,7 +715,7 @@
     return pl.CostEstimate(flops=micros * 10**9, bytes_accessed=10**7, transcendentals=0)
 
 
-def run_first(plan, block, tok, gain, shift, w_qkv, qv_bias, bounds, out_grad):
+def run_first(plan, block, tok, gain, shift, w_qkv, qv_bias, order, out_grad):
     own, depth = tok.shape
     rows = own * plan.devices
     width = w_qkv.shape[2]
@@ -629,7 +729,7 @@
             jax.ShapeDtypeStruct((8, rows), f32),
             jax.ShapeDtypeStruct((rows, depth), bf16),
         ),
-        in_specs=[VMEM, VMEM, VMEM, ANY, VMEM, SMEM, ANY],
+        in_specs=[VMEM, VMEM, VMEM, ANY, VMEM, SMEM, SMEM, SMEM, ANY],
         out_specs=(ANY,) * 5,
         scratch_shapes=[
             pltpu.VMEM((rows, depth), bf16),
@@ -644,13 +744,17 @@
         compiler_params=params(0),
         name="first",
         cost_estimate=cost(80),
-    )(tok, gain, shift, w_qkv, qv_bias, bounds, out_grad)
+    )(tok, gain, shift, w_qkv, qv_bias, *order, out_grad)
+
+
+def joined(ref, pieces):
+    return jnp.concatenate([ref[piece, :] for piece in pieces], axis=0)
 
 
 def feed_kernel(
     plan, tok, att, w_out, out_bias, gain, shift, w_in, in_bias, w_down, grad_all,
     second_out, act_out, hidden_out, middle_out, bias_out,
-    att_in, w_o, w_i, w_d, grad_in, buf, act, back, middle, local, *rest,
+    att_in, w_o, w_i, w_d, grad_in, up, buf, act, back, middle, local, *rest,
 ):
     scatter_refs, gather_sems = rest[:9], rest[9:]
     place = Place(plan)
@@ -661,8 +765,16 @@
     moves = Moves(local)
     load_att = moves.start(att, att_in)
     load_out = moves.start(w_out, w_o)
+    load_down = moves.start(w_down, w_d)
+    grad_loads = {}
+
+    def load_grad(number):
+        lines = pl.ds(number * chip_rows, chip_rows)
+        grad_loads[number] = moves.start(grad_all.at[lines, :], grad_in.at[number % 2])
+
+    load_grad(0)
+    load_grad(1)
     load_in = moves.start(w_in, w_i)
-    load_down = moves.start(w_down, w_d)
     place.barrier()
     scatter = Scatter(place, own, depth, *scatter_refs[:5], scatter_refs[5:])
     load_att.wait()
@@ -677,8 +789,25 @@
 
         loop(depth, tile, columns)
 
+    part_cols = min(512, hidden_width)
+    chips = rows // chip_rows
+
+    def raise_grad(number):
+        grad_loads[number].wait()
+
+        def columns(start):
+            cols = pl.ds(start, part_cols)
+            up[pl.ds(number * chip_rows, chip_rows), cols] = dot(grad_in[number % 2], w_d[cols, :], 1, 1)
+
+        loop(hidden_width, part_cols, columns)
+        if number + 2 < chips:
+            load_grad(number + 2)
+
     scatter.begin(partial)
     scatter.middle()
+    load_down.wait()
+    for number in range(chips):
+        raise_grad(number)
     mine = pl.multiple_of(place.me * own, own)
 
     def close(start, count, value):
@@ -688,65 +817,50 @@
         unit, _ = norm_rows(total)
         buf[pl.ds(pl.multiple_of(mine + start, count), count), :] = (unit * gain[...] + shift[...]).astype(bf16)
 
-    scatter.end(close)
     gather = Gather(place, buf, None, own, gather_sems)
-    gather.start()
+    for half in range(plan.halves):
+        scatter.end(close, half)
+        gather.start(half)
     scatter.finish()
     stores = [moves.start(middle, middle_out)]
     load_in.wait()
-    load_down.wait()
     bias_out[...] = jnp.zeros_like(bias_out)
-    part_cols = min(512, hidden_width)
-
-    def chip_span(offset):
-        chip = lax.div(flip(place.me, offset), 2)
-        return pl.ds(pl.multiple_of(chip * chip_rows, chip_rows), chip_rows)
-
-    order = []
-
-    def prefetch(offset):
-        slot = len(order) % 2
-        order.append(moves.start(grad_all.at[chip_span(offset), :], grad_in.at[slot]))
-
-    def expand(offset, slot):
-        span = chip_span(offset)
-        stores.append(moves.start(buf.at[span, :], second_out.at[span, :]))
-        order[slot].wait()
+
+    def expand(offset, half):
+        pieces = gather.pieces(offset, half)
+        count = own // plan.halves
 
         def columns(start):
             cols = pl.ds(start, part_cols)
-            pre = dot(buf[span, :], w_i[:, cols], 1, 0) + in_bias[:, cols]
-            up = dot(grad_in[slot % 2], w_d[cols, :], 1, 1)
+            pre = dot(joined(buf, pieces), w_i[:, cols], 1, 0) + in_bias[:, cols]
+            raised = jnp.concatenate([up[piece, cols] for piece in pieces], axis=0)
             root = 0.7978845608028654
             square = pre * pre
             inner = jnp.tanh(root * (pre + 0.044715 * (square * pre)))
-            half = 0.5 * (1.0 + inner)
-            slope = half + 0.5 * pre * (1.0 - inner * inner) * (root * (1.0 + 3 * 0.044715 * square))
-            act[span, cols] = (pre * half).astype(bf16)
-            down = (up * slope).astype(bf16)
-            back[span, cols] = down
+            rise = 0.5 * (1.0 + inner)
+            slope = rise + 0.5 * pre * (1.0 - inner * inner) * (root * (1.0 + 3 * 0.044715 * square))
+            lifted = (pre * rise).astype(bf16)
+            down = (raised * slope).astype(bf16)
+            for index, piece in enumerate(pieces):
+                act[piece, cols] = lifted[index * count : (index + 1) * count]
+                back[piece, cols] = down[index * count : (index + 1) * count]
             bias_out[:, cols] += jnp.sum(down.astype(f32), axis=0, keepdims=True)
 
         loop(hidden_width, part_cols, columns)
-        stores.append(moves.start(act.at[span, :], act_out.at[span, :]))
-        stores.append(moves.start(back.at[span, :], hidden_out.at[span, :]))
-
-    arrivals, chips = gather.steps()
-    sequence = [0] + [offset for offsets in chips for offset in offsets]
-    prefetch(sequence[0])
-    prefetch(sequence[1])
-    gather.share(0)
-    expand(0, 0)
-    number = 1
-    for keys, offsets in zip(arrivals, chips):
+        for piece in pieces:
+            stores.append(moves.start(buf.at[piece, :], second_out.at[piece, :]))
+            stores.append(moves.start(act.at[piece, :], act_out.at[piece, :]))
+            stores.append(moves.start(back.at[piece, :], hidden_out.at[piece, :]))
+
+    for half in range(plan.halves):
+        gather.share(0, half)
+        expand(0, half)
+    for half, keys, offsets in gather.steps():
         for key in keys:
             gather.arrive(key)
         for offset in offsets:
-            if number + 1 < len(sequence):
-                prefetch(sequence[number + 1])
-            gather.share(offset)
-            expand(offset, number)
-            number += 1
+            gather.share(offset, half)
+            expand(offset, half)
     gather.finish()
     for copy in stores:
         copy.wait()
@@ -774,11 +888,12 @@
             pltpu.VMEM((depth, hidden), bf16),
             pltpu.VMEM((hidden, depth), bf16),
             pltpu.VMEM((2, 2 * own, depth), bf16),
+            pltpu.VMEM((rows, hidden), f32),
             pltpu.VMEM((rows, depth), bf16),
             pltpu.VMEM((rows, hidden), bf16),
             pltpu.VMEM((rows, hidden), bf16),
             pltpu.VMEM((own, depth), f32),
-            pltpu.SemaphoreType.DMA((48,)),
+            pltpu.SemaphoreType.DMA((128,)),
         ]
         + Scatter.scratch(plan, own, depth, bf16)
         + Gather.semaphores(plan),
@@ -791,12 +906,40 @@
 PIECES = 2
 
 
+def add_parts(place, parts, target):
+    below, above = place.batch > 0, place.batch < place.groups - 1
+    step = min(32, target.shape[0])
+
+    def add(chosen):
+        def rows_of(start):
+            rows = pl.ds(start, step)
+            value = chosen[0][rows, :].astype(f32)
+            for part in chosen[1:]:
+                value += part[rows, :].astype(f32)
+            target[rows, :] = value
+
+        loop(target.shape[0], step, rows_of)
+
+    pl.when(jnp.logical_not(above))(lambda: add([parts[0], parts[1]]))
+    pl.when(jnp.logical_not(below))(lambda: add([parts[0], parts[2]]))
+    pl.when(below & above)(lambda: add(parts))
+
+
+def spread_rows(place, target, rows):
+    mine = lax.broadcasted_iota(jnp.int32, (target.shape[0], 1), 0) == place.me
+    start = 0
+    for row in rows:
+        target[:, pl.ds(start, row.shape[1])] = jnp.where(mine, row, 0.0)
+        start += row.shape[1]
+
+
 def middle_kernel(
-    plan, hidden_grad, w_in, middle, out_grad, gain, w_out, activated, grad_all, second_all,
-    middle_grad_out, branch_out, att_grad_out, sums_out, down_out, in_part_out,
-    h_in, w_i, w_o, buf, middle_grad, att_grad, act, staged, total, local, *rest,
+    plan, hidden_grad, w_in, middle, out_grad, gain, w_out, activated, grad_all, second_all, in_sums,
+    middle_grad_out, branch_out, att_grad_out, sums_out, in_sums_out, down_out0, down_out1, down_out2, in_part_out,
+    h_in, w_i, w_o, buf, middle_grad, att_grad, act, staged, local, *rest,
 ):
-    scatter_refs, gather_sems, line_refs = rest[:9], rest[9:13], rest[13:]
+    down_outs = (down_out0, down_out1, down_out2)
+    scatter_refs, gather_sems, line_refs, total_refs = rest[:9], rest[9:13], rest[13:20], rest[20:]
     place = Place(plan)
     own, depth = middle.shape
     rows = buf.shape[0]
@@ -807,13 +950,15 @@
     moves = Moves(local)
     loads = [moves.start(hidden_grad, h_in), moves.start(w_in, w_i)]
     load_act = moves.start(activated, act)
-    load_grad = moves.start(grad_all, buf)
+    order = [index for pair in zip(range(groups - 1, -1, -1), range(groups)) for index in pair][:groups]
+    load_grad = [
+        moves.start(grad_all.at[:, pl.ds(target * cut, cut)], buf.at[:, pl.ds(target * cut, cut)])
+        for target in order
+    ]
     load_out = moves.start(w_out, w_o)
-    place.barrier(line=True)
+    place.barrier(groups=True)
     scatter = Scatter(place, own, depth, *scatter_refs[:5], scatter_refs[5:])
     line = Line(place, *line_refs[:3], PIECES, line_refs[3:])
-    for copy in loads:
-        copy.wait()
     tile = min(1024, depth)
 
     def partial(owner, target):
@@ -824,27 +969,32 @@
 
         loop(depth, tile, columns)
 
-    order = line.order()
     part = min(512, hidden)
 
-    def down_slice(target):
+    def down_slice(index):
+        target = order[index]
+        load_grad[index].wait()
+
         def piece(start):
             line.own[target, pl.ds(start, part), :] = dot(
                 act[:, pl.ds(start, part)], buf[:, pl.ds(target * cut, cut)], 0, 0
             ).astype(bf16)
 
         loop(hidden, part, piece)
-        line.start(target)
+        line.start(target, False)
+
+    for copy in loads:
+        copy.wait()
 
     def between(number):
         if number == 0:
             load_act.wait()
-            load_grad.wait()
-            for target in order[:2]:
-                down_slice(target)
-        if number == 1:
-            for target in order[2:]:
-                down_slice(target)
+            for index in range(groups // 2):
+                down_slice(index)
+        if number == min(2, len(plan.offsets) - 1):
+            for index in range(groups // 2, groups):
+                down_slice(index)
+            line.start_near()
 
     scatter.begin(partial, between)
 
@@ -877,12 +1027,17 @@
         load_slice(number)
     line.tick(ticks.pop(0))
     scatter.middle()
-    half = groups // 2
-    for number in range(half):
+    half_groups = groups // 2
+    for number in range(half_groups):
         in_slice(number)
     line.tick(ticks.pop(0))
     mine = pl.multiple_of(place.me * own, own)
-    sums_out[...] = jnp.zeros_like(sums_out)
+    totals = [
+        Total(place, *total_refs[index : index + 4], total_refs[index + 4 : index + 8]) for index in (0, 8)
+    ]
+    own_sums = totals[0].value
+    own_sums[...] = jnp.zeros_like(own_sums)
+    totals[1].value[...] = in_sums[...]
 
     def close(start, count, value):
         span = pl.ds(start, count)
@@ -890,49 +1045,56 @@
         sum_rows = out_grad[span, :].astype(f32) + norm_back(value, unit, inverse, gain[...])
         middle_grad[span, :] = sum_rows
         buf[pl.ds(pl.multiple_of(mine + start, count), count), :] = sum_rows.astype(bf16)
-        sums_out[0:1, :] += jnp.sum(value * unit, axis=0, keepdims=True)
-        sums_out[1:2, :] += jnp.sum(value, axis=0, keepdims=True)
-        sums_out[2:3, :] += jnp.sum(sum_rows, axis=0, keepdims=True)
-        sums_out[3:4, :] += jnp.sum(out_grad[span, :].astype(f32), axis=0, keepdims=True)
-
-    scatter.end(close)
+        own_sums[0:1, :] += jnp.sum(value * unit, axis=0, keepdims=True)
+        own_sums[1:2, :] += jnp.sum(value, axis=0, keepdims=True)
+        own_sums[2:3, :] += jnp.sum(sum_rows, axis=0, keepdims=True)
+        own_sums[3:4, :] += jnp.sum(out_grad[span, :].astype(f32), axis=0, keepdims=True)
+
     gather = Gather(place, buf, None, own, gather_sems)
-    gather.start()
+    for half in range(plan.halves):
+        scatter.end(close, half)
+        gather.start(half)
+    for total in totals:
+        total.begin()
+    line.tick(ticks.pop(0))
     scatter.finish()
     stores = [moves.start(middle_grad, middle_grad_out)]
     load_out.wait()
 
-    def project(offset):
-        chip = lax.div(flip(place.me, offset), 2)
-        span = pl.ds(pl.multiple_of(chip * chip_rows, chip_rows), chip_rows)
-        stores.append(moves.start(buf.at[span, :], branch_out.at[span, :]))
-        att_grad[span, :] = dot(buf[span, :], w_o[...], 1, 1).astype(bf16)
-
-    gather.share(0)
-    project(0)
-    for number in range(half, groups):
+    def project(offset, half):
+        pieces = gather.pieces(offset, half)
+        count = own // plan.halves
+        product = dot(joined(buf, pieces), w_o[...], 1, 1).astype(bf16)
+        for index, piece in enumerate(pieces):
+            att_grad[piece, :] = product[index * count : (index + 1) * count]
+            stores.append(moves.start(buf.at[piece, :], branch_out.at[piece, :]))
+
+    for half in range(plan.halves):
+        gather.share(0, half)
+        project(0, half)
+    for number in range(half_groups, groups):
         in_slice(number)
     line.tick(ticks.pop(0))
-    arrivals, chips = gather.steps()
-    for keys, offsets in zip(arrivals, chips):
+    for half, keys, offsets in gather.steps():
         for key in keys:
             gather.arrive(key)
         for offset in offsets:
-            gather.share(offset)
-            project(offset)
-        line.tick(ticks.pop(0))
+            gather.share(offset, half)
+            project(offset, half)
     stores.append(moves.start(att_grad, att_grad_out))
     for number in ticks:
         line.tick(number)
-    line.end(total)
-    stores.append(moves.start(total, down_out))
+    exported = line.export(down_outs, moves)
+    for total, total_out in zip(totals, (sums_out, in_sums_out)):
+        total.end(total_out)
     gather.finish()
     line.finish()
     for copy in stores + in_stores[-2:]:
         copy.wait()
-
-
-def run_middle(plan, groups, hidden_grad, w_in, middle, out_grad, gain, w_out, activated, grad_all, second_all):
+    exported()
+
+
+def run_middle(plan, groups, hidden_grad, w_in, middle, out_grad, gain, w_out, activated, grad_all, second_all, in_sums):
     own, depth = middle.shape
     rows = own * plan.devices
     width = w_out.shape[0]
@@ -944,12 +1106,13 @@
             jax.ShapeDtypeStruct((own, depth), f32),
             jax.ShapeDtypeStruct((rows, depth), bf16),
             jax.ShapeDtypeStruct((rows, width), bf16),
-            jax.ShapeDtypeStruct((8, depth), f32),
-            jax.ShapeDtypeStruct((hidden, cut), f32),
-            jax.ShapeDtypeStruct((groups, cut, hidden), bf16),
-        ),
-        in_specs=[ANY, ANY, VMEM, VMEM, VMEM, ANY, ANY, ANY, ANY],
-        out_specs=(ANY, ANY, ANY, VMEM, ANY, ANY),
+            jax.ShapeDtypeStruct((4, depth), f32),
+            jax.ShapeDtypeStruct(in_sums.shape, f32),
+        )
+        + (jax.ShapeDtypeStruct((hidden, cut), bf16),) * 3
+        + (jax.ShapeDtypeStruct((groups, cut, hidden), bf16),),
+        in_specs=[ANY, ANY, VMEM, VMEM, VMEM, ANY, ANY, ANY, ANY, VMEM],
+        out_specs=(ANY, ANY, ANY, VMEM, VMEM, ANY, ANY, ANY, ANY),
         scratch_shapes=[
             pltpu.VMEM((rows, hidden), bf16),
             pltpu.VMEM((depth, hidden), bf16),
@@ -959,25 +1122,29 @@
             pltpu.VMEM((rows, width), bf16),
             pltpu.VMEM((rows, max(hidden, 2 * cut)), bf16),
             pltpu.VMEM((2, cut, hidden), bf16),
-            pltpu.VMEM((hidden, cut), f32),
-            pltpu.SemaphoreType.DMA((40,)),
+            pltpu.SemaphoreType.DMA((64,)),
         ]
         + Scatter.scratch(plan, own, depth, bf16)
         + Gather.semaphores(plan)
-        + Line.scratch(groups, hidden, cut, PIECES),
+        + Line.scratch(groups, hidden, cut, PIECES)
+        + Total.scratch(plan, groups, (4, depth))
+        + Total.scratch(plan, groups, in_sums.shape),
         compiler_params=params(2),
         name="middle",
         cost_estimate=cost(80),
-    )(hidden_grad, w_in, middle, out_grad, gain, w_out, activated, grad_all, second_all)
+    )(hidden_grad, w_in, middle, out_grad, gain, w_out, activated, grad_all, second_all, in_sums)
 
 
 def back_kernel(
-    plan, block, bounds, qkv, att, att_grad, sums, activated, w_down, middle, down_bias, in_part, branch_all,
-    qkv_grad_out, block_out, bias_out, in_out, out_part_out,
-    qkv_in, att_in, grad_in, act_in, w_d, starts, key_grad, value_grad, result, branch, staged, total, local,
+    plan, block, lengths, scripts, places, qkv, att, att_grad, sums, activated, w_down, middle, down_bias, in_part, branch_all, sums2, in_sums,
+    down0, down1, down2,
+    qkv_grad_out, block_out, down_out, in_out0, in_out1, in_out2, out_part_out, vectors_out, spread_out,
+    qkv_in, att_in, grad_in, act_in, w_d, starts, key_grad, value_grad, result, branch, staged, bias_out, down_sum,
+    local,
     *rest,
 ):
-    scatter_refs, line_refs = rest[:9], rest[9:]
+    in_outs = (in_out0, in_out1, in_out2)
+    scatter_refs, line_refs, total_refs = rest[:9], rest[9:16], rest[16:]
     place = Place(plan)
     own, depth = middle.shape
     rows = qkv_in.shape[0]
@@ -998,11 +1165,12 @@
 
     for number in range(min(2, groups)):
         load_slice(number)
-    place.barrier(line=True)
+    place.barrier(groups=True)
     scatter = Scatter(place, own, depth, *scatter_refs[:5], scatter_refs[5:])
     for target, copy in zip(order, parts):
         copy.wait()
-        line.start(target)
+        line.start(target, False)
+    line.start_near()
     for copy in feeds:
         copy.wait()
     tile = min(1024, depth)
@@ -1018,7 +1186,7 @@
     scatter.begin(partial)
     ticks = list(line.ticks())
     line.tick(ticks.pop(0))
-    starts[...] = segment_starts(bounds, rows)
+    starts[...] = segment_starts(place.batch, lengths, scripts, places, rows)
     bias_out[...] = jnp.zeros_like(bias_out)
     key_grad[...] = jnp.zeros_like(key_grad)
     value_grad[...] = jnp.zeros_like(value_grad)
@@ -1030,6 +1198,12 @@
         if number + 2 < groups:
             load_slice(number + 2)
     stores = [moves.start(staged, out_part_out)]
+    down_rows = down_sum.shape[0]
+    fit = rows // down_rows
+    down_parts = [
+        branch.at[index // fit, pl.ds((index % fit) * down_rows, down_rows), :] for index in range(3)
+    ]
+    down_loads = [moves.start(part, target) for part, target in zip((down0, down1, down2), down_parts)]
     scale = HEAD_DIM ** (-0.5)
     row_in = lax.broadcasted_iota(jnp.int32, (block, block), 0)
     col_in = lax.broadcasted_iota(jnp.int32, (block, block), 1)
@@ -1081,7 +1255,7 @@
         attend(index)
         if index == blocks // 2:
             scatter.middle()
-        if index:
+        if 0 < index < blocks - 1:
             line.tick(ticks.pop(0))
     kept = min(256, rows)
 
@@ -1094,25 +1268,38 @@
 
     loop(rows, kept, write)
     stores.append(moves.start(qkv_in, qkv_grad_out))
+    for number in ticks:
+        line.tick(number)
+    for copy in down_loads:
+        copy.wait()
+    add_parts(place, down_parts, down_sum)
+    stores.append(moves.start(down_sum, down_out))
 
     def close(start, count, value):
         span = pl.ds(start, count)
         result[span, :] = (middle[span, :] + value + down_bias[...]).astype(bf16)
 
-    scatter.end(close)
+    for half in range(plan.halves):
+        scatter.end(close, half)
     stores.append(moves.start(result, block_out))
-    for number in ticks:
-        line.tick(number)
-    line.end(total)
-    stores.append(moves.start(total, in_out))
+    vectors = Total(place, *total_refs[:4], total_refs[4:8])
+    spread = Total(place, *total_refs[8:12], total_refs[12:])
+    vectors.value[...] = sums2[...]
+    spread_rows(place, spread.value, [bias_out[0:1, :], bias_out[1:2, :], in_sums[...]])
+    vectors.plane([spread])
+    vectors_out[...] = vectors.value[...]
+    spread_out[...] = spread.value[...]
+    exported = line.export(in_outs, moves)
     scatter.finish()
     line.finish()
     for copy in stores:
         copy.wait()
+    exported()
 
 
 def run_back(
-    plan, groups, block, bounds, qkv, att, att_grad, sums, activated, w_down, middle, down_bias, in_part, branch_all
+    plan, groups, block, order, qkv, att, att_grad, sums, activated, w_down, middle, down_bias, in_part, branch_all,
+    sums2, in_sums, down_parts,
 ):
     own, depth = middle.shape
     rows, width = att.shape
@@ -1123,12 +1310,16 @@
         out_shape=(
             jax.ShapeDtypeStruct((rows, 3 * width), bf16),
             jax.ShapeDtypeStruct((own, depth), bf16),
-            jax.ShapeDtypeStruct((8, width), f32),
-            jax.ShapeDtypeStruct((cut, hidden), f32),
+            jax.ShapeDtypeStruct((hidden, cut), f32),
+            jax.ShapeDtypeStruct((cut, hidden), bf16),
+            jax.ShapeDtypeStruct((cut, hidden), bf16),
+            jax.ShapeDtypeStruct((cut, hidden), bf16),
             jax.ShapeDtypeStruct((groups, width, cut), bf16),
+            jax.ShapeDtypeStruct(sums2.shape, f32),
+            jax.ShapeDtypeStruct((plan.devices, 2 * width + hidden), f32),
         ),
-        in_specs=[SMEM, ANY, ANY, ANY, VMEM, ANY, ANY, VMEM, VMEM, ANY, ANY],
-        out_specs=(ANY, ANY, VMEM, ANY, ANY),
+        in_specs=[SMEM, SMEM, SMEM, ANY, ANY, ANY, VMEM, ANY, ANY, VMEM, VMEM, ANY, ANY, VMEM, VMEM, ANY, ANY, ANY],
+        out_specs=(ANY, ANY, ANY, ANY, ANY, ANY, ANY, VMEM, VMEM),
         scratch_shapes=[
             pltpu.VMEM((rows, 3 * width), bf16),
             pltpu.VMEM((rows, width), bf16),
@@ -1141,25 +1332,31 @@
             pltpu.VMEM((own, depth), bf16),
             pltpu.VMEM((2, rows, cut), bf16),
             pltpu.VMEM((groups, width, cut), bf16),
-            pltpu.VMEM((cut, hidden), f32),
-            pltpu.SemaphoreType.DMA((40,)),
+            pltpu.VMEM((2, width), f32),
+            pltpu.VMEM((hidden, cut), f32),
+            pltpu.SemaphoreType.DMA((64,)),
         ]
         + Scatter.scratch(plan, own, depth, bf16)
-        + Line.scratch(groups, cut, hidden, PIECES),
+        + Line.scratch(groups, cut, hidden, PIECES)
+        + Total.scratch(plan, 1, sums2.shape)
+        + Total.scratch(plan, 1, (plan.devices, 2 * width + hidden)),
         compiler_params=params(3),
         name="back",
         cost_estimate=cost(75),
-    )(bounds, qkv, att, att_grad, sums, activated, w_down, middle, down_bias, in_part, branch_all)
+    )(*order, qkv, att, att_grad, sums, activated, w_down, middle, down_bias, in_part, branch_all, sums2, in_sums, *down_parts)
 
 
 def last_kernel(
-    plan, qkv_grad, w_qkv, tok, middle_grad, gain, out_part, first_all, sums2, in_sums, qv_sums,
-    input_out, out_out, qkv_out, vectors_out, spread_out,
-    g_in, weights, result, first, out_total, qkv_total, wide, many, wide_in, many_in, local, *rest,
+    plan, qkv_grad, w_qkv, tok, middle_grad, gain, out_part, first_all, qv_sums,
+    in0, in1, in2,
+    input_out, in_out, out_out0, out_out1, out_out2, qkv_out0, qkv_out1, qkv_out2, vectors_out, spread_out,
+    g_in, weights, result, first, in_parts, in_sum, local, *rest,
 ):
+    out_outs = (out_out0, out_out1, out_out2)
+    qkv_outs = (qkv_out0, qkv_out1, qkv_out2)
     scatter_refs, rest = rest[:9], rest[9:]
     out_refs, rest = rest[:7], rest[7:]
-    qkv_refs, (wide_send, wide_recv, many_send, many_recv) = rest[:7], rest[7:]
+    qkv_refs, total_refs = rest[:7], rest[7:]
     place = Place(plan)
     own, depth = tok.shape
     width = w_qkv.shape[2]
@@ -1182,11 +1379,13 @@
 
     for number in range(min(2, groups)):
         load_slice(number)
-    place.barrier(line=True, halves=True)
+    in_loads = [moves.start(part, in_parts.at[index]) for index, part in enumerate((in0, in1, in2))]
+    place.barrier(groups=True)
     scatter = Scatter(place, own, depth, *scatter_refs[:5], scatter_refs[5:])
     for target, copy in zip(order, parts):
         copy.wait()
-        out_line.start(target)
+        out_line.start(target, False)
+    out_line.start_near()
     for copy in loads:
         copy.wait()
     tile = min(1024, depth)
@@ -1202,7 +1401,7 @@
     def qkv_slice(number):
         first_loads[number].wait()
         qkv_line.own[order[number]] = dot(first[number % 2], g_in[...], 0, 0).astype(bf16)
-        qkv_line.start(order[number])
+        qkv_line.start(order[number], False)
         if number + 2 < groups:
             load_slice(number + 2)
 
@@ -1213,6 +1412,7 @@
         if number == 1:
             for index in range(groups // 2, groups):
                 qkv_slice(index)
+            qkv_line.start_near(range(PIECES - 1))
 
     scatter.begin(partial, between)
     for number in out_line.ticks():
@@ -1220,14 +1420,18 @@
     ticks = list(qkv_line.ticks())
     scatter.middle()
     qkv_line.tick(ticks.pop(0))
-    out_line.end(out_total)
-    stores = [moves.start(out_total, out_out)]
-    wide[...] = jnp.zeros_like(wide)
-    wide[2:6, :] = sums2[0:4, :]
-    mine = lax.broadcasted_iota(jnp.int32, (many.shape[0], 1), 0) == place.me
-    many[:, pl.ds(0, width)] = jnp.where(mine, qv_sums[0:1, :], 0.0)
-    many[:, pl.ds(width, width)] = jnp.where(mine, qv_sums[1:2, :], 0.0)
-    many[:, pl.ds(2 * width, in_sums.shape[1])] = jnp.where(mine, in_sums[...], 0.0)
+    exported = [out_line.export(out_outs, moves)]
+    stores = []
+    totals = [
+        Total(place, *total_refs[index : index + 4], total_refs[index + 4 : index + 8]) for index in (0, 8)
+    ]
+    vectors, spread = totals
+    spread.value[...] = qv_sums[...]
+    for copy in in_loads:
+        copy.wait()
+    add_parts(place, [in_parts.at[index] for index in range(3)], in_sum)
+    stores.append(moves.start(in_sum, in_out))
+    vectors.value[...] = jnp.zeros_like(vectors.value)
     qkv_line.tick(ticks.pop(0))
 
     def close(start, count, value):
@@ -1235,112 +1439,68 @@
         unit, inverse = norm_rows(tok[span, :].astype(f32))
         sum_rows = middle_grad[span, :] + norm_back(value, unit, inverse, gain[...])
         result[span, :] = sum_rows.astype(bf16)
-        wide[0:1, :] += jnp.sum(value * unit, axis=0, keepdims=True)
-        wide[1:2, :] += jnp.sum(value, axis=0, keepdims=True)
-
-    scatter.end(close)
+        vectors.value[0:1, :] += jnp.sum(value * unit, axis=0, keepdims=True)
+        vectors.value[1:2, :] += jnp.sum(value, axis=0, keepdims=True)
+
+    for half in range(plan.halves):
+        scatter.end(close, half)
     stores.append(moves.start(result, input_out))
     qkv_line.tick(ticks.pop(0))
-    partners = [place.at(mask) for mask in [1] + plan.bits]
-    partners += [place.across(bit) for bit in place.group_bits()]
-    for index, partner in enumerate(partners):
-        copies = [
-            pltpu.make_async_remote_copy(
-                src_ref=source.at[index],
-                dst_ref=target.at[index],
-                send_sem=send.at[index],
-                recv_sem=recv.at[index],
-                device_id=partner,
-                device_id_type=MESH,
-            )
-            for source, target, send, recv in (
-                (wide_in[0], wide_in[1], wide_send, wide_recv),
-                (many_in[0], many_in[1], many_send, many_recv),
-            )
-        ]
-        wide_in[0][index] = wide[...]
-        many_in[0][index] = many[...]
-        for copy in copies:
-            copy.start()
-        for copy in copies:
-            copy.wait_recv()
-        wide[...] = wide_in[0][index] + wide_in[1][index]
-        many[...] = many_in[0][index] + many_in[1][index]
-        for copy in copies:
-            copy.wait_send()
-    vectors_out[...] = wide[...]
-    spread_out[...] = many[...]
+    vectors.plane()
+    for total in totals:
+        total.begin()
+    qkv_line.start_near([PIECES - 1])
     for number in ticks:
         qkv_line.tick(number)
-    qkv_line.end(qkv_total)
-    for part in range(3):
-        stores.append(moves.start(qkv_total.at[:, pl.ds(part * width, width)], qkv_out.at[part]))
+    exported.append(qkv_line.export(qkv_outs, moves, width))
     scatter.finish()
     out_line.finish()
     qkv_line.finish()
+    for total, result_out in zip(totals, (vectors_out, spread_out)):
+        total.end(result_out)
     for copy in stores:
         copy.wait()
-
-
-def run_last(plan, groups, qkv_grad, w_qkv, tok, middle_grad, gain, out_part, first_all, sums2, in_sums, qv_sums):
+    for wait in exported:
+        wait()
+
+
+def run_last(plan, groups, qkv_grad, w_qkv, tok, middle_grad, gain, out_part, first_all, qv_sums, in_parts):
     own, depth = tok.shape
     rows = qkv_grad.shape[0]
     width = w_qkv.shape[2]
     cut = depth // groups
-    many = (plan.devices, 2 * width + in_sums.shape[1])
-    rounds = (plan.devices.bit_length() - 1) + (groups.bit_length() - 1)
-
-    def kernel(*refs):
-        head, tail = refs[: 10 + 5 + 8], refs[10 + 5 + 8 :]
-        last_kernel(plan, *head, (tail[0], tail[1]), (tail[2], tail[3]), *tail[4:])
-
     return pl.pallas_call(
-        kernel,
+        functools.partial(last_kernel, plan),
         out_shape=(
             jax.ShapeDtypeStruct((own, depth), bf16),
-            jax.ShapeDtypeStruct((width, cut), f32),
-            jax.ShapeDtypeStruct((3, cut, width), f32),
-            jax.ShapeDtypeStruct((8, depth), f32),
-            jax.ShapeDtypeStruct(many, f32),
+            jax.ShapeDtypeStruct(in_parts[0].shape, f32),
+        )
+        + (jax.ShapeDtypeStruct((width, cut), bf16),) * 3
+        + (jax.ShapeDtypeStruct((3, cut, width), bf16),) * 3
+        + (
+            jax.ShapeDtypeStruct((2, depth), f32),
+            jax.ShapeDtypeStruct((plan.devices, 2 * width), f32),
         ),
-        in_specs=[ANY, ANY, VMEM, VMEM, VMEM, ANY, ANY, VMEM, VMEM, VMEM],
-        out_specs=(ANY, ANY, ANY, VMEM, VMEM),
+        in_specs=[ANY, ANY, VMEM, VMEM, VMEM, ANY, ANY, VMEM, ANY, ANY, ANY],
+        out_specs=(ANY,) * 8 + (VMEM,) * 2,
         scratch_shapes=[
             pltpu.VMEM((rows, 3 * width), bf16),
             pltpu.VMEM((depth, 3 * width), bf16),
             pltpu.VMEM((own, depth), bf16),
             pltpu.VMEM((2, rows, cut), bf16),
-            pltpu.VMEM((width, cut), f32),
-            pltpu.VMEM((cut, 3 * width), f32),
-            pltpu.VMEM((8, depth), f32),
-            pltpu.VMEM(many, f32),
-            pltpu.VMEM((rounds, 8, depth), f32),
-            pltpu.VMEM((rounds, 8, depth), f32),
-            pltpu.VMEM((rounds,) + many, f32),
-            pltpu.VMEM((rounds,) + many, f32),
-            pltpu.SemaphoreType.DMA((40,)),
+            pltpu.VMEM((3,) + in_parts[0].shape, bf16),
+            pltpu.VMEM(in_parts[0].shape, f32),
+            pltpu.SemaphoreType.DMA((64,)),
         ]
         + Scatter.scratch(plan, own, depth, bf16)
         + Line.scratch(groups, width, cut, 1)
         + Line.scratch(groups, cut, 3 * width, PIECES)
-        + [pltpu.SemaphoreType.DMA((rounds,))] * 4,
+        + Total.scratch(plan, groups, (2, depth))
+        + Total.scratch(plan, groups, (plan.devices, 2 * width)),
         compiler_params=params(4),
         name="last",
         cost_estimate=cost(75),
-    )(qkv_grad, w_qkv, tok, middle_grad, gain, out_part, first_all, sums2, in_sums, qv_sums)
-
-
-def segment_bounds(group, seq_lengths, seq_scripts, seq_place):
-    count = seq_lengths.shape[0]
-    numbers = jnp.arange(count, dtype=jnp.int32)
-    order_key = seq_scripts * count + numbers
-    same = seq_place[:, None] == seq_place[None, :]
-    before = order_key[None, :] < order_key[:, None]
-    offsets = jnp.sum(jnp.where(same & before, seq_lengths[None, :], 0), axis=1)
-    mine = seq_place == group
-    firsts = jnp.where(mine, offsets, 0)
-    total = jnp.sum(jnp.where(mine, seq_lengths, 0))
-    return jnp.concatenate([firsts, total[None]]).astype(jnp.int32)
+    )(qkv_grad, w_qkv, tok, middle_grad, gain, out_part, first_all, qv_sums, *in_parts)
 
 
 def body(
@@ -1365,51 +1525,59 @@
     own, depth = tokens.shape
     devices = lax.axis_size("mp")
     plan = Plan(devices)
+    fine = Plan(devices, 2)
     rows = own * devices
     width = w_qkv.shape[2]
     block = min(512, rows)
-    bounds = segment_bounds(lax.axis_index("batch"), seq_lengths, seq_scripts, seq_place)
+    order = (seq_lengths, seq_scripts, seq_place)
 
     def line(vector):
         return vector.reshape(1, -1)
 
-    bias3 = jnp.concatenate([qv_bias[0], jnp.zeros_like(qv_bias[0]), qv_bias[1]])
     first_all, qkv, att, sums, grad_all = run_first(
-        plan, block, tokens, line(norm1_gain), line(norm1_shift), w_qkv, line(bias3), bounds, out_grad
+        plan, block, tokens, line(norm1_gain), line(norm1_shift), w_qkv, qv_bias, order, out_grad
     )
     second_all, activated, hidden_grad, middle, in_part = run_feed(
-        plan, tokens, att, w_out, line(out_bias), line(norm2_gain), line(norm2_shift), w_in, line(in_bias),
+        fine, tokens, att, w_out, line(out_bias), line(norm2_gain), line(norm2_shift), w_in, line(in_bias),
         w_down, grad_all,
     )
 
     groups = lax.axis_size("batch")
-    middle_grad, branch_all, att_grad, sums2, down_weight_grad, in_part2 = run_middle(
-        plan, groups, hidden_grad, w_in, middle, out_grad, line(norm2_gain), w_out, activated, grad_all, second_all
+    batch = lax.axis_index("batch")
+
+    def added(parts):
+        total = parts[0].astype(f32)
+        total += jnp.where(batch > 0, parts[1].astype(f32), 0.0)
+        return total + jnp.where(batch < groups - 1, parts[2].astype(f32), 0.0)
+
+    middle_grad, branch_all, att_grad, sums2, in_sums, *down_parts, in_part2 = run_middle(
+        fine, groups, hidden_grad, w_in, middle, out_grad, line(norm2_gain), w_out, activated, grad_all, second_all,
+        in_part,
     )
-    qkv_grad, block_out, qv_part, in_weight_grad, out_part = run_back(
-        plan, groups, block, bounds, qkv, att, att_grad, sums, activated, w_down, middle, line(down_bias),
-        in_part2, branch_all,
+    qkv_grad, block_out, down_weight_grad, *in_parts, out_part, vectors2, spread2 = run_back(
+        plan, groups, block, order, qkv, att, att_grad, sums, activated, w_down, middle, line(down_bias),
+        in_part2, branch_all, sums2, in_sums, down_parts,
     )
-    input_grad, out_weight_grad, qkv_weight_grad, vectors, spread = run_last(
-        plan, groups, qkv_grad, w_qkv, tokens, middle_grad, line(norm1_gain), out_part, first_all, sums2, in_part,
-        qv_part,
+    input_grad, in_weight_grad, *weight_parts, vectors, spread = run_last(
+        plan, groups, qkv_grad, w_qkv, tokens, middle_grad, line(norm1_gain), out_part, first_all,
+        spread2[:, : 2 * width], in_parts,
     )
-    qv_bias_grad = jnp.stack([spread[:, :width].reshape(-1), spread[:, width : 2 * width].reshape(-1)])
+    qv_bias_grad = jnp.stack([spread[:, :width].reshape(-1), spread[:, width:].reshape(-1)])
     return (
         block_out,
         input_grad,
         vectors[0],
         vectors[1],
-        qkv_weight_grad,
+        added(weight_parts[3:]),
         qv_bias_grad,
-        out_weight_grad,
-        vectors[4],
-        vectors[2],
-        vectors[3],
+        added(weight_parts[:3]),
+        vectors2[2],
+        vectors2[0],
+        vectors2[1],
         in_weight_grad,
-        spread[:, 2 * width :].reshape(-1),
+        spread2[:, 2 * width :].reshape(-1),
         down_weight_grad,
-        vectors[5],
+        vectors2[3],
     )
 
 

time: 485 us -> 449 us (0.926)
  Pallas kernels: 457 us -> 424 us
    pallas_call x1, Pallas kernels: 95 us -> 82.8 us  [run_last(): pl.pallas_call(functools.partial(last_kernel, plan), out_shape=(jax.Shape...]
    pallas_call x1, Pallas kernels: 102 us -> 94.5 us  [run_middle(): pl.pallas_call(functools.partial(middle_kernel, plan), out_shape=(jax.Sha...]
    pallas_call x1, Pallas kernels: 83.3 us -> 77.4 us  [run_first(): pl.pallas_call(functools.partial(first_kernel, plan, block), out_shape=(j...]
    unnamed x21 -> x23, local copies, waits for them, and re-layouts: 10.3 us -> 7.07 us
where the time goes in v3:
time: 449 us; the launch traced here: 440 us
  Pallas kernels  424 us (94%)
  local copies, waits for them, and re-layouts  9.64 us (2%)
  other arithmetic  5.85 us (1%)
    pallas_call x1, Pallas kernels, run_middle(): pl.pallas_call(functools.partial(middle_kernel, plan), out_shape=(jax.Sha...  94.5 us
    pallas_call x1, Pallas kernels, run_feed(): pl.pallas_call(functools.partial(feed_kernel, plan), out_shape=(jax.Shape...  88.6 us
    pallas_call x1, Pallas kernels, run_last(): pl.pallas_call(functools.partial(last_kernel, plan), out_shape=(jax.Shape...  82.8 us
    pallas_call x1, Pallas kernels, run_back(): pl.pallas_call(functools.partial(back_kernel, plan, block), out_shape=(ja...  80.2 us
    pallas_call x1, Pallas kernels, run_first(): pl.pallas_call(functools.partial(first_kernel, plan, block), out_shape=(j...  77.4 us

profile of v3, /device:TPU:8, one launch (start us, length us, event | category | flops | bytes accessed | tf_op | source)
XLA Modules:
  0.0 439.9 jit_solution(13018004516598284281)
XLA Ops:
  0.6 77.4 %first.1 = (bf16[2048,2048]{1,0:T(8,128)(2,1)}, bf16[2048,768]{1,0:T(8,128)(2,1)}, bf16[2048,256]{1,0:T(8,128)(2,1)}, f32[8,2048]{1,0:T(8,128)}, bf16[2048,2048]{1,0:T(8,128)(2,1)}) custom-call(bf16[256,2048]{1,0:T(8,128)(2,1)} %tok.5, f32[1,2048]{1,0:T(1,128)} %bitcast.41, f32[1,2048]{1,0:T(1,128)} %bitcast.35, bf16[3,2048,256]{2,1,0:T(8,128)(2,1)} %w_qkv.3, ...), custom_call_target="tpu_custom_call" | custom-call | flops 80000000000 | bytes 10000000 | tf_op jit(solution)/shard_map/first/pallas_call | solution.py:723
  78.1 88.6 %feed.1 = (bf16[2048,2048]{1,0:T(8,128)(2,1)}, bf16[2048,1024]{1,0:T(8,128)(2,1)}, bf16[2048,1024]{1,0:T(8,128)(2,1)}, f32[256,2048]{1,0:T(8,128)}, f32[1,1024]{1,0:T(1,128)}) custom-call(bf16[256,2048]{1,0:T(8,128)(2,1)} %tok.5, bf16[2048,256]{1,0:T(8,128)(2,1)} %get-tuple-element.53.att, bf16[256,2048]{1,0:T(8,128)(2,1)} %w_out.3, f32[1,2048]{1,0:T(1,128)} %bitcast.36, ...), custom_call_target="tpu_custom_call" | custom-call | flops 89999998976 | bytes 10000000 | tf_op jit(solution)/shard_map/feed/pallas_call | solution.py:874
  166.7 94.5 %middle.1 = (f32[256,2048]{1,0:T(8,128)}, bf16[2048,2048]{1,0:T(8,128)(2,1)}, bf16[2048,256]{1,0:T(8,128)(2,1)}, f32[4,2048]{1,0:T(4,128)}, f32[1,1024]{1,0:T(1,...) custom-call(bf16[2048,1024]{1,0:T(8,128)(2,1)} %get-tuple-element.55, ...), custom_call_target="tpu_custom_call" | custom-call | flops 80000000000 | bytes 10000000 | tf_op jit(solution)/shard_map/middle/pallas_call | solution.py:1103
  261.2 80.2 %back.1 = (bf16[2048,768]{1,0:T(8,128)(2,1)}, bf16[256,2048]{1,0:T(8,128)(2,1)}, f32[1024,512]{1,0:T(8,128)}, bf16[512,1024]{1,0:T(8,128)(2,1)}, bf16[512,1024]{...) custom-call(s32[8]{0:T(128)} %lengths.3, ...), custom_call_target="tpu_custom_call" | custom-call | flops 74999996416 | bytes 10000000 | tf_op jit(solution)/shard_map/back/pallas_call | solution.py:1308
  341.5 1.3 slice.30.qv_sums
  342.8 82.8 %last.1 = (bf16[256,2048]{1,0:T(8,128)(2,1)}, f32[512,1024]{1,0:T(8,128)}, bf16[256,512]{1,0:T(8,128)(2,1)}, bf16[256,512]{1,0:T(8,128)(2,1)}, bf16[256,512]{1,0...) custom-call(bf16[2048,768]{1,0:T(8,128)(2,1)} %get-tuple-element.70., ...), custom_call_target="tpu_custom_call" | custom-call | flops 74999996416 | bytes 10000000 | tf_op jit(solution)/shard_map/last/pallas_call | solution.py:1472
  425.6 2.0 select_add_fusion.1
  427.6 0.0 copy-start.6
  427.6 0.0 copy-start.4
  427.6 0.7 slice_bitcast_fusion.2
  428.3 0.0 copy-start.5
  428.4 0.6 pad_maximum_fusion
  429.0 0.0 copy-start.2
  429.0 3.2 select_add_fusion
  432.2 0.0 copy-start.3
  432.2 0.0 copy-done.6
  432.2 0.6 fusion.1
  432.8 0.0 copy-done.4
  432.8 0.6 copy.35
  433.4 0.0 copy-done.5
  433.4 0.6 fusion
  434.1 0.0 copy-done.2
  434.1 0.0 copy-start.1
  434.1 1.0 copy.40
  435.0 0.0 copy-done.3
  435.0 1.0 copy.41
  436.0 0.1 copy-done.1
  436.1 0.0 copy-start
  436.1 1.3 copy.42
  437.4 1.0 copy-done
  438.4 1.3 copy.43
  (3 shorter events, 0.0 us)
Async XLA Ops:
  427.6 4.6 %copy-start.6 = (f32[2,2048]{1,0:T(2,128)S(1)}, f32[2,2048]{1,0:T(2,128)}, u32[]{:S(2)}) copy-start(f32[2,2048]{1,0:T(2,128)} %get-tuple-element.79) | copy-start | bytes 49156
  427.6 5.2 %copy-start.4 = (f32[8,1536]{1,0:T(8,128)S(1)}, f32[8,1536]{1,0:T(8,128)}, u32[]{:S(2)}) copy-start(f32[8,1536]{1,0:T(8,128)} %get-tuple-element.74) | copy-start | bytes 147460
  428.3 5.1 %copy-start.5 = (f32[4,2048]{1,0:T(4,128)S(1)}, f32[4,2048]{1,0:T(4,128)}, u32[]{:S(2)}) copy-start(f32[4,2048]{1,0:T(4,128)} %get-tuple-element.87) | copy-start | bytes 98308
  429.0 5.1 %copy-start.2 = (bf16[256,2048]{1,0:T(8,128)(2,1)S(1)}, bf16[256,2048]{1,0:T(8,128)(2,1)}, u32[]{:S(2)}) copy-start(bf16[256,2048]{1,0:T(8,128)(2,1)} %get-tuple-element.112) | copy-start | bytes 3145732
  432.2 2.9 copy-start.3
  434.1 2.0 copy-start.1
  436.1 2.3 copy-start

commit v4 on v3

--- a/solution.py
+++ b/solution.py
@@ -585,28 +585,52 @@
     return pl.ds(part * width + head * HEAD_DIM, HEAD_DIM)
 
 
-def first_kernel(
-    plan, block, tok, gain, shift, w_qkv, qv_bias, lengths, scripts, places, out_grad, first_out, qkv_out, att_out,
-    sum_out, grad_out, buf, weights, qkv, starts, sums, attended, local, *sems,
+def params(number):
+    return pltpu.CompilerParams(
+        collective_id=number, has_side_effects=True, vmem_limit_bytes=62 * 2**20
+    )
+
+
+def cost(micros):
+    return pl.CostEstimate(flops=micros * 10**9, bytes_accessed=10**7, transcendentals=0)
+
+
+def joined(ref, pieces):
+    return jnp.concatenate([ref[piece, :] for piece in pieces], axis=0)
+
+
+def front_kernel(
+    plan, fine, block, tok, gain1, shift1, w_qkv, qv_bias, lengths, scripts, places, out_grad,
+    w_out, out_bias, gain, shift, w_in, in_bias, w_down,
+    first_out, qkv_out, att_out, sum_out, grad_out, second_out, act_out, hidden_out, middle_out, bias_out,
+    starts, sums, attended, w_o, w_i, w_d, grad_in, up, buf, act, back, middle, local, *rest,
 ):
+    first_sems, grad_sems, gather_sems, scatter_refs = rest[:4], rest[4:8], rest[8:12], rest[12:]
     place = Place(plan)
     own, depth = tok.shape
     rows = buf.shape[0]
     width = w_qkv.shape[2]
+    hidden_width = w_in.shape[1]
+    chip_rows = 2 * own
     moves = Moves(local)
+    qkv = act.at[:, pl.ds(0, 3 * width)]
+    weights = back.at[pl.ds(0, depth), pl.ds(0, 3 * width)]
     loads = [
-        moves.start(w_qkv.at[part], weights.at[:, pl.ds(part * width, width)]) for part in range(3)
+        moves.start(w_qkv.at[part], back.at[pl.ds(0, depth), pl.ds(part * width, width)]) for part in range(3)
     ]
+    load_out = moves.start(w_out, w_o)
+    load_down = moves.start(w_down, w_d)
+    load_in = moves.start(w_in, w_i)
     place.barrier()
     step = min(32, own)
     mine = pl.multiple_of(place.me * own, own)
 
     def normalise(start):
         unit, _ = norm_rows(tok[pl.ds(start, step), :].astype(f32))
-        buf[pl.ds(pl.multiple_of(mine + start, step), step), :] = (unit * gain[...] + shift[...]).astype(bf16)
+        buf[pl.ds(pl.multiple_of(mine + start, step), step), :] = (unit * gain1[...] + shift1[...]).astype(bf16)
 
     loop(own, step, normalise)
-    gather = Gather(place, buf, None, own, sems[:4])
+    gather = Gather(place, buf, None, own, first_sems)
     gather.start()
     stores = [moves.start(out_grad, grad_out.at[pl.ds(mine, own), :])]
     starts[...] = segment_starts(place.batch, lengths, scripts, places, rows)
@@ -615,7 +639,7 @@
 
     def project(offset):
         chip = lax.div(flip(place.me, offset), 2)
-        span = pl.ds(pl.multiple_of(chip * 2 * own, 2 * own), 2 * own)
+        span = pl.ds(pl.multiple_of(chip * chip_rows, chip_rows), chip_rows)
         stores.append(moves.start(buf.at[span, :], first_out.at[span, :]))
         product = dot(buf[span, :], weights[...], 1, 0)
         qkv[span, 0:width] = (product[:, 0:width] + qv_bias[0:1, :]).astype(bf16)
@@ -625,7 +649,7 @@
     gather.share(0)
     project(0)
     steps = gather.steps()
-    grads = Gather(place, grad_out, out_grad, own, sems[4:])
+    grads = Gather(place, grad_out, out_grad, own, grad_sems)
     for number, (half, keys, offsets) in enumerate(steps):
         for key in keys:
             gather.arrive(key)
@@ -635,7 +659,6 @@
             gather.share(offset)
             project(offset)
     gather.finish()
-    gather = grads
     stores.append(moves.start(qkv, qkv_out))
 
     scale = HEAD_DIM ** (-0.5) * LOG2E
@@ -685,130 +708,64 @@
             sums[pl.ds(head, 1), span] = top + jnp.log2(total)
 
     blocks = rows // block
-    taken = 0
+    waiting = [key for _, keys, _ in steps for key in keys]
     for index in range(blocks):
         attend(index)
-        if index >= blocks - 2 and taken < len(steps):
-            for key in steps[taken][1]:
-                gather.arrive(key)
-            taken += 1
-    stores.append(moves.start(attended, att_out))
-    stores.append(moves.start(sums, sum_out))
-    while taken < len(steps):
-        for key in steps[taken][1]:
-            gather.arrive(key)
-        taken += 1
-    for offset in plan.offsets:
-        gather.share(offset)
-    gather.finish()
+        if index == blocks - 2:
+            while waiting and plan.later(*waiting[0]) and bin(waiting[0][1]).count("1") == 1:
+                grads.arrive(waiting.pop(0))
     for copy in stores:
         copy.wait()
-
-
-def params(number):
-    return pltpu.CompilerParams(
-        collective_id=number, has_side_effects=True, vmem_limit_bytes=62 * 2**20
-    )
-
-
-def cost(micros):
-    return pl.CostEstimate(flops=micros * 10**9, bytes_accessed=10**7, transcendentals=0)
-
-
-def run_first(plan, block, tok, gain, shift, w_qkv, qv_bias, order, out_grad):
-    own, depth = tok.shape
-    rows = own * plan.devices
-    width = w_qkv.shape[2]
-    heads = width // HEAD_DIM
-    return pl.pallas_call(
-        functools.partial(first_kernel, plan, block),
-        out_shape=(
-            jax.ShapeDtypeStruct((rows, depth), bf16),
-            jax.ShapeDtypeStruct((rows, 3 * width), bf16),
-            jax.ShapeDtypeStruct((rows, width), bf16),
-            jax.ShapeDtypeStruct((8, rows), f32),
-            jax.ShapeDtypeStruct((rows, depth), bf16),
-        ),
-        in_specs=[VMEM, VMEM, VMEM, ANY, VMEM, SMEM, SMEM, SMEM, ANY],
-        out_specs=(ANY,) * 5,
-        scratch_shapes=[
-            pltpu.VMEM((rows, depth), bf16),
-            pltpu.VMEM((depth, 3 * width), bf16),
-            pltpu.VMEM((rows, 3 * width), bf16),
-            pltpu.VMEM((1, rows), jnp.int32),
-            pltpu.VMEM((8, rows), f32),
-            pltpu.VMEM((rows, width), bf16),
-            pltpu.SemaphoreType.DMA((16,)),
-        ]
-        + Gather.semaphores(plan) * 2,
-        compiler_params=params(0),
-        name="first",
-        cost_estimate=cost(80),
-    )(tok, gain, shift, w_qkv, qv_bias, *order, out_grad)
-
-
-def joined(ref, pieces):
-    return jnp.concatenate([ref[piece, :] for piece in pieces], axis=0)
-
-
-def feed_kernel(
-    plan, tok, att, w_out, out_bias, gain, shift, w_in, in_bias, w_down, grad_all,
-    second_out, act_out, hidden_out, middle_out, bias_out,
-    att_in, w_o, w_i, w_d, grad_in, up, buf, act, back, middle, local, *rest,
-):
-    scatter_refs, gather_sems = rest[:9], rest[9:]
-    place = Place(plan)
-    own, depth = tok.shape
-    rows = buf.shape[0]
-    hidden_width = w_in.shape[1]
-    chip_rows = 2 * own
-    moves = Moves(local)
-    load_att = moves.start(att, att_in)
-    load_out = moves.start(w_out, w_o)
-    load_down = moves.start(w_down, w_d)
-    grad_loads = {}
-
-    def load_grad(number):
-        lines = pl.ds(number * chip_rows, chip_rows)
-        grad_loads[number] = moves.start(grad_all.at[lines, :], grad_in.at[number % 2])
-
-    load_grad(0)
-    load_grad(1)
-    load_in = moves.start(w_in, w_i)
-    place.barrier()
+    stores = [moves.start(attended, att_out), moves.start(sums, sum_out)]
+
+    place = Place(fine)
     scatter = Scatter(place, own, depth, *scatter_refs[:5], scatter_refs[5:])
-    load_att.wait()
     load_out.wait()
     tile = min(1024, depth)
 
     def partial(owner, target):
-        lines = att_in[pl.ds(pl.multiple_of(owner * own, own), own), :]
+        lines = attended[pl.ds(pl.multiple_of(owner * own, own), own), :]
 
         def columns(start):
             target[:, pl.ds(start, tile)] = dot(lines, w_o[:, pl.ds(start, tile)], 1, 0).astype(target.dtype)
 
         loop(depth, tile, columns)
 
+    grad_loads = {}
+
+    def load_grad(number):
+        lines = pl.ds(number * own, own)
+        grad_loads[number] = moves.start(grad_out.at[lines, :], grad_in.at[number % 2])
+
+    def between(number):
+        if number == max(len(plan.offsets) - 2, 0):
+            for key in waiting:
+                grads.arrive(key)
+            for offset in plan.offsets:
+                grads.share(offset)
+            load_grad(0)
+            load_grad(1)
+
     part_cols = min(512, hidden_width)
-    chips = rows // chip_rows
+    chips = rows // own
 
     def raise_grad(number):
         grad_loads[number].wait()
 
         def columns(start):
             cols = pl.ds(start, part_cols)
-            up[pl.ds(number * chip_rows, chip_rows), cols] = dot(grad_in[number % 2], w_d[cols, :], 1, 1)
+            up[pl.ds(number * own, own), cols] = dot(grad_in[number % 2], w_d[cols, :], 1, 1)
 
         loop(hidden_width, part_cols, columns)
         if number + 2 < chips:
             load_grad(number + 2)
 
-    scatter.begin(partial)
-    scatter.middle()
+    scatter.begin(partial, between)
     load_down.wait()
     for number in range(chips):
         raise_grad(number)
-    mine = pl.multiple_of(place.me * own, own)
+    scatter.middle()
+    grads.finish()
 
     def close(start, count, value):
         span = pl.ds(start, count)
@@ -818,17 +775,17 @@
         buf[pl.ds(pl.multiple_of(mine + start, count), count), :] = (unit * gain[...] + shift[...]).astype(bf16)
 
     gather = Gather(place, buf, None, own, gather_sems)
-    for half in range(plan.halves):
+    for half in range(fine.halves):
         scatter.end(close, half)
         gather.start(half)
     scatter.finish()
-    stores = [moves.start(middle, middle_out)]
+    stores.append(moves.start(middle, middle_out))
     load_in.wait()
     bias_out[...] = jnp.zeros_like(bias_out)
 
     def expand(offset, half):
         pieces = gather.pieces(offset, half)
-        count = own // plan.halves
+        count = own // fine.halves
 
         def columns(start):
             cols = pl.ds(start, part_cols)
@@ -852,7 +809,7 @@
             stores.append(moves.start(act.at[piece, :], act_out.at[piece, :]))
             stores.append(moves.start(back.at[piece, :], hidden_out.at[piece, :]))
 
-    for half in range(plan.halves):
+    for half in range(fine.halves):
         gather.share(0, half)
         expand(0, half)
     for half, keys, offsets in gather.steps():
@@ -866,41 +823,52 @@
         copy.wait()
 
 
-def run_feed(plan, tok, att, w_out, out_bias, gain, shift, w_in, in_bias, w_down, grad_all):
+def run_front(
+    plan, fine, block, tok, gain1, shift1, w_qkv, qv_bias, order, out_grad, w_out, out_bias, gain, shift, w_in, in_bias,
+    w_down,
+):
     own, depth = tok.shape
     rows = own * plan.devices
-    width = att.shape[1]
+    width = w_qkv.shape[2]
     hidden = w_in.shape[1]
     return pl.pallas_call(
-        functools.partial(feed_kernel, plan),
+        functools.partial(front_kernel, plan, fine, block),
         out_shape=(
+            jax.ShapeDtypeStruct((rows, depth), bf16),
+            jax.ShapeDtypeStruct((rows, 3 * width), bf16),
+            jax.ShapeDtypeStruct((rows, width), bf16),
+            jax.ShapeDtypeStruct((8, rows), f32),
+            jax.ShapeDtypeStruct((rows, depth), bf16),
             jax.ShapeDtypeStruct((rows, depth), bf16),
             jax.ShapeDtypeStruct((rows, hidden), bf16),
             jax.ShapeDtypeStruct((rows, hidden), bf16),
             jax.ShapeDtypeStruct((own, depth), f32),
             jax.ShapeDtypeStruct((1, hidden), f32),
         ),
-        in_specs=[VMEM, ANY, ANY, VMEM, VMEM, VMEM, ANY, VMEM, ANY, ANY],
-        out_specs=(ANY, ANY, ANY, ANY, VMEM),
+        in_specs=[VMEM, VMEM, VMEM, ANY, VMEM, SMEM, SMEM, SMEM, ANY, ANY, VMEM, VMEM, VMEM, ANY, VMEM, ANY],
+        out_specs=(ANY,) * 9 + (VMEM,),
         scratch_shapes=[
+            pltpu.VMEM((1, rows), jnp.int32),
+            pltpu.VMEM((8, rows), f32),
             pltpu.VMEM((rows, width), bf16),
             pltpu.VMEM((width, depth), bf16),
             pltpu.VMEM((depth, hidden), bf16),
             pltpu.VMEM((hidden, depth), bf16),
-            pltpu.VMEM((2, 2 * own, depth), bf16),
+            pltpu.VMEM((2, own, depth), bf16),
             pltpu.VMEM((rows, hidden), f32),
             pltpu.VMEM((rows, depth), bf16),
             pltpu.VMEM((rows, hidden), bf16),
-            pltpu.VMEM((rows, hidden), bf16),
+            pltpu.VMEM((max(rows, depth), hidden), bf16),
             pltpu.VMEM((own, depth), f32),
-            pltpu.SemaphoreType.DMA((128,)),
+            pltpu.SemaphoreType.DMA((160,)),
         ]
-        + Scatter.scratch(plan, own, depth, bf16)
-        + Gather.semaphores(plan),
-        compiler_params=params(1),
-        name="feed",
-        cost_estimate=cost(90),
-    )(tok, att, w_out, out_bias, gain, shift, w_in, in_bias, w_down, grad_all)
+        + Gather.semaphores(plan) * 2
+        + Gather.semaphores(fine)
+        + Scatter.scratch(fine, own, depth, bf16),
+        compiler_params=params(0),
+        name="front",
+        cost_estimate=cost(150),
+    )(tok, gain1, shift1, w_qkv, qv_bias, *order, out_grad, w_out, out_bias, gain, shift, w_in, in_bias, w_down)
 
 
 PIECES = 2
@@ -1426,7 +1394,7 @@
         Total(place, *total_refs[index : index + 4], total_refs[index + 4 : index + 8]) for index in (0, 8)
     ]
     vectors, spread = totals
-    spread.value[...] = qv_sums[...]
+    spread.value[...] = qv_sums[:, 0 : 2 * width]
     for copy in in_loads:
         copy.wait()
     add_parts(place, [in_parts.at[index] for index in range(3)], in_sum)
@@ -1534,14 +1502,12 @@
     def line(vector):
         return vector.reshape(1, -1)
 
-    first_all, qkv, att, sums, grad_all = run_first(
-        plan, block, tokens, line(norm1_gain), line(norm1_shift), w_qkv, qv_bias, order, out_grad
+    (
+        first_all, qkv, att, sums, grad_all, second_all, activated, hidden_grad, middle, in_part,
+    ) = run_front(
+        plan, fine, block, tokens, line(norm1_gain), line(norm1_shift), w_qkv, qv_bias, order, out_grad,
+        w_out, line(out_bias), line(norm2_gain), line(norm2_shift), w_in, line(in_bias), w_down,
     )
-    second_all, activated, hidden_grad, middle, in_part = run_feed(
-        fine, tokens, att, w_out, line(out_bias), line(norm2_gain), line(norm2_shift), w_in, line(in_bias),
-        w_down, grad_all,
-    )
-
     groups = lax.axis_size("batch")
     batch = lax.axis_index("batch")
 
@@ -1560,7 +1526,7 @@
     )
     input_grad, in_weight_grad, *weight_parts, vectors, spread = run_last(
         plan, groups, qkv_grad, w_qkv, tokens, middle_grad, line(norm1_gain), out_part, first_all,
-        spread2[:, : 2 * width], in_parts,
+        spread2, in_parts,
     )
     qv_bias_grad = jnp.stack([spread[:, :width].reshape(-1), spread[:, width:].reshape(-1)])
     return (

time: 449 us -> 437 us (0.973)
  Pallas kernels: 424 us -> 414 us
    pallas_call x2 -> x1, Pallas kernels: 166 us -> 155 us  [run_front(): pl.pallas_call(functools.partial(front_kernel, plan, fine, block), out_sh...]
where the time goes in v4:
time: 437 us; the launch traced here: 429 us
  Pallas kernels  414 us (95%)
  local copies, waits for them, and re-layouts  8.31 us (2%)
  other arithmetic  5.85 us (1%)
    pallas_call x1, Pallas kernels, run_front(): pl.pallas_call(functools.partial(front_kernel, plan, fine, block), out_sh...  155 us
    pallas_call x1, Pallas kernels, run_middle(): pl.pallas_call(functools.partial(middle_kernel, plan), out_shape=(jax.Sha...  94.2 us
    pallas_call x1, Pallas kernels, run_last(): pl.pallas_call(functools.partial(last_kernel, plan), out_shape=(jax.Shape...  83.8 us
    pallas_call x1, Pallas kernels, run_back(): pl.pallas_call(functools.partial(back_kernel, plan, block), out_shape=(ja...  80.8 us

profile of v4, /device:TPU:8, one launch (start us, length us, event | category | flops | bytes accessed | tf_op | source)
XLA Modules:
  0.0 428.6 jit_solution(17301826954392495777)
XLA Ops:
  0.6 154.7 %front.1 = (bf16[2048,2048]{1,0:T(8,128)(2,1)}, bf16[2048,768]{1,0:T(8,128)(2,1)}, bf16[2048,256]{1,0:T(8,128)(2,1)}, f32[8,2048]{1,0:T(8,128)}, bf16[2048,2048]...) custom-call(bf16[256,2048]{1,0:T(8,128)(2,1)} %tok.3, ...), custom_call_target="tpu_custom_call" | custom-call | flops 149999992832 | bytes 10000000 | tf_op jit(solution)/shard_map/front/pallas_call | solution.py:834
  155.4 94.2 %middle.1 = (f32[256,2048]{1,0:T(8,128)}, bf16[2048,2048]{1,0:T(8,128)(2,1)}, bf16[2048,256]{1,0:T(8,128)(2,1)}, f32[4,2048]{1,0:T(4,128)}, f32[1,1024]{1,0:T(1,...) custom-call(bf16[2048,1024]{1,0:T(8,128)(2,1)} %get-tuple-element.54, ...), custom_call_target="tpu_custom_call" | custom-call | flops 80000000000 | bytes 10000000 | tf_op jit(solution)/shard_map/middle/pallas_call | solution.py:1071
  249.6 80.8 %back.1 = (bf16[2048,768]{1,0:T(8,128)(2,1)}, bf16[256,2048]{1,0:T(8,128)(2,1)}, f32[1024,512]{1,0:T(8,128)}, bf16[512,1024]{1,0:T(8,128)(2,1)}, bf16[512,1024]{...) custom-call(s32[8]{0:T(128)} %lengths.3, ...), custom_call_target="tpu_custom_call" | custom-call | flops 74999996416 | bytes 10000000 | tf_op jit(solution)/shard_map/back/pallas_call | solution.py:1276
  330.4 83.8 %last.1 = (bf16[256,2048]{1,0:T(8,128)(2,1)}, f32[512,1024]{1,0:T(8,128)}, bf16[256,512]{1,0:T(8,128)(2,1)}, bf16[256,512]{1,0:T(8,128)(2,1)}, bf16[256,512]{1,0...) custom-call(bf16[2048,768]{1,0:T(8,128)(2,1)} %get-tuple-element.70., ...), custom_call_target="tpu_custom_call" | custom-call | flops 74999996416 | bytes 10000000 | tf_op jit(solution)/shard_map/last/pallas_call | solution.py:1440
  414.2 2.0 select_add_fusion.1
  416.2 0.0 copy-start.6
  416.2 0.0 copy-start.5
  416.2 0.7 slice_bitcast_fusion.2
  417.0 0.0 copy-start.4
  417.0 0.6 pad_maximum_fusion
  417.6 0.0 copy-start.2
  417.6 3.2 select_add_fusion
  420.8 0.0 copy-start.3
  420.8 0.0 copy-done.6
  420.8 0.6 fusion.1
  421.4 0.0 copy-done.5
  421.4 0.6 copy.35
  422.1 0.0 copy-done.4
  422.1 0.6 fusion
  422.7 0.0 copy-done.2
  422.7 0.0 copy-start.1
  422.7 1.0 copy.40
  423.7 0.0 copy-done.3
  423.7 1.0 copy.41
  424.6 0.1 copy-done.1
  424.7 0.0 copy-start
  424.7 1.3 copy.42
  426.0 1.0 copy-done
  427.1 1.3 copy.43
  (3 shorter events, 0.0 us)
Async XLA Ops:
  416.2 4.6 %copy-start.6 = (f32[2,2048]{1,0:T(2,128)S(1)}, f32[2,2048]{1,0:T(2,128)}, u32[]{:S(2)}) copy-start(f32[2,2048]{1,0:T(2,128)} %get-tuple-element.79) | copy-start | bytes 49156
  416.2 5.2 %copy-start.5 = (f32[8,1536]{1,0:T(8,128)S(1)}, f32[8,1536]{1,0:T(8,128)}, u32[]{:S(2)}) copy-start(f32[8,1536]{1,0:T(8,128)} %get-tuple-element.74.qv_sums) | copy-start | bytes 147460
  417.0 5.1 %copy-start.4 = (f32[4,2048]{1,0:T(4,128)S(1)}, f32[4,2048]{1,0:T(4,128)}, u32[]{:S(2)}) copy-start(f32[4,2048]{1,0:T(4,128)} %get-tuple-element.87) | copy-start | bytes 98308
  417.6 5.1 %copy-start.2 = (bf16[256,2048]{1,0:T(8,128)(2,1)S(1)}, bf16[256,2048]{1,0:T(8,128)(2,1)}, u32[]{:S(2)}) copy-start(bf16[256,2048]{1,0:T(8,128)(2,1)} %get-tuple-element.112) | copy-start | bytes 3145732
  420.8 2.9 copy-start.3
  422.7 2.0 copy-start.1
  424.7 2.3 copy-start
